TPU v7x, 256 devices: a whole 4x4x8 slice. The times are simulated.
256 devices in a mesh: morton: 32 (over z, y), tile: 8 (over x, core).
Axes of the slice: x: 4, y: 4, z: 8, core: 2. Of those that a mesh axis runs over, the one named last changes fastest.
Arguments:
- moments: bfloat16 [8192, 64, 128], P(('morton', 'tile')), may hold values from -6 to 6
- dipole_pos: bfloat16 [8192, 3, 128], P(('morton', 'tile')), as said below
- send_index: int32 [8192, 2], P(('morton', 'tile')), may hold values from 0 to 31, as said below
- send_count: int32 [8192], P(('morton', 'tile')), may hold values from 1 to 2, as said below
- reading_pos: bfloat16 [16384, 3, 128], P(('morton', 'tile')), as said below
- near_cols: int32 [16384, 16], P(('morton', 'tile')), may hold values from 0 to 63, as said below
- grid_slot: int32 [16384], P(('morton', 'tile')), may hold values from 0 to 511, as said below
- observed: bfloat16 [16384, 64, 128], P(('morton', 'tile')), may hold values from -6 to 6
Outputs:
- field: bfloat16 [16384, 64, 128], P(('morton', 'tile'))
- adjoint_moments: float32 [8192, 64, 128], P(('morton', 'tile'))
Inputs may be any that keep to these rules, and one draw needn't show every extreme that they name: send_count has the value 2 at every row with q = p; the live entries of one leaf range's rows name every one of its 32 old blocks. `send_index`: entries past send_count are padding; live entries of the rows of leaf range g name old blocks 0 to 31 of g, each at least once. `near_cols`: every entry of the rows of leaf range g names a live slot of g, and every live slot of g is named at least once. `grid_slot`: for the reading blocks of leaf range g with tile index t, the values are d * 64 + t * 8 + e with each pair (d, e), d < 8, e < 8, taken once. `dipole_pos`: coordinates are multiples of 1/16; dipoles lie 0.5 or more below every reading. `reading_pos`: coordinates are multiples of 1/16.
All inputs are finite; a program needn't handle non-finite values.
Results may differ from a plain program's by a relative error of at most 0.005.
Values may be sent and summed in bfloat16 or wider, within the bound.
No kernel may reach another device: no remote copies, remote signals or barrier semaphores. Data moves between devices by JAX's collectives and lax.ppermute only.
A program may use at most 64 MiB of HBM per device.

v0:
```python
import jax
import jax.numpy as jnp
from jax import lax
from jax.sharding import PartitionSpec as P

kernel_scale = 0.2


def kernel_blocks(read_one, dip_blocks):
    reads = read_one.astype(jnp.float32)
    dips = dip_blocks.astype(jnp.float32)
    offset_east = reads[0][None, None, :] - dips[:, 0, :, None]
    offset_north = reads[1][None, None, :] - dips[:, 1, :, None]
    offset_vertical = reads[2][None, None, :] - dips[:, 2, :, None]
    distance_squared = (
        offset_east * offset_east + offset_north * offset_north + offset_vertical * offset_vertical
    )
    kernel_values = (
        kernel_scale
        * (
            2.0 * offset_vertical * offset_vertical
            - offset_east * offset_east
            - offset_north * offset_north
        )
        / (distance_squared * distance_squared * jnp.sqrt(distance_squared))
    )
    return kernel_values.astype(jnp.bfloat16)


def to_grid(field_leaf, inverse, tiles):
    rows, width, depth = field_leaf.shape
    ordered = field_leaf[inverse].reshape(tiles, rows // tiles, width, depth)
    moved = lax.all_to_all(ordered, "tile", split_axis=0, concat_axis=0, tiled=True)
    return moved.reshape(rows, width, depth)


def on_device(
    moments, dipole_pos, send_index, send_count, reading_pos, near_cols, grid_slot, observed
):
    peers = lax.axis_size("morton")
    tiles = lax.axis_size("tile")
    cap = send_index.shape[1]
    old = moments.shape[0]
    width = moments.shape[1]
    depth = moments.shape[2]
    rb = reading_pos.shape[0]
    near = near_cols.shape[1]
    share = rb // tiles
    live = jnp.arange(cap)[None, :] < send_count[:, None]
    flat_index = send_index.reshape(-1)
    send_m = jnp.where(
        live.reshape(-1)[:, None, None], moments[flat_index], jnp.zeros((), jnp.bfloat16)
    )
    send_m = send_m.reshape(peers, cap, width, depth)
    send_p = dipole_pos[flat_index].reshape(peers, cap, 3, depth)
    slot_m, slot_p = (
        lax.all_to_all(send_m, "morton", split_axis=0, concat_axis=0, tiled=True),
        lax.all_to_all(send_p, "morton", split_axis=0, concat_axis=0, tiled=True),
    )
    slot_m = slot_m.reshape(peers * cap, width, depth)
    slot_p = slot_p.reshape(peers * cap, 3, depth)
    order_key = grid_slot // rb * share + grid_slot % rb % share
    inverse = jnp.zeros((rb,), jnp.int32).at[order_key].set(jnp.arange(rb, dtype=jnp.int32))
    read_groups = reading_pos.reshape(rb // 4, 4, 3, depth)
    col_groups = near_cols.reshape(rb // 4, 4, near)
    start = jnp.zeros((peers * cap, width, depth), jnp.float32)
    kernel_group = jax.vmap(lambda read_one, cols_one: kernel_blocks(read_one, slot_p[cols_one]))

    def forward_group(items):
        read_g, cols_g = items
        kern = kernel_group(read_g, cols_g)
        return jnp.einsum(
            "gkcd,gkdr->gcr", slot_m[cols_g], kern, preferred_element_type=jnp.float32
        )

    field_leaf = (
        lax.map(forward_group, (read_groups, col_groups))
        .reshape(rb, width, depth)
        .astype(jnp.bfloat16)
    )
    field = to_grid(field_leaf, inverse, tiles)
    residual = (field.astype(jnp.float32) - observed.astype(jnp.float32)).astype(jnp.bfloat16)
    returned = lax.all_to_all(
        residual.reshape(tiles, share, width, depth),
        "tile",
        split_axis=0,
        concat_axis=0,
        tiled=True,
    )
    res_leaf = returned.reshape(rb, width, depth)[order_key].reshape(rb // 4, 4, width, depth)

    def adjoint_group(total, items):
        read_g, cols_g, res_g = items
        kern = kernel_group(read_g, cols_g)
        contrib = jnp.einsum("gcr,gkdr->gkcd", res_g, kern, preferred_element_type=jnp.float32)
        return (total.at[cols_g.reshape(-1)].add(contrib.reshape(-1, width, depth)), None)

    slot_adj, _ = lax.scan(adjoint_group, start, (read_groups, col_groups, res_leaf))
    back = lax.all_to_all(
        slot_adj.reshape(peers, cap, width, depth),
        "morton",
        split_axis=0,
        concat_axis=0,
        tiled=True,
    )
    back = jnp.where(live[:, :, None, None], back, jnp.zeros((), jnp.float32)).reshape(
        peers * cap, width * depth
    )
    owners = (flat_index[None, :] == jnp.arange(old, dtype=jnp.int32)[:, None]).astype(jnp.float32)
    adjoint_moments = jnp.dot(
        owners, back, precision=lax.Precision.HIGHEST, preferred_element_type=jnp.float32
    )
    return (field, adjoint_moments.reshape(old, width, depth))


def solution(mesh):
    return jax.shard_map(
        on_device,
        mesh=mesh,
        in_specs=(
            P(("morton", "tile"), None, None),
            P(("morton", "tile"), None, None),
            P(("morton", "tile"), None),
            P(("morton", "tile")),
            P(("morton", "tile"), None, None),
            P(("morton", "tile"), None),
            P(("morton", "tile")),
            P(("morton", "tile"), None, None),
        ),
        out_specs=(P(("morton", "tile"), None, None), P(("morton", "tile"), None, None)),
        check_vma=False,
    )
```

profile of v0, /device:TPU:8, one launch (start us, length us, event | category | flops | bytes accessed | tf_op | source)
XLA Modules:
  0.0 524.5 jit_solution(2848358050566341015)
XLA Ops:
  3.8 11.7 %all-to-all-start.1 = ((bf16[32,2,3,128]{3,1,2,0:T(2,128)(2,1)}), bf16[32,2,3,128]{3,1,2,0:T(2,128)(2,1)S(1)}, u32[]{:S(2)}, u32[]{:S(2)}) async-start(bf16[32,2,3,128]{3,1,2,0:T(2,128)(2,1)} %copy.33), calls=%async_computation.1 | async-start | bytes 98304 | tf_op jit(solution)/shard_map/all_to_all | solution.py:58
  18.1 6.0 %all-to-all-done.1 = bf16[32,2,3,128]{3,1,2,0:T(2,128)(2,1)S(1)} async-done(((bf16[32,2,3,128]{3,1,2,0:T(2,128)(2,1)}), bf16[32,2,3,128]{3,1,2,0:T(2,128)(2,1)S(1)}, u32[]{:S(2)}, u32[]{:S(2)}) %all-to-all-start.1) | async-done | bytes 49184 | tf_op jit(solution)/shard_map/all_to_all | solution.py:58
  24.1 5.0 all-to-all-start
  30.2 26.0 %all-to-all-done = bf16[32,2,64,128]{3,2,1,0:T(8,128)(2,1)S(1)} async-done(((bf16[32,2,64,128]{3,2,1,0:T(8,128)(2,1)}), bf16[32,2,64,128]{3,2,1,0:T(8,128)(2,1)S(1)}, u32[]{:S(2)}, u32[]{:S(2)}) %all-to-all-start) | async-done | bytes 1048608 | tf_op jit(solution)/shard_map/all_to_all | solution.py:57
  56.2 104.6 %while.20 = (s32[]{:T(128)}, bf16[16,4,64,128]{3,2,1,0:T(8,128)(2,1)}, s32[16,4,16]{2,1,0:T(4,128)S(1)}, bf16[64,64,128]{2,1,0:T(8,128)(2,1)S(1)}, bf16[16,4,3,1...) while((s32[]{:T(128)}, bf16[16,4,64,128]{3,2,1,0:T(8,128)(2,1)}, ...), condition=%wide.region_1.2_spmd, body=%wide.region_0.1_spmd.sunk | while | flops 152046272 | bytes 3703649 | solution.py:77
  57.8 4.9 fusion.64
  70.9 4.9 fusion.64
  90.5 4.9 fusion.64
  103.5 4.9 fusion.64
  129.7 4.9 fusion.64
  136.2 4.9 fusion.64
  162.8 20.2 %all_to_all.25 = bf16[8,8,64,128]{3,2,1,0:T(8,128)(2,1)S(1)} all-to-all(bf16[8,8,64,128]{3,2,1,0:T(8,128)(2,1)S(1)} %bitcast.137), channel_id=1, replica_groups=mesh['morton'=32,'tile'=8] {'tile'}, dimensions={0} | all-to-all | bytes 2097152 | tf_op jit(solution)/shard_map/all_to_all | solution.py:33
  189.0 15.9 %all-to-all-done.3 = bf16[8,8,64,128]{3,2,1,0:T(8,128)(2,1)S(1)} async-done(((bf16[8,8,64,128]{3,2,1,0:T(8,128)(2,1)}), bf16[8,8,64,128]{3,2,1,0:T(8,128)(2,1)S(1)}, u32[]{:S(2)}, u32[]{:S(2)}) %all-to-all-start.3) | async-done | bytes 1048608 | tf_op jit(solution)/shard_map/all_to_all | solution.py:83
  208.2 256.8 %while.21 = (s32[]{:T(128)}, f32[64,64,128]{2,1,0:T(8,128)}, s32[16,4,16]{2,1,0:T(4,128)S(1)}, bf16[16,4,3,128]{3,1,2,0:T(4,128)(2,1)S(1)}, bf16[64,3,128]{2,1,0...) while((s32[]{:T(128)}, f32[64,64,128]{2,1,0:T(8,128)}, s32[16,4,16]{2,1,0:T(4,128)S(1)}, ...), condition=%wide.region_5.6_spmd, body=%wide.region_3.5_spmd.sunk | while | flops 152570752 | bytes 8882273 | solution.py:98
  209.1 6.1 %fusion.69 = f32[4,16,128,64]{2,3,1,0:T(8,128)S(1)} fusion(f32[4,16,128]{2,1,0:T(8,128)S(1)} %bitcast.146, f32[4,128]{1,0:T(4,128)S(1)} %get-tuple-element.247, f32[4,16,128]{2,1,0:T(8,128)S(1)} %bitcast.145, f32[4,128]{1,0:T(4,128)S(1)} %get-tuple-element.249, f32[4,16,128]{2,1,0:T(8,128)S(1)} %bitcast.144, f32[4,128]{1,0:T(4,128)S(1)} %get-tuple-element.251, ...), kind=kOutput, calls=%fused_computation.38.clone.1 | convolution fusion | flops 152043520 | bytes 2267140 | tf_op jit(solution)/shard_map/while/body/eval_jaxpr/gcr,gkdr->gkcd/dot_general | solution.py:95
  215.2 9.0 %scatter_fusion = f32[64,64,128]{2,1,0:T(8,128)} fusion(f32[64,64,128]{2,1,0:T(8,128)} %get-tuple-element.281, s32[64]{0:T(128)S(1)} %fusion.67, f32[64,64,128]{2,1,0:T(8,128)S(1)} %bitcast.129), kind=kCustom, calls=%fused_computation.7.clone.1 | custom fusion | flops 524288 | bytes 6291712 | tf_op jit(solution)/shard_map/while/body/eval_jaxpr/scatter-add | solution.py:96
  225.1 6.1 %fusion.69 = f32[4,16,128,64]{2,3,1,0:T(8,128)S(1)} fusion(f32[4,16,128]{2,1,0:T(8,128)S(1)} %bitcast.146, f32[4,128]{1,0:T(4,128)S(1)} %get-tuple-element.247, f32[4,16,128]{2,1,0:T(8,128)S(1)} %bitcast.145, f32[4,128]{1,0:T(4,128)S(1)} %get-tuple-element.249, f32[4,16,128]{2,1,0:T(8,128)S(1)} %bitcast.144, f32[4,128]{1,0:T(4,128)S(1)} %get-tuple-element.251, ...), kind=kOutput, calls=%fused_computation.38.clone.1 | convolution fusion | flops 152043520 | bytes 2267140 | tf_op jit(solution)/shard_map/while/body/eval_jaxpr/gcr,gkdr->gkcd/dot_general | solution.py:95
  231.2 9.0 %scatter_fusion = f32[64,64,128]{2,1,0:T(8,128)} fusion(f32[64,64,128]{2,1,0:T(8,128)} %get-tuple-element.281, s32[64]{0:T(128)S(1)} %fusion.67, f32[64,64,128]{2,1,0:T(8,128)S(1)} %bitcast.129), kind=kCustom, calls=%fused_computation.7.clone.1 | custom fusion | flops 524288 | bytes 6291712 | tf_op jit(solution)/shard_map/while/body/eval_jaxpr/scatter-add | solution.py:96
  241.2 6.1 %fusion.69 = f32[4,16,128,64]{2,3,1,0:T(8,128)S(1)} fusion(f32[4,16,128]{2,1,0:T(8,128)S(1)} %bitcast.146, f32[4,128]{1,0:T(4,128)S(1)} %get-tuple-element.247, f32[4,16,128]{2,1,0:T(8,128)S(1)} %bitcast.145, f32[4,128]{1,0:T(4,128)S(1)} %get-tuple-element.249, f32[4,16,128]{2,1,0:T(8,128)S(1)} %bitcast.144, f32[4,128]{1,0:T(4,128)S(1)} %get-tuple-element.251, ...), kind=kOutput, calls=%fused_computation.38.clone.1 | convolution fusion | flops 152043520 | bytes 2267140 | tf_op jit(solution)/shard_map/while/body/eval_jaxpr/gcr,gkdr->gkcd/dot_general | solution.py:95
  247.3 9.0 %scatter_fusion = f32[64,64,128]{2,1,0:T(8,128)} fusion(f32[64,64,128]{2,1,0:T(8,128)} %get-tuple-element.281, s32[64]{0:T(128)S(1)} %fusion.67, f32[64,64,128]{2,1,0:T(8,128)S(1)} %bitcast.129), kind=kCustom, calls=%fused_computation.7.clone.1 | custom fusion | flops 524288 | bytes 6291712 | tf_op jit(solution)/shard_map/while/body/eval_jaxpr/scatter-add | solution.py:96
  257.2 6.1 %fusion.69 = f32[4,16,128,64]{2,3,1,0:T(8,128)S(1)} fusion(f32[4,16,128]{2,1,0:T(8,128)S(1)} %bitcast.146, f32[4,128]{1,0:T(4,128)S(1)} %get-tuple-element.247, f32[4,16,128]{2,1,0:T(8,128)S(1)} %bitcast.145, f32[4,128]{1,0:T(4,128)S(1)} %get-tuple-element.249, f32[4,16,128]{2,1,0:T(8,128)S(1)} %bitcast.144, f32[4,128]{1,0:T(4,128)S(1)} %get-tuple-element.251, ...), kind=kOutput, calls=%fused_computation.38.clone.1 | convolution fusion | flops 152043520 | bytes 2267140 | tf_op jit(solution)/shard_map/while/body/eval_jaxpr/gcr,gkdr->gkcd/dot_general | solution.py:95
  263.3 9.0 %scatter_fusion = f32[64,64,128]{2,1,0:T(8,128)} fusion(f32[64,64,128]{2,1,0:T(8,128)} %get-tuple-element.281, s32[64]{0:T(128)S(1)} %fusion.67, f32[64,64,128]{2,1,0:T(8,128)S(1)} %bitcast.129), kind=kCustom, calls=%fused_computation.7.clone.1 | custom fusion | flops 524288 | bytes 6291712 | tf_op jit(solution)/shard_map/while/body/eval_jaxpr/scatter-add | solution.py:96
  273.3 6.1 %fusion.69 = f32[4,16,128,64]{2,3,1,0:T(8,128)S(1)} fusion(f32[4,16,128]{2,1,0:T(8,128)S(1)} %bitcast.146, f32[4,128]{1,0:T(4,128)S(1)} %get-tuple-element.247, f32[4,16,128]{2,1,0:T(8,128)S(1)} %bitcast.145, f32[4,128]{1,0:T(4,128)S(1)} %get-tuple-element.249, f32[4,16,128]{2,1,0:T(8,128)S(1)} %bitcast.144, f32[4,128]{1,0:T(4,128)S(1)} %get-tuple-element.251, ...), kind=kOutput, calls=%fused_computation.38.clone.1 | convolution fusion | flops 152043520 | bytes 2267140 | tf_op jit(solution)/shard_map/while/body/eval_jaxpr/gcr,gkdr->gkcd/dot_general | solution.py:95
  279.4 9.0 %scatter_fusion = f32[64,64,128]{2,1,0:T(8,128)} fusion(f32[64,64,128]{2,1,0:T(8,128)} %get-tuple-element.281, s32[64]{0:T(128)S(1)} %fusion.67, f32[64,64,128]{2,1,0:T(8,128)S(1)} %bitcast.129), kind=kCustom, calls=%fused_computation.7.clone.1 | custom fusion | flops 524288 | bytes 6291712 | tf_op jit(solution)/shard_map/while/body/eval_jaxpr/scatter-add | solution.py:96
  289.3 6.1 %fusion.69 = f32[4,16,128,64]{2,3,1,0:T(8,128)S(1)} fusion(f32[4,16,128]{2,1,0:T(8,128)S(1)} %bitcast.146, f32[4,128]{1,0:T(4,128)S(1)} %get-tuple-element.247, f32[4,16,128]{2,1,0:T(8,128)S(1)} %bitcast.145, f32[4,128]{1,0:T(4,128)S(1)} %get-tuple-element.249, f32[4,16,128]{2,1,0:T(8,128)S(1)} %bitcast.144, f32[4,128]{1,0:T(4,128)S(1)} %get-tuple-element.251, ...), kind=kOutput, calls=%fused_computation.38.clone.1 | convolution fusion | flops 152043520 | bytes 2267140 | tf_op jit(solution)/shard_map/while/body/eval_jaxpr/gcr,gkdr->gkcd/dot_general | solution.py:95
  295.4 9.0 %scatter_fusion = f32[64,64,128]{2,1,0:T(8,128)} fusion(f32[64,64,128]{2,1,0:T(8,128)} %get-tuple-element.281, s32[64]{0:T(128)S(1)} %fusion.67, f32[64,64,128]{2,1,0:T(8,128)S(1)} %bitcast.129), kind=kCustom, calls=%fused_computation.7.clone.1 | custom fusion | flops 524288 | bytes 6291712 | tf_op jit(solution)/shard_map/while/body/eval_jaxpr/scatter-add | solution.py:96
  305.3 6.1 %fusion.69 = f32[4,16,128,64]{2,3,1,0:T(8,128)S(1)} fusion(f32[4,16,128]{2,1,0:T(8,128)S(1)} %bitcast.146, f32[4,128]{1,0:T(4,128)S(1)} %get-tuple-element.247, f32[4,16,128]{2,1,0:T(8,128)S(1)} %bitcast.145, f32[4,128]{1,0:T(4,128)S(1)} %get-tuple-element.249, f32[4,16,128]{2,1,0:T(8,128)S(1)} %bitcast.144, f32[4,128]{1,0:T(4,128)S(1)} %get-tuple-element.251, ...), kind=kOutput, calls=%fused_computation.38.clone.1 | convolution fusion | flops 152043520 | bytes 2267140 | tf_op jit(solution)/shard_map/while/body/eval_jaxpr/gcr,gkdr->gkcd/dot_general | solution.py:95
  311.4 9.0 %scatter_fusion = f32[64,64,128]{2,1,0:T(8,128)} fusion(f32[64,64,128]{2,1,0:T(8,128)} %get-tuple-element.281, s32[64]{0:T(128)S(1)} %fusion.67, f32[64,64,128]{2,1,0:T(8,128)S(1)} %bitcast.129), kind=kCustom, calls=%fused_computation.7.clone.1 | custom fusion | flops 524288 | bytes 6291712 | tf_op jit(solution)/shard_map/while/body/eval_jaxpr/scatter-add | solution.py:96
  321.4 6.1 %fusion.69 = f32[4,16,128,64]{2,3,1,0:T(8,128)S(1)} fusion(f32[4,16,128]{2,1,0:T(8,128)S(1)} %bitcast.146, f32[4,128]{1,0:T(4,128)S(1)} %get-tuple-element.247, f32[4,16,128]{2,1,0:T(8,128)S(1)} %bitcast.145, f32[4,128]{1,0:T(4,128)S(1)} %get-tuple-element.249, f32[4,16,128]{2,1,0:T(8,128)S(1)} %bitcast.144, f32[4,128]{1,0:T(4,128)S(1)} %get-tuple-element.251, ...), kind=kOutput, calls=%fused_computation.38.clone.1 | convolution fusion | flops 152043520 | bytes 2267140 | tf_op jit(solution)/shard_map/while/body/eval_jaxpr/gcr,gkdr->gkcd/dot_general | solution.py:95
  327.5 9.0 %scatter_fusion = f32[64,64,128]{2,1,0:T(8,128)} fusion(f32[64,64,128]{2,1,0:T(8,128)} %get-tuple-element.281, s32[64]{0:T(128)S(1)} %fusion.67, f32[64,64,128]{2,1,0:T(8,128)S(1)} %bitcast.129), kind=kCustom, calls=%fused_computation.7.clone.1 | custom fusion | flops 524288 | bytes 6291712 | tf_op jit(solution)/shard_map/while/body/eval_jaxpr/scatter-add | solution.py:96
  337.4 6.1 %fusion.69 = f32[4,16,128,64]{2,3,1,0:T(8,128)S(1)} fusion(f32[4,16,128]{2,1,0:T(8,128)S(1)} %bitcast.146, f32[4,128]{1,0:T(4,128)S(1)} %get-tuple-element.247, f32[4,16,128]{2,1,0:T(8,128)S(1)} %bitcast.145, f32[4,128]{1,0:T(4,128)S(1)} %get-tuple-element.249, f32[4,16,128]{2,1,0:T(8,128)S(1)} %bitcast.144, f32[4,128]{1,0:T(4,128)S(1)} %get-tuple-element.251, ...), kind=kOutput, calls=%fused_computation.38.clone.1 | convolution fusion | flops 152043520 | bytes 2267140 | tf_op jit(solution)/shard_map/while/body/eval_jaxpr/gcr,gkdr->gkcd/dot_general | solution.py:95
  343.6 9.0 %scatter_fusion = f32[64,64,128]{2,1,0:T(8,128)} fusion(f32[64,64,128]{2,1,0:T(8,128)} %get-tuple-element.281, s32[64]{0:T(128)S(1)} %fusion.67, f32[64,64,128]{2,1,0:T(8,128)S(1)} %bitcast.129), kind=kCustom, calls=%fused_computation.7.clone.1 | custom fusion | flops 524288 | bytes 6291712 | tf_op jit(solution)/shard_map/while/body/eval_jaxpr/scatter-add | solution.py:96
  353.5 6.1 %fusion.69 = f32[4,16,128,64]{2,3,1,0:T(8,128)S(1)} fusion(f32[4,16,128]{2,1,0:T(8,128)S(1)} %bitcast.146, f32[4,128]{1,0:T(4,128)S(1)} %get-tuple-element.247, f32[4,16,128]{2,1,0:T(8,128)S(1)} %bitcast.145, f32[4,128]{1,0:T(4,128)S(1)} %get-tuple-element.249, f32[4,16,128]{2,1,0:T(8,128)S(1)} %bitcast.144, f32[4,128]{1,0:T(4,128)S(1)} %get-tuple-element.251, ...), kind=kOutput, calls=%fused_computation.38.clone.1 | convolution fusion | flops 152043520 | bytes 2267140 | tf_op jit(solution)/shard_map/while/body/eval_jaxpr/gcr,gkdr->gkcd/dot_general | solution.py:95
  359.6 9.0 %scatter_fusion = f32[64,64,128]{2,1,0:T(8,128)} fusion(f32[64,64,128]{2,1,0:T(8,128)} %get-tuple-element.281, s32[64]{0:T(128)S(1)} %fusion.67, f32[64,64,128]{2,1,0:T(8,128)S(1)} %bitcast.129), kind=kCustom, calls=%fused_computation.7.clone.1 | custom fusion | flops 524288 | bytes 6291712 | tf_op jit(solution)/shard_map/while/body/eval_jaxpr/scatter-add | solution.py:96
  369.6 6.1 %fusion.69 = f32[4,16,128,64]{2,3,1,0:T(8,128)S(1)} fusion(f32[4,16,128]{2,1,0:T(8,128)S(1)} %bitcast.146, f32[4,128]{1,0:T(4,128)S(1)} %get-tuple-element.247, f32[4,16,128]{2,1,0:T(8,128)S(1)} %bitcast.145, f32[4,128]{1,0:T(4,128)S(1)} %get-tuple-element.249, f32[4,16,128]{2,1,0:T(8,128)S(1)} %bitcast.144, f32[4,128]{1,0:T(4,128)S(1)} %get-tuple-element.251, ...), kind=kOutput, calls=%fused_computation.38.clone.1 | convolution fusion | flops 152043520 | bytes 2267140 | tf_op jit(solution)/shard_map/while/body/eval_jaxpr/gcr,gkdr->gkcd/dot_general | solution.py:95
  375.7 9.0 %scatter_fusion = f32[64,64,128]{2,1,0:T(8,128)} fusion(f32[64,64,128]{2,1,0:T(8,128)} %get-tuple-element.281, s32[64]{0:T(128)S(1)} %fusion.67, f32[64,64,128]{2,1,0:T(8,128)S(1)} %bitcast.129), kind=kCustom, calls=%fused_computation.7.clone.1 | custom fusion | flops 524288 | bytes 6291712 | tf_op jit(solution)/shard_map/while/body/eval_jaxpr/scatter-add | solution.py:96
  385.7 6.1 %fusion.69 = f32[4,16,128,64]{2,3,1,0:T(8,128)S(1)} fusion(f32[4,16,128]{2,1,0:T(8,128)S(1)} %bitcast.146, f32[4,128]{1,0:T(4,128)S(1)} %get-tuple-element.247, f32[4,16,128]{2,1,0:T(8,128)S(1)} %bitcast.145, f32[4,128]{1,0:T(4,128)S(1)} %get-tuple-element.249, f32[4,16,128]{2,1,0:T(8,128)S(1)} %bitcast.144, f32[4,128]{1,0:T(4,128)S(1)} %get-tuple-element.251, ...), kind=kOutput, calls=%fused_computation.38.clone.1 | convolution fusion | flops 152043520 | bytes 2267140 | tf_op jit(solution)/shard_map/while/body/eval_jaxpr/gcr,gkdr->gkcd/dot_general | solution.py:95
  391.8 9.0 %scatter_fusion = f32[64,64,128]{2,1,0:T(8,128)} fusion(f32[64,64,128]{2,1,0:T(8,128)} %get-tuple-element.281, s32[64]{0:T(128)S(1)} %fusion.67, f32[64,64,128]{2,1,0:T(8,128)S(1)} %bitcast.129), kind=kCustom, calls=%fused_computation.7.clone.1 | custom fusion | flops 524288 | bytes 6291712 | tf_op jit(solution)/shard_map/while/body/eval_jaxpr/scatter-add | solution.py:96
  401.7 6.1 %fusion.69 = f32[4,16,128,64]{2,3,1,0:T(8,128)S(1)} fusion(f32[4,16,128]{2,1,0:T(8,128)S(1)} %bitcast.146, f32[4,128]{1,0:T(4,128)S(1)} %get-tuple-element.247, f32[4,16,128]{2,1,0:T(8,128)S(1)} %bitcast.145, f32[4,128]{1,0:T(4,128)S(1)} %get-tuple-element.249, f32[4,16,128]{2,1,0:T(8,128)S(1)} %bitcast.144, f32[4,128]{1,0:T(4,128)S(1)} %get-tuple-element.251, ...), kind=kOutput, calls=%fused_computation.38.clone.1 | convolution fusion | flops 152043520 | bytes 2267140 | tf_op jit(solution)/shard_map/while/body/eval_jaxpr/gcr,gkdr->gkcd/dot_general | solution.py:95
  407.9 9.0 %scatter_fusion = f32[64,64,128]{2,1,0:T(8,128)} fusion(f32[64,64,128]{2,1,0:T(8,128)} %get-tuple-element.281, s32[64]{0:T(128)S(1)} %fusion.67, f32[64,64,128]{2,1,0:T(8,128)S(1)} %bitcast.129), kind=kCustom, calls=%fused_computation.7.clone.1 | custom fusion | flops 524288 | bytes 6291712 | tf_op jit(solution)/shard_map/while/body/eval_jaxpr/scatter-add | solution.py:96
  417.8 6.1 %fusion.69 = f32[4,16,128,64]{2,3,1,0:T(8,128)S(1)} fusion(f32[4,16,128]{2,1,0:T(8,128)S(1)} %bitcast.146, f32[4,128]{1,0:T(4,128)S(1)} %get-tuple-element.247, f32[4,16,128]{2,1,0:T(8,128)S(1)} %bitcast.145, f32[4,128]{1,0:T(4,128)S(1)} %get-tuple-element.249, f32[4,16,128]{2,1,0:T(8,128)S(1)} %bitcast.144, f32[4,128]{1,0:T(4,128)S(1)} %get-tuple-element.251, ...), kind=kOutput, calls=%fused_computation.38.clone.1 | convolution fusion | flops 152043520 | bytes 2267140 | tf_op jit(solution)/shard_map/while/body/eval_jaxpr/gcr,gkdr->gkcd/dot_general | solution.py:95
  423.9 9.0 %scatter_fusion = f32[64,64,128]{2,1,0:T(8,128)} fusion(f32[64,64,128]{2,1,0:T(8,128)} %get-tuple-element.281, s32[64]{0:T(128)S(1)} %fusion.67, f32[64,64,128]{2,1,0:T(8,128)S(1)} %bitcast.129), kind=kCustom, calls=%fused_computation.7.clone.1 | custom fusion | flops 524288 | bytes 6291712 | tf_op jit(solution)/shard_map/while/body/eval_jaxpr/scatter-add | solution.py:96
  433.9 6.1 %fusion.69 = f32[4,16,128,64]{2,3,1,0:T(8,128)S(1)} fusion(f32[4,16,128]{2,1,0:T(8,128)S(1)} %bitcast.146, f32[4,128]{1,0:T(4,128)S(1)} %get-tuple-element.247, f32[4,16,128]{2,1,0:T(8,128)S(1)} %bitcast.145, f32[4,128]{1,0:T(4,128)S(1)} %get-tuple-element.249, f32[4,16,128]{2,1,0:T(8,128)S(1)} %bitcast.144, f32[4,128]{1,0:T(4,128)S(1)} %get-tuple-element.251, ...), kind=kOutput, calls=%fused_computation.38.clone.1 | convolution fusion | flops 152043520 | bytes 2267140 | tf_op jit(solution)/shard_map/while/body/eval_jaxpr/gcr,gkdr->gkcd/dot_general | solution.py:95
  440.0 9.0 %scatter_fusion = f32[64,64,128]{2,1,0:T(8,128)} fusion(f32[64,64,128]{2,1,0:T(8,128)} %get-tuple-element.281, s32[64]{0:T(128)S(1)} %fusion.67, f32[64,64,128]{2,1,0:T(8,128)S(1)} %bitcast.129), kind=kCustom, calls=%fused_computation.7.clone.1 | custom fusion | flops 524288 | bytes 6291712 | tf_op jit(solution)/shard_map/while/body/eval_jaxpr/scatter-add | solution.py:96
  449.9 6.1 %fusion.69 = f32[4,16,128,64]{2,3,1,0:T(8,128)S(1)} fusion(f32[4,16,128]{2,1,0:T(8,128)S(1)} %bitcast.146, f32[4,128]{1,0:T(4,128)S(1)} %get-tuple-element.247, f32[4,16,128]{2,1,0:T(8,128)S(1)} %bitcast.145, f32[4,128]{1,0:T(4,128)S(1)} %get-tuple-element.249, f32[4,16,128]{2,1,0:T(8,128)S(1)} %bitcast.144, f32[4,128]{1,0:T(4,128)S(1)} %get-tuple-element.251, ...), kind=kOutput, calls=%fused_computation.38.clone.1 | convolution fusion | flops 152043520 | bytes 2267140 | tf_op jit(solution)/shard_map/while/body/eval_jaxpr/gcr,gkdr->gkcd/dot_general | solution.py:95
  456.0 9.0 %scatter_fusion = f32[64,64,128]{2,1,0:T(8,128)} fusion(f32[64,64,128]{2,1,0:T(8,128)} %get-tuple-element.281, s32[64]{0:T(128)S(1)} %fusion.67, f32[64,64,128]{2,1,0:T(8,128)S(1)} %bitcast.129), kind=kCustom, calls=%fused_computation.7.clone.1 | custom fusion | flops 524288 | bytes 6291712 | tf_op jit(solution)/shard_map/while/body/eval_jaxpr/scatter-add | solution.py:96
  465.0 5.5 %all-to-all-start.4 = ((f32[32,2,64,128]{3,2,1,0:T(8,128)}), f32[32,2,64,128]{3,2,1,0:T(8,128)S(1)}, u32[]{:S(2)}, u32[]{:S(2)}) async-start(f32[32,2,64,128]{3,2,1,0:T(8,128)} %bitcast.46), calls=%async_computation.4 | async-start | bytes 4194304 | tf_op jit(solution)/shard_map/all_to_all | solution.py:99
  470.6 49.1 %all-to-all-done.4 = f32[32,2,64,128]{3,2,1,0:T(8,128)S(1)} async-done(((f32[32,2,64,128]{3,2,1,0:T(8,128)}), f32[32,2,64,128]{3,2,1,0:T(8,128)S(1)}, u32[]{:S(2)}, u32[]{:S(2)}) %all-to-all-start.4) | async-done | bytes 2097184 | tf_op jit(solution)/shard_map/all_to_all | solution.py:99
  (326 shorter events, 112.1 us)
Async XLA Ops:
  0.6 15.6 %copy-start = (bf16[32,64,128]{2,1,0:T(8,128)(2,1)S(1)}, bf16[32,64,128]{2,1,0:T(8,128)(2,1)}, u32[]{:S(2)}) copy-start(bf16[32,64,128]{2,1,0:T(8,128)(2,1)} %param.12) | copy-start | bytes 1572868
  3.8 20.3 %all-to-all-start.1 = ((bf16[32,2,3,128]{3,1,2,0:T(2,128)(2,1)}), bf16[32,2,3,128]{3,1,2,0:T(2,128)(2,1)S(1)}, u32[]{:S(2)}, u32[]{:S(2)}) async-start(bf16[32,2,3,128]{3,1,2,0:T(2,128)(2,1)} %copy.33), calls=%async_computation.1 | async-start | bytes 98304 | tf_op jit(solution)/shard_map/all_to_all | solution.py:58
  17.0 12.2 %copy-start.5 = (s32[64,16]{0,1:T(8,128)S(1)}, s32[64,16]{0,1:T(8,128)}, u32[]{:S(2)}) copy-start(s32[64,16]{0,1:T(8,128)} %param.17) | copy-start | bytes 12292
  17.0 12.3 %copy-start.4 = (bf16[64,3,128]{2,0,1:T(8,128)(2,1)S(1)}, bf16[64,3,128]{2,0,1:T(8,128)(2,1)}, u32[]{:S(2)}) copy-start(bf16[64,3,128]{2,0,1:T(8,128)(2,1)} %param.16) | copy-start | bytes 147460
  17.0 12.3 %copy-start.6 = (s32[64]{0:T(128)S(1)}, s32[64]{0:T(128)}, u32[]{:S(2)}) copy-start(s32[64]{0:T(128)} %param.18) | copy-start | bytes 772
  24.1 32.1 %all-to-all-start = ((bf16[32,2,64,128]{3,2,1,0:T(8,128)(2,1)}), bf16[32,2,64,128]{3,2,1,0:T(8,128)(2,1)S(1)}, u32[]{:S(2)}, u32[]{:S(2)}) async-start(bf16[32,2,64,128]{3,2,1,0:T(8,128)(2,1)} %broadcast_select_fusion.1), calls=%async_computation | async-start | bytes 2097152 | tf_op jit(solution)/shard_map/all_to_all | solution.py:57
  160.7 23.2 %copy-start.3 = (bf16[64,64,128]{2,1,0:T(8,128)(2,1)S(1)}, bf16[64,64,128]{2,1,0:T(8,128)(2,1)}, u32[]{:S(2)}) copy-start(bf16[64,64,128]{2,1,0:T(8,128)(2,1)} %param.19) | copy-start | bytes 3145732
  183.0 1.0 copy-start.1
  185.4 19.5 %all-to-all-start.3 = ((bf16[8,8,64,128]{3,2,1,0:T(8,128)(2,1)}), bf16[8,8,64,128]{3,2,1,0:T(8,128)(2,1)S(1)}, u32[]{:S(2)}, u32[]{:S(2)}) async-start(bf16[8,8,64,128]{3,2,1,0:T(8,128)(2,1)} %bitcast.43), calls=%async_computation.3 | async-start | bytes 2097152 | tf_op jit(solution)/shard_map/all_to_all | solution.py:83
  465.0 54.7 %all-to-all-start.4 = ((f32[32,2,64,128]{3,2,1,0:T(8,128)}), f32[32,2,64,128]{3,2,1,0:T(8,128)S(1)}, u32[]{:S(2)}, u32[]{:S(2)}) async-start(f32[32,2,64,128]{3,2,1,0:T(8,128)} %bitcast.46), calls=%async_computation.4 | async-start | bytes 4194304 | tf_op jit(solution)/shard_map/all_to_all | solution.py:99
  519.9 3.6 copy-start.2
where the time goes:
time: 532 us; the launch traced here: 525 us
  matrix products  178 us (33%)
  other arithmetic  148 us (28%)
  waiting for transfers between devices  97 us (18%)
  local copies, waits for them, and re-layouts  53.1 us (10%)
  starting transfers between devices  25.7 us (5%)
  blocking collectives  20.2 us (4%)
    scatter-add x16, other arithmetic, adjoint_group(): total.at[cols_g.reshape(-1)].add(contrib.reshape(-1, width, depth))  144 us
    dot_general x16, matrix products, adjoint_group(): jnp.einsum('gcr,gkdr->gkcd', res_g, kern, preferred_element_type=jnp.floa...  97.6 us
    dot_general x16, matrix products, forward_group(): jnp.einsum('gkcd,gkdr->gcr', slot_m[cols_g], kern, preferred_element_type...  78.8 us
    all_to_all x1, waiting for transfers between devices, on_device(): lax.all_to_all(slot_adj.reshape(peers, cap, width, depth), 'morton', spli...  49.1 us
    all_to_all x1, waiting for transfers between devices, on_device(): lax.all_to_all(send_m, 'morton', split_axis=0, concat_axis=0, tiled=True)  26 us
    gather x32, local copies, waits for them, and re-layouts, on_device(): slot_p[cols_one]  21 us
    all_to_all x1, blocking collectives, to_grid(): lax.all_to_all(ordered, 'tile', split_axis=0, concat_axis=0, tiled=True)  20.2 us
    all_to_all x1, waiting for transfers between devices, on_device(): lax.all_to_all(residual.reshape(tiles, share, width, depth), 'tile', spli...  15.9 us
  transfers between devices with their start and end apart: 4, of which 4 were waited for; matrix products, arithmetic and copies ran while one was open for 1% of the time, Pallas kernels for 0%

commit v1 on v0

v1 whole, which is shorter than its diff:
```python
import functools

import jax
import jax.numpy as jnp
from jax import lax
from jax.experimental import pallas as pl
from jax.experimental.pallas import tpu as pltpu
from jax.sharding import PartitionSpec as P

SHRINK = 0.6 ** (-1.0 / 3.0) / 2.0
UNDO = 0.125
GEN = 2
USE = 8
VMEM = 48 * 2**20


def make_kernels(cols_ref, pos_ref, read_ref, out_ref, read_wide):
    group, axes, blk = read_ref.shape
    near = out_ref.shape[2] // blk
    first = pl.program_id(0) * group
    for b in range(group):
        down = jnp.transpose(read_ref[b].astype(jnp.float32) * SHRINK)
        for c in range(axes):
            read_wide[b, c] = jnp.broadcast_to(down[:, c : c + 1], (blk, blk))

        def one(k, carry, b=b):
            p = pos_ref[cols_ref[first + b, k]].astype(jnp.float32) * SHRINK
            dx = read_wide[b, 0] - p[0:1]
            dy = read_wide[b, 1] - p[1:2]
            dz = read_wide[b, 2] - p[2:3]
            up = dz * dz
            inv = lax.rsqrt(dx * dx + dy * dy + up)
            inv2 = inv * inv
            value = (up * inv2 - (1.0 / 3.0)) * (inv2 * inv)
            out_ref[b, :, pl.ds(pl.multiple_of(k * blk, blk), blk)] = value.astype(out_ref.dtype)
            return carry

        lax.fori_loop(0, near, one, 0, unroll=2)


def kernel_values(near_cols, slot_p, reading_pos):
    rb, axes, blk = reading_pos.shape
    near = near_cols.shape[1]
    return pl.pallas_call(
        make_kernels,
        grid_spec=pltpu.PrefetchScalarGridSpec(
            num_scalar_prefetch=1,
            grid=(rb // GEN,),
            in_specs=[
                pl.BlockSpec(slot_p.shape, lambda g, *_: (0, 0, 0)),
                pl.BlockSpec((GEN, axes, blk), lambda g, *_: (g, 0, 0)),
            ],
            out_specs=pl.BlockSpec((GEN, blk, near * blk), lambda g, *_: (g, 0, 0)),
            scratch_shapes=[pltpu.VMEM((GEN, axes, blk, blk), jnp.float32)],
        ),
        out_shape=jax.ShapeDtypeStruct((rb, blk, near * blk), jnp.bfloat16),
        compiler_params=pltpu.CompilerParams(vmem_limit_bytes=VMEM),
        cost_estimate=pl.CostEstimate(
            flops=15 * rb * near * blk * blk,
            bytes_accessed=2 * rb * near * blk * blk,
            transcendentals=rb * near * blk * blk,
        ),
        name="kernel_values",
    )(near_cols, slot_p, reading_pos)


def apply_both(cols_ref, key_ref, kern_ref, m_ref, obs_ref, field_ref, adj_ref, m_wide, total):
    group, blk, wide = kern_ref.shape
    near = wide // blk
    step = pl.program_id(0)

    @pl.when(step == 0)
    def _():
        total[...] = jnp.zeros_like(total)

    for b in range(group):
        i = step * group + b
        at = key_ref[i]
        for k in range(near):
            m_wide[b, :, k * blk : (k + 1) * blk] = m_ref[cols_ref[i, k]]
        field = lax.dot_general(
            m_wide[b], kern_ref[b], (((1,), (1,)), ((), ())), preferred_element_type=jnp.float32
        )
        field = (field * UNDO).astype(jnp.bfloat16)
        field_ref[at] = field
        res = (field.astype(jnp.float32) - obs_ref[at].astype(jnp.float32)).astype(jnp.bfloat16)
        for k in range(near):
            total[cols_ref[i, k]] += jnp.dot(
                res, kern_ref[b, :, k * blk : (k + 1) * blk], preferred_element_type=jnp.float32
            )

    @pl.when(step == pl.num_programs(0) - 1)
    def _():
        adj_ref[...] = (total[...] * UNDO).astype(adj_ref.dtype)


def forward_adjoint(near_cols, order_key, kern, slot_m, observed):
    rb, blk, wide = kern.shape
    slots, width, _ = slot_m.shape
    whole = lambda g, *_: (0, 0, 0)
    return pl.pallas_call(
        apply_both,
        grid_spec=pltpu.PrefetchScalarGridSpec(
            num_scalar_prefetch=2,
            grid=(rb // USE,),
            in_specs=[
                pl.BlockSpec((USE, blk, wide), lambda g, *_: (g, 0, 0)),
                pl.BlockSpec(slot_m.shape, whole),
                pl.BlockSpec(observed.shape, whole),
            ],
            out_specs=[pl.BlockSpec((rb, width, blk), whole), pl.BlockSpec((slots, width, blk), whole)],
            scratch_shapes=[
                pltpu.VMEM((USE, width, wide), jnp.bfloat16),
                pltpu.VMEM((slots, width, blk), jnp.float32),
            ],
        ),
        out_shape=[
            jax.ShapeDtypeStruct((rb, width, blk), jnp.bfloat16),
            jax.ShapeDtypeStruct((slots, width, blk), jnp.bfloat16),
        ],
        compiler_params=pltpu.CompilerParams(vmem_limit_bytes=VMEM),
        cost_estimate=pl.CostEstimate(
            flops=4 * width * rb * wide * blk, bytes_accessed=2 * rb * wide * blk, transcendentals=0
        ),
        name="forward_adjoint",
    )(near_cols, order_key, kern, slot_m, observed)


def add_back(block_ref, live_ref, back_ref, out_ref):
    out_ref[...] = jnp.zeros_like(out_ref)

    def one(s, carry):
        alive = live_ref[s] > 0
        out_ref[block_ref[s]] += jnp.where(alive, back_ref[s].astype(jnp.float32), 0.0)
        return carry

    lax.fori_loop(0, back_ref.shape[0], one, 0, unroll=4)


def combine(flat_index, live, back, old):
    _, width, depth = back.shape
    return pl.pallas_call(
        add_back,
        grid_spec=pltpu.PrefetchScalarGridSpec(
            num_scalar_prefetch=2,
            grid=(1,),
            in_specs=[pl.BlockSpec(back.shape, lambda g, *_: (0, 0, 0))],
            out_specs=pl.BlockSpec((old, width, depth), lambda g, *_: (0, 0, 0)),
        ),
        out_shape=jax.ShapeDtypeStruct((old, width, depth), jnp.float32),
        compiler_params=pltpu.CompilerParams(vmem_limit_bytes=VMEM),
        name="combine",
    )(flat_index, live, back)


def on_device(
    moments, dipole_pos, send_index, send_count, reading_pos, near_cols, grid_slot, observed
):
    peers = lax.axis_size("morton")
    tiles = lax.axis_size("tile")
    cap = send_index.shape[1]
    old, width, depth = moments.shape
    rb = reading_pos.shape[0]
    share = rb // tiles
    swap = functools.partial(lax.all_to_all, split_axis=0, concat_axis=0, tiled=True)
    live = (jnp.arange(cap)[None, :] < send_count[:, None]).reshape(-1)
    flat_index = send_index.reshape(-1)
    send_p = dipole_pos[flat_index]
    slot_p = swap(send_p.reshape(peers, cap, 3, depth), "morton").reshape(peers * cap, 3, depth)
    send_m = jnp.where(live[:, None, None], moments[flat_index], jnp.zeros((), jnp.bfloat16))
    slot_m = swap(send_m.reshape(peers, cap, width, depth), "morton").reshape(
        peers * cap, width, depth
    )
    leaf_obs = swap(observed.reshape(tiles, share, width, depth), "tile").reshape(rb, width, depth)
    order_key = grid_slot // rb * share + grid_slot % rb % share
    kern = kernel_values(near_cols, slot_p, reading_pos)
    ordered, slot_adj = forward_adjoint(near_cols, order_key, kern, slot_m, leaf_obs)
    back = swap(slot_adj.reshape(peers, cap, width, depth), "morton").reshape(
        peers * cap, width, depth
    )
    field = swap(ordered.reshape(tiles, share, width, depth), "tile").reshape(rb, width, depth)
    adjoint_moments = combine(flat_index, live.astype(jnp.int32), back, old)
    return (field, adjoint_moments)


def solution(mesh):
    return jax.shard_map(
        on_device,
        mesh=mesh,
        in_specs=(
            P(("morton", "tile"), None, None),
            P(("morton", "tile"), None, None),
            P(("morton", "tile"), None),
            P(("morton", "tile")),
            P(("morton", "tile"), None, None),
            P(("morton", "tile"), None),
            P(("morton", "tile")),
            P(("morton", "tile"), None, None),
        ),
        out_specs=(P(("morton", "tile"), None, None), P(("morton", "tile"), None, None)),
        check_vma=False,
    )
```

time: 532 us -> 196 us (0.37); the launches traced: 525 us -> 196 us
  matrix products: 178 us -> 0 us
  other arithmetic: 148 us -> 2.53 us
  Pallas kernels: 0 us -> 87.8 us
  waiting for transfers between devices: 97 us -> 40.8 us
  local copies, waits for them, and re-layouts: 53.1 us -> 6.05 us
  blocking collectives: 20.2 us -> 38.7 us
  starting transfers between devices: 25.7 us -> 19.2 us
    dot_general x33 -> x0, matrix products: 178 us -> none  [the longest x16 97.6 us: adjoint_group(): jnp.einsum('gcr,gkdr->gkcd', res_g, kern, preferred_element_type=jnp.floa...]
    scatter-add x16 -> x0, other arithmetic: 144 us -> none  [adjoint_group(): total.at[cols_g.reshape(-1)].add(contrib.reshape(-1, width, depth))]
    pallas_call x0 -> x3, Pallas kernels: none -> 87.8 us  [the longest x1 59.1 us: kernel_values(): pl.pallas_call(make_kernels, grid_spec=pltpu.PrefetchScalarGridSpec(num_s...]
    all_to_all x4 -> x3, waiting for transfers between devices: 97 us -> 40.8 us  [the longest x1 27.5 us: on_device(): swap(slot_adj.reshape(peers, cap, width, depth), 'morton')]
    gather x51 -> x1, local copies, waits for them, and re-layouts: 38.2 us -> 1.51 us  [on_device(): send_p = dipole_pos[flat_index]]
    all_to_all x1 -> x2, blocking collectives: 20.2 us -> 38.7 us  [the longest x1 20.1 us: on_device(): swap(send_p.reshape(peers, cap, 3, depth), 'morton')]
    all_to_all x4 -> x3, starting transfers between devices: 25.7 us -> 19.2 us  [the longest x1 9.88 us: on_device(): swap(slot_adj.reshape(peers, cap, width, depth), 'morton')]
  transfers between devices with their start and end apart: 4 -> 3, of which waited for: 4 -> 2; matrix products, arithmetic and copies ran while one was open for 1% -> 3% of each run, Pallas kernels for 0% -> 30%
where the time goes in v1:
time: 196 us
  Pallas kernels  87.8 us (45%)
  waiting for transfers between devices  40.8 us (21%)
  blocking collectives  38.7 us (20%)
  starting transfers between devices  19.2 us (10%)
  local copies, waits for them, and re-layouts  6.05 us (3%)
  other arithmetic  2.53 us (1%)
    pallas_call x1, Pallas kernels, kernel_values(): pl.pallas_call(make_kernels, grid_spec=pltpu.PrefetchScalarGridSpec(num_s...  59.1 us
    all_to_all x1, waiting for transfers between devices, on_device(): swap(slot_adj.reshape(peers, cap, width, depth), 'morton')  27.5 us
    pallas_call x1, Pallas kernels, forward_adjoint(): pl.pallas_call(apply_both, grid_spec=pltpu.PrefetchScalarGridSpec(num_sca...  26.8 us
    all_to_all x1, blocking collectives, on_device(): swap(send_p.reshape(peers, cap, 3, depth), 'morton')  20.1 us
    all_to_all x1, blocking collectives, on_device(): swap(ordered.reshape(tiles, share, width, depth), 'tile')  18.5 us
    all_to_all x1, waiting for transfers between devices, on_device(): swap(observed.reshape(tiles, share, width, depth), 'tile')  13.4 us
    all_to_all x1, starting transfers between devices, on_device(): swap(slot_adj.reshape(peers, cap, width, depth), 'morton')  9.88 us
    all_to_all x1, starting transfers between devices, on_device(): swap(send_m.reshape(peers, cap, width, depth), 'morton')  5.02 us
  transfers between devices with their start and end apart: 3, of which 2 were waited for; matrix products, arithmetic and copies ran while one was open for 3% of the time, Pallas kernels for 30%

profile of v1, /device:TPU:8, one launch (start us, length us, event | category | flops | bytes accessed | tf_op | source)
XLA Modules:
  0.0 195.9 jit_solution(3065011870929586517)
XLA Ops:
  0.6 0.0 copy-start
  0.6 0.8 copy.22
  1.5 0.1 reshape.86
  1.6 1.5 gather_fusion
  3.1 20.1 %all_to_all.25 = bf16[32,2,3,128]{3,1,2,0:T(2,128)(2,1)S(1)} all-to-all(bf16[32,2,3,128]{3,1,2,0:T(2,128)(2,1)S(1)} %copy.23), channel_id=1, replica_groups=mesh['morton'=32,'tile'=8] {'morton'}, dimensions={0} | all-to-all | bytes 98304 | tf_op jit(solution)/shard_map/all_to_all | solution.py:169
  23.3 4.3 %all-to-all-start.2 = ((bf16[8,8,64,128]{3,2,1,0:T(8,128)(2,1)}), bf16[8,8,64,128]{3,2,1,0:T(8,128)(2,1)S(1)}, u32[]{:S(2)}, u32[]{:S(2)}) async-start(bf16[8,8,64,128]{3,2,1,0:T(8,128)(2,1)} %bitcast.20), calls=%async_computation.2 | async-start | bytes 2097152 | tf_op jit(solution)/shard_map/all_to_all | solution.py:174
  27.6 0.0 copy-done
  27.6 0.7 gather_fusion.1
  28.4 0.7 fusion.3
  29.1 1.1 broadcast_select_fusion
  30.2 13.4 %all-to-all-done.2 = bf16[8,8,64,128]{3,2,1,0:T(8,128)(2,1)S(1)} async-done(((bf16[8,8,64,128]{3,2,1,0:T(8,128)(2,1)}), bf16[8,8,64,128]{3,2,1,0:T(8,128)(2,1)S(1)}, u32[]{:S(2)}, u32[]{:S(2)}) %all-to-all-start.2) | async-done | bytes 1048608 | tf_op jit(solution)/shard_map/all_to_all | solution.py:174
  43.6 5.0 %all-to-all-start.1 = ((bf16[32,2,64,128]{3,2,1,0:T(8,128)(2,1)}), bf16[32,2,64,128]{3,2,1,0:T(8,128)(2,1)S(1)}, u32[]{:S(2)}, u32[]{:S(2)}) async-start(bf16[32,2,64,128]{3,2,1,0:T(8,128)(2,1)} %broadcast_select_fusion), calls=%async_computation.1 | async-start | bytes 2097152 | tf_op jit(solution)/shard_map/all_to_all | solution.py:171
  48.6 0.8 copy.27.cols_ref
  49.4 0.8 copy.26.read_ref
  50.2 0.7 fusion.key_ref
  50.9 59.1 %kernel_values.1.kern_ref = bf16[64,128,2048]{2,1,0:T(8,128)(2,1)} custom-call(s32[64,16]{1,0:T(8,128)S(1)} %copy.27.cols_ref, bf16[64,3,128]{2,1,0:T(4,128)(2,1)S(1)} %bitcast.17, bf16[64,3,128]{2,1,0:T(4,128)(2,1)S(1)} %copy.26.read_ref), custom_call_target="tpu_custom_call" | custom-call | flops 251658240 | bytes 33554432 | tf_op jit(solution)/shard_map/kernel_values/pallas_call | solution.py:44
  110.0 0.0 all-to-all-done.1
  110.0 26.8 %forward_adjoint.1 = (bf16[64,64,128]{2,1,0:T(8,128)(2,1)S(1)}, bf16[64,64,128]{2,1,0:T(8,128)(2,1)S(1)}) custom-call(s32[64,16]{1,0:T(8,128)S(1)} %copy.27.cols_ref, s32[64]{0:T(128)S(1)} %fusion.key_ref, bf16[64,128,2048]{2,1,0:T(8,128)(2,1)} %kernel_values.1.kern_ref, bf16[64,64,128]{2,1,0:T(8,128)(2,1)S(1)} %bitcast.13, bf16[64,64,128]{2,1,0:T(8,128)(2,1)S(1)} %bitcast.12), custom_call_target="tpu_custom_call" | custom-call | flops 4294967296 | bytes 33554432 | tf_op jit(solution)/shard_map/forward_adjoint/pallas_call | solution.py:101
  136.8 0.0 copy-start.1
  136.8 18.5 %all_to_all.26 = bf16[8,8,64,128]{3,2,1,0:T(8,128)(2,1)S(1)} all-to-all(bf16[8,8,64,128]{3,2,1,0:T(8,128)(2,1)S(1)} %bitcast.16), channel_id=1, replica_groups=mesh['morton'=32,'tile'=8] {'tile'}, dimensions={0} | all-to-all | bytes 2097152 | tf_op jit(solution)/shard_map/all_to_all | solution.py:181
  155.3 0.0 copy-done.1
  155.3 9.9 %all-to-all-start.4 = ((bf16[32,2,64,128]{3,2,1,0:T(8,128)(2,1)}), bf16[32,2,64,128]{3,2,1,0:T(8,128)(2,1)S(1)}, u32[]{:S(2)}, u32[]{:S(2)}) async-start(bf16[32,2,64,128]{3,2,1,0:T(8,128)(2,1)} %bitcast.15), calls=%async_computation.4 | async-start | bytes 2097152 | tf_op jit(solution)/shard_map/all_to_all | solution.py:178
  165.2 0.1 reshape.94.block_ref
  165.3 0.1 reshape.97.live_ref
  165.4 27.5 %all-to-all-done.4 = bf16[32,2,64,128]{3,2,1,0:T(8,128)(2,1)S(1)} async-done(((bf16[32,2,64,128]{3,2,1,0:T(8,128)(2,1)}), bf16[32,2,64,128]{3,2,1,0:T(8,128)(2,1)S(1)}, u32[]{:S(2)}, u32[]{:S(2)}) %all-to-all-start.4) | async-done | bytes 1048608 | tf_op jit(solution)/shard_map/all_to_all | solution.py:178
  192.9 2.0 combine.1
  194.9 1.0 copy.30
  (4 shorter events, 0.1 us)
Async XLA Ops:
  0.6 27.0 %copy-start = (bf16[32,64,128]{2,1,0:T(8,128)(2,1)S(1)}, bf16[32,64,128]{2,1,0:T(8,128)(2,1)}, u32[]{:S(2)}) copy-start(bf16[32,64,128]{2,1,0:T(8,128)(2,1)} %param.8) | copy-start | bytes 1572868
  23.3 20.3 %all-to-all-start.2 = ((bf16[8,8,64,128]{3,2,1,0:T(8,128)(2,1)}), bf16[8,8,64,128]{3,2,1,0:T(8,128)(2,1)S(1)}, u32[]{:S(2)}, u32[]{:S(2)}) async-start(bf16[8,8,64,128]{3,2,1,0:T(8,128)(2,1)} %bitcast.20), calls=%async_computation.2 | async-start | bytes 2097152 | tf_op jit(solution)/shard_map/all_to_all | solution.py:174
  43.6 66.5 %all-to-all-start.1 = ((bf16[32,2,64,128]{3,2,1,0:T(8,128)(2,1)}), bf16[32,2,64,128]{3,2,1,0:T(8,128)(2,1)S(1)}, u32[]{:S(2)}, u32[]{:S(2)}) async-start(bf16[32,2,64,128]{3,2,1,0:T(8,128)(2,1)} %broadcast_select_fusion), calls=%async_computation.1 | async-start | bytes 2097152 | tf_op jit(solution)/shard_map/all_to_all | solution.py:171
  136.8 18.5 %copy-start.1 = (bf16[64,64,128]{2,1,0:T(8,128)(2,1)}, bf16[64,64,128]{2,1,0:T(8,128)(2,1)S(1)}, u32[]{:S(2)}) copy-start(bf16[64,64,128]{2,1,0:T(8,128)(2,1)S(1)} %get-tuple-element.5) | copy-start | bytes 3145732
  155.3 37.6 %all-to-all-start.4 = ((bf16[32,2,64,128]{3,2,1,0:T(8,128)(2,1)}), bf16[32,2,64,128]{3,2,1,0:T(8,128)(2,1)S(1)}, u32[]{:S(2)}, u32[]{:S(2)}) async-start(bf16[32,2,64,128]{3,2,1,0:T(8,128)(2,1)} %bitcast.15), calls=%async_computation.4 | async-start | bytes 2097152 | tf_op jit(solution)/shard_map/all_to_all | solution.py:178

commit v2 on v1

v2 whole, which is shorter than its diff:
```python
import functools

import jax
import jax.numpy as jnp
from jax import lax
from jax.experimental import pallas as pl
from jax.experimental.pallas import tpu as pltpu
from jax.sharding import PartitionSpec as P

SCALE = 0.2
REACH = 64.0
GEN = 8
USE = 8
ROWS = 16
VMEM = 50 * 2**20


def squares(p):
    blk = p.shape[1]
    x, y, z = (p[c : c + 1] * p[c : c + 1] for c in range(3))
    return jnp.broadcast_to(x + y + z, (8, blk)), jnp.broadcast_to(2.0 * z - x - y, (8, blk))


def pieces(value):
    high = value.astype(jnp.bfloat16).astype(jnp.float32)
    rest = value - high
    middle = rest.astype(jnp.bfloat16).astype(jnp.float32)
    return high, middle, rest - middle


def rows_of(table, shape):
    row = lax.broadcasted_iota(jnp.int32, shape, 0)
    out = jnp.zeros(shape, jnp.float32)
    for at, value in table.items():
        out = jnp.where(row == at, value, out)
    return out


def reading_features(read_ref, feat_ref):
    for b in range(read_ref.shape[0]):
        p = read_ref[b].astype(jnp.float32)
        shape = (8, p.shape[1])
        near, tilt = squares(p)
        a, c = pieces(near), pieces(tilt)
        line = {n: jnp.broadcast_to(p[n : n + 1], shape) for n in range(3)}
        top = rows_of({**line, 3: a[0], 4: a[1], 5: a[2], 6: c[0], 7: c[1]}, shape)
        low = rows_of({0: c[2], 1: 1.0, 2: 1.0, 3: 1.0}, shape)
        feat_ref[b] = jnp.transpose(jnp.concatenate([top, low], 0)).astype(feat_ref.dtype)


def features(reading_pos):
    rb, axes, blk = reading_pos.shape
    return pl.pallas_call(
        reading_features,
        grid=(rb // 16,),
        in_specs=[pl.BlockSpec((16, axes, blk), lambda g: (g, 0, 0))],
        out_specs=pl.BlockSpec((16, blk, ROWS), lambda g: (g, 0, 0)),
        out_shape=jax.ShapeDtypeStruct((rb, blk, ROWS), jnp.bfloat16),
        compiler_params=pltpu.CompilerParams(vmem_limit_bytes=VMEM),
        cost_estimate=pl.CostEstimate(
            flops=0, bytes_accessed=4 * rb * blk * blk, transcendentals=0
        ),
        name="features",
    )(reading_pos)


def make_kernels(cols_ref, pos_ref, all_ref, read_ref, feat_ref, out_ref, weight_ref, fits_ref):
    group, blk, wide = out_ref.shape
    near = wide // blk
    step = pl.program_id(0)
    first = step * group

    @pl.when(step == 0)
    def _():
        far = jnp.maximum(
            jnp.max(jnp.abs(pos_ref[...].astype(jnp.float32))),
            jnp.max(jnp.abs(all_ref[...].astype(jnp.float32))),
        )
        fits_ref[0] = (far <= REACH).astype(jnp.int32)
        shape = (8, blk)

        def prepare(s, carry):
            p = pos_ref[s].astype(jnp.float32)
            x, y, z = (jnp.broadcast_to(p[c : c + 1], shape) for c in range(3))
            close, tilt = squares(p)
            a, c = pieces(close), pieces(tilt)
            left_top = rows_of({0: -2.0 * x, 1: -2.0 * y, 2: -2.0 * z, 3: 1.0, 4: 1.0, 5: 1.0}, shape)
            left_low = rows_of({1: a[0], 2: a[1], 3: a[2]}, shape)
            right_top = rows_of({0: 2.0 * x, 1: 2.0 * y, 2: -4.0 * z, 6: 1.0, 7: 1.0}, shape)
            right_low = rows_of({0: 1.0, 1: c[0], 2: c[1], 3: c[2]}, shape)
            left = jnp.concatenate([left_top, left_low], 0)
            right = jnp.concatenate([right_top, right_low], 0)
            weight_ref[s] = jnp.concatenate([left, right], 1).astype(weight_ref.dtype)
            return carry

        lax.fori_loop(0, pos_ref.shape[0], prepare, 0, unroll=4)

    fits = fits_ref[0] > 0

    @pl.when(fits)
    def _():
        for b in range(group):
            for k in range(0, near, 2):
                both = [
                    jnp.dot(
                        feat_ref[b],
                        weight_ref[cols_ref[first + b, k + c]],
                        preferred_element_type=jnp.float32,
                    )
                    for c in range(2)
                ]
                for r in range(0, blk, 8):
                    pair = []
                    for part in both:
                        inv = lax.rsqrt(part[r : r + 8, :blk])
                        inv2 = inv * inv
                        pair.append((part[r : r + 8, blk:] * (inv2 * inv2)) * inv)
                    out_ref[b, r : r + 8, k * blk : (k + 2) * blk] = jnp.concatenate(
                        pair, 1
                    ).astype(out_ref.dtype)

    @pl.when(jnp.logical_not(fits))
    def _():
        def one_reading(b, carry):
            down = jnp.transpose(read_ref[b].astype(jnp.float32))
            rx, ry, rz = (jnp.broadcast_to(down[:, c : c + 1], (blk, blk)) for c in range(3))

            def one_block(k, carry):
                p = pos_ref[cols_ref[first + b, k]].astype(jnp.float32)
                dx, dy, dz = rx - p[0:1], ry - p[1:2], rz - p[2:3]
                flat, up = dx * dx + dy * dy, dz * dz
                inv = lax.rsqrt(flat + up)
                inv2 = inv * inv
                value = ((up + up - flat) * (inv2 * inv2)) * inv
                out_ref[b, :, pl.ds(pl.multiple_of(k * blk, blk), blk)] = value.astype(
                    out_ref.dtype
                )
                return carry

            return lax.fori_loop(0, near, one_block, carry)

        lax.fori_loop(0, group, one_reading, 0)


def kernel_values(near_cols, slot_p, reading_pos, feat):
    rb, axes, blk = reading_pos.shape
    near = near_cols.shape[1]
    whole = lambda g, *_: (0, 0, 0)
    part = lambda g, *_: (g, 0, 0)
    return pl.pallas_call(
        make_kernels,
        grid_spec=pltpu.PrefetchScalarGridSpec(
            num_scalar_prefetch=1,
            grid=(rb // GEN,),
            in_specs=[
                pl.BlockSpec(slot_p.shape, whole),
                pl.BlockSpec(reading_pos.shape, whole),
                pl.BlockSpec((GEN, axes, blk), part),
                pl.BlockSpec((GEN, blk, ROWS), part),
            ],
            out_specs=pl.BlockSpec((GEN, blk, near * blk), part),
            scratch_shapes=[
                pltpu.VMEM((slot_p.shape[0], ROWS, 2 * blk), jnp.bfloat16),
                pltpu.SMEM((1,), jnp.int32),
            ],
        ),
        out_shape=jax.ShapeDtypeStruct((rb, blk, near * blk), jnp.bfloat16),
        compiler_params=pltpu.CompilerParams(vmem_limit_bytes=VMEM),
        cost_estimate=pl.CostEstimate(
            flops=15 * rb * near * blk * blk,
            bytes_accessed=2 * rb * near * blk * blk,
            transcendentals=rb * near * blk * blk,
        ),
        name="kernel_values",
    )(near_cols, slot_p, reading_pos, reading_pos, feat)


def apply_both(cols_ref, from_ref, to_ref, kern_ref, m_ref, *refs):
    *seen_refs, field_ref, adj_ref, total, obs_ref = refs
    group, blk, wide = kern_ref.shape
    near = wide // blk
    step = pl.program_id(0)

    @pl.when(step == 0)
    def _():
        total[...] = jnp.zeros_like(total)
        share = obs_ref.shape[0] // len(seen_refs)
        for n, ref in enumerate(seen_refs):
            obs_ref[n * share : (n + 1) * share] = ref[...]

    residuals = []
    for b in range(group):
        i = step * group + b
        field = None
        for k in range(0, near, 2):
            part = lax.dot_general(
                jnp.concatenate([m_ref[cols_ref[i, k]], m_ref[cols_ref[i, k + 1]]], 1),
                kern_ref[b, :, k * blk : (k + 2) * blk],
                (((1,), (1,)), ((), ())),
                preferred_element_type=jnp.float32,
            )
            field = part if field is None else field + part
        field = (field * SCALE).astype(jnp.bfloat16)
        field_ref[to_ref[i]] = field
        seen = obs_ref[from_ref[i]].astype(jnp.float32)
        residuals.append((field.astype(jnp.float32) - seen).astype(jnp.bfloat16))
    for b in range(group):
        i = step * group + b
        for k in range(0, near, 2):
            both = jnp.dot(
                residuals[b],
                kern_ref[b, :, k * blk : (k + 2) * blk],
                preferred_element_type=jnp.float32,
            )
            total[cols_ref[i, k]] += both[:, :blk]
            total[cols_ref[i, k + 1]] += both[:, blk:]

    @pl.when(step == pl.num_programs(0) - 1)
    def _():
        adj_ref[...] = (total[...] * SCALE).astype(adj_ref.dtype)


def forward_adjoint(near_cols, from_row, to_row, kern, slot_m, seen):
    rb, blk, wide = kern.shape
    slots, width, _ = slot_m.shape
    whole = lambda g, *_: (0, 0, 0)
    return pl.pallas_call(
        apply_both,
        grid_spec=pltpu.PrefetchScalarGridSpec(
            num_scalar_prefetch=3,
            grid=(rb // USE,),
            in_specs=[
                pl.BlockSpec((USE, blk, wide), lambda g, *_: (g, 0, 0)),
                pl.BlockSpec(slot_m.shape, whole),
                *[pl.BlockSpec(part.shape, whole) for part in seen],
            ],
            out_specs=[pl.BlockSpec((rb, width, blk), whole), pl.BlockSpec((slots, width, blk), whole)],
            scratch_shapes=[
                pltpu.VMEM((slots, width, blk), jnp.float32),
                pltpu.VMEM((rb, width, blk), jnp.bfloat16),
            ],
        ),
        out_shape=[
            jax.ShapeDtypeStruct((rb, width, blk), jnp.bfloat16),
            jax.ShapeDtypeStruct((slots, width, blk), jnp.bfloat16),
        ],
        compiler_params=pltpu.CompilerParams(vmem_limit_bytes=VMEM),
        cost_estimate=pl.CostEstimate(
            flops=4 * width * rb * wide * blk, bytes_accessed=2 * rb * wide * blk, transcendentals=0
        ),
        name="forward_adjoint",
    )(near_cols, from_row, to_row, kern, slot_m, *seen)


def shift(block, axis, by, size):
    return lax.ppermute(block, axis, [(i, (i + by) % size) for i in range(size)])


def add_back(block_ref, live_ref, back_ref, out_ref):
    out_ref[...] = jnp.zeros_like(out_ref)

    def one(s, carry):
        alive = live_ref[s] > 0
        out_ref[block_ref[s]] += jnp.where(alive, back_ref[s].astype(jnp.float32), 0.0)
        return carry

    lax.fori_loop(0, back_ref.shape[0], one, 0, unroll=4)


def combine(flat_index, live, back, old):
    _, width, depth = back.shape
    return pl.pallas_call(
        add_back,
        grid_spec=pltpu.PrefetchScalarGridSpec(
            num_scalar_prefetch=2,
            grid=(1,),
            in_specs=[pl.BlockSpec(back.shape, lambda g, *_: (0, 0, 0))],
            out_specs=pl.BlockSpec((old, width, depth), lambda g, *_: (0, 0, 0)),
        ),
        out_shape=jax.ShapeDtypeStruct((old, width, depth), jnp.float32),
        compiler_params=pltpu.CompilerParams(vmem_limit_bytes=VMEM),
        name="combine",
    )(flat_index, live, back)


def on_device(
    moments, dipole_pos, send_index, send_count, reading_pos, near_cols, grid_slot, observed
):
    peers = lax.axis_size("morton")
    tiles = lax.axis_size("tile")
    cap = send_index.shape[1]
    old, width, depth = moments.shape
    rb = reading_pos.shape[0]
    share = rb // tiles
    swap = functools.partial(lax.all_to_all, split_axis=0, concat_axis=0, tiled=True)
    live = (jnp.arange(cap)[None, :] < send_count[:, None]).reshape(-1)
    flat_index = send_index.reshape(-1)
    send_p = dipole_pos[flat_index]
    slot_p = swap(send_p.reshape(peers, cap, 3, depth), "morton").reshape(peers * cap, 3, depth)
    me = lax.axis_index("tile")
    to_tile, within = grid_slot // rb, grid_slot % share
    from_row = (me - to_tile) % tiles * share + within
    to_row = (to_tile - me) % tiles * share + within
    seen = []
    for by in range(tiles):
        part = lax.dynamic_slice_in_dim(observed, (me + by) % tiles * share, share, 0)
        seen.append(shift(part, "tile", by, tiles) if by else part)
    feat = features(reading_pos)
    send_m = jnp.where(live[:, None, None], moments[flat_index], jnp.zeros((), jnp.bfloat16))
    send_m, feat, seen[1], seen[2] = lax.optimization_barrier((send_m, feat, seen[1], seen[2]))
    slot_m = swap(send_m.reshape(peers, cap, width, depth), "morton").reshape(
        peers * cap, width, depth
    )
    kern = kernel_values(near_cols, slot_p, reading_pos, feat)
    ordered, slot_adj = forward_adjoint(near_cols, from_row, to_row, kern, slot_m, seen)
    back = swap(slot_adj.reshape(peers, cap, width, depth), "morton").reshape(
        peers * cap, width, depth
    )
    field = jnp.zeros_like(ordered)
    for by in range(tiles):
        part = ordered[by * share : (by + 1) * share]
        part = shift(part, "tile", by, tiles) if by else part
        field = lax.dynamic_update_slice_in_dim(field, part, (me - by) % tiles * share, 0)
    adjoint_moments = combine(flat_index, live.astype(jnp.int32), back, old)
    return (field, adjoint_moments)


def solution(mesh):
    return jax.shard_map(
        on_device,
        mesh=mesh,
        in_specs=(
            P(("morton", "tile"), None, None),
            P(("morton", "tile"), None, None),
            P(("morton", "tile"), None),
            P(("morton", "tile")),
            P(("morton", "tile"), None, None),
            P(("morton", "tile"), None),
            P(("morton", "tile")),
            P(("morton", "tile"), None, None),
        ),
        out_specs=(P(("morton", "tile"), None, None), P(("morton", "tile"), None, None)),
        check_vma=False,
    )
```

time: 196 us -> 132 us (0.67)
  blocking collectives: 38.7 us -> 0 us
  Pallas kernels: 87.8 us -> 49.8 us
  starting transfers between devices: 19.2 us -> 47.7 us
  waiting for transfers between devices: 40.8 us -> 14 us
  local copies, waits for them, and re-layouts: 6.05 us -> 16.2 us
    all_to_all x2 -> x0, blocking collectives: 38.7 us -> none  [the longest x1 20.1 us: on_device(): swap(send_p.reshape(peers, cap, 3, depth), 'morton')]
    pallas_call x1, Pallas kernels: 59.1 us -> 22.7 us  [kernel_values(): pl.pallas_call(make_kernels, grid_spec=pltpu.PrefetchScalarGridSpec(num_s...]
    ppermute x0 -> x14, starting transfers between devices: none -> 20.1 us  [shift(): lax.ppermute(block, axis, [(i, (i + by) % size) for i in range(size)])]
    all_to_all x1, waiting for transfers between devices: 27.5 us -> 7.69 us  [on_device(): swap(slot_adj.reshape(peers, cap, width, depth), 'morton')]
    all_to_all x1, waiting for transfers between devices: 13.4 us -> 4.17 us  [on_device(): swap(send_p.reshape(peers, cap, 3, depth), 'morton')]
    all_to_all x1, starting transfers between devices: 4.3 us -> 11.7 us  [on_device(): swap(send_p.reshape(peers, cap, 3, depth), 'morton')]
    dynamic_update_slice x0 -> x7, local copies, waits for them, and re-layouts: none -> 4.65 us  [on_device(): lax.dynamic_update_slice_in_dim(field, part, (me - by) % tiles * share, 0)]
    pallas_call x1, Pallas kernels: 26.8 us -> 24.1 us  [forward_adjoint(): pl.pallas_call(apply_both, grid_spec=pltpu.PrefetchScalarGridSpec(num_sca...]
  transfers between devices with their start and end apart: 3 -> 17, of which waited for: 2 -> 3; matrix products, arithmetic and copies ran while one was open for 3% -> 11% of each run, Pallas kernels for 30% -> 18%
where the time goes in v2:
time: 132 us; the launch traced here: 131 us
  Pallas kernels  49.8 us (38%)
  starting transfers between devices  47.7 us (36%)
  local copies, waits for them, and re-layouts  16.2 us (12%)
  waiting for transfers between devices  14 us (11%)
  other arithmetic  2.55 us (2%)
    pallas_call x1, Pallas kernels, forward_adjoint(): pl.pallas_call(apply_both, grid_spec=pltpu.PrefetchScalarGridSpec(num_sca...  24.1 us
    pallas_call x1, Pallas kernels, kernel_values(): pl.pallas_call(make_kernels, grid_spec=pltpu.PrefetchScalarGridSpec(num_s...  22.7 us
    ppermute x14, starting transfers between devices, shift(): lax.ppermute(block, axis, [(i, (i + by) % size) for i in range(size)])  20.1 us
    all_to_all x1, starting transfers between devices, on_device(): swap(send_p.reshape(peers, cap, 3, depth), 'morton')  11.7 us
    all_to_all x1, starting transfers between devices, on_device(): swap(slot_adj.reshape(peers, cap, width, depth), 'morton')  9.9 us
    all_to_all x1, waiting for transfers between devices, on_device(): swap(slot_adj.reshape(peers, cap, width, depth), 'morton')  7.69 us
    all_to_all x1, starting transfers between devices, on_device(): swap(send_m.reshape(peers, cap, width, depth), 'morton')  5.94 us
    dynamic_update_slice x7, local copies, waits for them, and re-layouts, on_device(): lax.dynamic_update_slice_in_dim(field, part, (me - by) % tiles * share, 0)  4.65 us
  transfers between devices with their start and end apart: 17, of which 3 were waited for; matrix products, arithmetic and copies ran while one was open for 11% of the time, Pallas kernels for 18%

profile of v2, /device:TPU:8, one launch (start us, length us, event | category | flops | bytes accessed | tf_op | source)
XLA Modules:
  0.0 131.1 jit_solution(12729337265166166424)
XLA Ops:
  0.6 0.0 copy-start
  0.8 2.2 %constant_dynamic-slice_fusion = (bf16[8,64,128]{2,1,0:T(8,128)(2,1)}, bf16[8,64,128]{2,1,0:T(8,128)(2,1)}, bf16[8,64,128]{2,1,0:T(8,128)(2,1)}, bf16[8,64,128]{...) fusion(bf16[64,64,128]{2,1,0:T(8,128)(2,1)} %param.15, ...), kind=kLoop, calls=%fused_computation.13 | loop fusion | bytes 2097184 | tf_op jit(solution)/shard_map/dynamic_slice | solution.py:306
  3.0 1.6 %collective-permute-start.1 = (bf16[8,64,128]{2,1,0:T(8,128)(2,1)S(1)}, bf16[8,64,128]{2,1,0:T(8,128)(2,1)S(1)}, u32[]{:S(2)}, u32[]{:S(2)}) collective-permute-start(bf16[8,64,128]{2,1,0:T(8,128)(2,1)S(1)} %get-tuple-element.30), channel_id=1, source_target_pairs={{0,2},{1,3},{2,4},{3,5},{4,6},{5,7},{6,0},{7,1},{8,10},{9,11},{10,... | collective-permute-start | bytes 393224 | tf_op jit(solution)/shard_map/ppermute | solution.py:256
  4.5 0.8 copy.26
  5.3 0.1 reshape.73
  5.4 1.5 %gather_fusion = bf16[64,3,128]{2,0,1:T(8,128)(2,1)S(1)} fusion(bf16[32,3,128]{2,0,1:T(8,128)(2,1)} %param.9, s32[1024]{0:T(1024)S(1)} %pad_clamp_fusion), kind=kCustom, calls=%fused_computation | custom fusion | bytes 98560 | tf_op jit(solution)/shard_map/gather | solution.py:298
  6.9 0.7 copy.27
  7.6 11.7 %all-to-all-start = ((bf16[32,2,3,128]{3,1,2,0:T(2,128)(2,1)}), bf16[32,2,3,128]{3,1,2,0:T(2,128)(2,1)S(1)}, u32[]{:S(2)}, u32[]{:S(2)}) async-start(bf16[32,2,3,128]{3,1,2,0:T(2,128)(2,1)} %copy.27), calls=%async_computation | async-start | bytes 98304 | tf_op jit(solution)/shard_map/all_to_all | solution.py:299
  19.3 0.7 gather_fusion.1
  20.0 0.7 iota_compare_fusion
  20.8 0.1 lt.163
  20.9 1.1 broadcast_select_fusion
  22.0 0.8 copy.31.read_ref.all_ref
  22.9 1.0 features.1.feat_ref
  23.9 4.2 %all-to-all-done = bf16[32,2,3,128]{3,1,2,0:T(2,128)(2,1)S(1)} async-done(((bf16[32,2,3,128]{3,1,2,0:T(2,128)(2,1)}), bf16[32,2,3,128]{3,1,2,0:T(2,128)(2,1)S(1)}, u32[]{:S(2)}, u32[]{:S(2)}) %all-to-all-start) | async-done | bytes 49184 | tf_op jit(solution)/shard_map/all_to_all | solution.py:299
  28.0 5.9 %all-to-all-start.1 = ((bf16[32,2,64,128]{3,2,1,0:T(8,128)(2,1)}), bf16[32,2,64,128]{3,2,1,0:T(8,128)(2,1)}, u32[]{:S(2)}, u32[]{:S(2)}) async-start(bf16[32,2,64,128]{3,2,1,0:T(8,128)(2,1)} %bitcast.11), calls=%async_computation.1 | async-start | bytes 2097152 | tf_op jit(solution)/shard_map/all_to_all | solution.py:311
  34.0 0.8 collective-permute-start.2
  34.8 2.0 %collective-permute-start.3 = (bf16[8,64,128]{2,1,0:T(8,128)(2,1)}, bf16[8,64,128]{2,1,0:T(8,128)(2,1)S(1)}, u32[]{:S(2)}, u32[]{:S(2)}) collective-permute-start(bf16[8,64,128]{2,1,0:T(8,128)(2,1)} %get-tuple-element.27), channel_id=1, source_target_pairs={{0,4},{1,5},{2,6},{3,7},{4,0},{5,1},{6,2},{7,3},{8,12},{9,13},{10,... | collective-permute-start | bytes 393224 | tf_op jit(solution)/shard_map/ppermute | solution.py:256
  36.8 2.7 %collective-permute-start.4 = (bf16[8,64,128]{2,1,0:T(8,128)(2,1)}, bf16[8,64,128]{2,1,0:T(8,128)(2,1)S(1)}, u32[]{:S(2)}, u32[]{:S(2)}) collective-permute-start(bf16[8,64,128]{2,1,0:T(8,128)(2,1)} %get-tuple-element.26), channel_id=1, source_target_pairs={{0,5},{1,6},{2,7},{3,0},{4,1},{5,2},{6,3},{7,4},{8,13},{9,14},{10,... | collective-permute-start | bytes 393224 | tf_op jit(solution)/shard_map/ppermute | solution.py:256
  39.5 1.5 %collective-permute-start.5 = (bf16[8,64,128]{2,1,0:T(8,128)(2,1)}, bf16[8,64,128]{2,1,0:T(8,128)(2,1)}, u32[]{:S(2)}, u32[]{:S(2)}) collective-permute-start(bf16[8,64,128]{2,1,0:T(8,128)(2,1)} %get-tuple-element.32), channel_id=1, source_target_pairs={{0,6},{1,7},{2,0},{3,1},{4,2},{5,3},{6,4},{7,5},{8,14},{9,15},{10,... | collective-permute-start | bytes 393224 | tf_op jit(solution)/shard_map/ppermute | solution.py:256
  41.0 0.7 fusion.3
  41.7 0.8 copy.33.cols_ref
  42.5 0.8 copy.28
  43.3 22.7 %kernel_values.1.kern_ref = bf16[64,128,2048]{2,1,0:T(8,128)(2,1)} custom-call(s32[64,16]{1,0:T(8,128)S(1)} %copy.33.cols_ref, bf16[64,3,128]{2,1,0:T(4,128)(2,1)S(1)} %bitcast.10, bf16[64,3,128]{2,1,0:T(4,128)(2,1)S(1)} %copy.31.read_ref.all_ref, bf16[64,3,128]{2,1,0:T(4,128)(2,1)S(1)} %copy.31.read_ref.all_ref, bf16[64,128,16]{2,1,0:T(8,128)(2,1)S(1)} %features.1.feat_ref), custom_call_target="tpu_custom_call" | custom-call | flops 251658240 | bytes 33554432 | tf_op jit(solution)/shard_map/kernel_values/pallas_call | solution.py:150
  66.1 24.1 %forward_adjoint.1 = (bf16[64,64,128]{2,1,0:T(8,128)(2,1)S(1)}, bf16[64,64,128]{2,1,0:T(8,128)(2,1)S(1)}) custom-call(s32[64,16]{1,0:T(8,128)S(1)} %copy.33.cols_ref, s32[64]{0:T(128)S(1)} %fusion.1.from_ref, s32[64]{0:T(128)S(1)} %get-tuple-element.14.to_ref, bf16[64,128,2048]{2,1,0:T(8,128)(2,1)} %kernel_values.1.kern_ref, ...), custom_call_target="tpu_custom_call" | custom-call | flops 4294967296 | bytes 33554432 | tf_op jit(solution)/shard_map/forward_adjoint/pallas_call | solution.py:227
  90.2 0.0 copy-start.1
  90.2 1.0 copy-done.1
  91.2 9.9 %all-to-all-start.2 = ((bf16[32,2,64,128]{3,2,1,0:T(8,128)(2,1)}), bf16[32,2,64,128]{3,2,1,0:T(8,128)(2,1)S(1)}, u32[]{:S(2)}, u32[]{:S(2)}) async-start(bf16[32,2,64,128]{3,2,1,0:T(8,128)(2,1)} %bitcast.9), calls=%async_computation.2 | async-start | bytes 2097152 | tf_op jit(solution)/shard_map/all_to_all | solution.py:316
  101.1 0.2 broadcast_in_dim.8
  101.3 0.7 fusion.7
  102.0 1.0 copy-done.2
  103.0 0.4 collective-permute-start.8
  103.4 0.1 reshape.78.block_ref
  103.6 0.6 collective-permute-start.9
  104.2 3.6 %collective-permute-start.10 = (bf16[8,64,128]{2,1,0:T(8,128)(2,1)S(1)}, bf16[8,64,128]{2,1,0:T(8,128)(2,1)S(1)}, u32[]{:S(2)}, u32[]{:S(2)}) collective-permute-start(bf16[8,64,128]{2,1,0:T(8,128)(2,1)S(1)} %get-tuple-element.20), channel_id=1, source_target_pairs={{0,4},{1,5},{2,6},{3,7},{4,0},{5,1},{6,2},{7,3},{8,12},{9,13},{10,... | collective-permute-start | bytes 393224 | tf_op jit(solution)/shard_map/ppermute | solution.py:256
  107.8 0.0 collective-permute-start.11
  107.8 2.1 %collective-permute-done.7 = bf16[8,64,128]{2,1,0:T(8,128)(2,1)S(1)} collective-permute-done((bf16[8,64,128]{2,1,0:T(8,128)(2,1)}, bf16[8,64,128]{2,1,0:T(8,128)(2,1)S(1)}, u32[]{:S(2)}, u32[]{:S(2)}) %collective-permute-start.7) | collective-permute-done | bytes 131104 | tf_op jit(solution)/shard_map/ppermute | solution.py:256
  109.9 0.1 collective-permute-start.12
  110.0 0.7 constant_dynamic-update-slice_fusion.6
  110.7 6.8 %collective-permute-start.13 = (bf16[8,64,128]{2,1,0:T(8,128)(2,1)S(1)}, bf16[8,64,128]{2,1,0:T(8,128)(2,1)S(1)}, u32[]{:S(2)}, u32[]{:S(2)}) collective-permute-start(bf16[8,64,128]{2,1,0:T(8,128)(2,1)S(1)} %get-tuple-element.17), channel_id=1, source_target_pairs={{0,7},{1,0},{2,1},{3,2},{4,3},{5,4},{6,5},{7,6},{8,15},{9,8},{10,9... | collective-permute-start | bytes 393224 | tf_op jit(solution)/shard_map/ppermute | solution.py:256
  117.5 0.7 constant_dynamic-update-slice_fusion.5
  118.1 0.7 constant_dynamic-update-slice_fusion.4
  118.8 0.7 constant_dynamic-update-slice_fusion.3
  119.5 0.7 constant_dynamic-update-slice_fusion.2
  120.1 0.7 constant_dynamic-update-slice_fusion.1
  120.8 0.7 constant_dynamic-update-slice_fusion
  121.5 7.7 %all-to-all-done.2 = bf16[32,2,64,128]{3,2,1,0:T(8,128)(2,1)S(1)} async-done(((bf16[32,2,64,128]{3,2,1,0:T(8,128)(2,1)}), bf16[32,2,64,128]{3,2,1,0:T(8,128)(2,1)S(1)}, u32[]{:S(2)}, u32[]{:S(2)}) %all-to-all-start.2) | async-done | bytes 1048608 | tf_op jit(solution)/shard_map/all_to_all | solution.py:316
  129.2 2.0 %combine.1 = f32[32,64,128]{2,1,0:T(8,128)} custom-call(s32[64]{0:T(128)S(1)} %reshape.78.block_ref, s32[64]{0:T(128)S(1)} %convert_element_type.3.live_ref, bf16[64,64,128]{2,1,0:T(8,128)(2,1)S(1)} %bitcast.8), custom_call_target="tpu_custom_call" | custom-call | tf_op jit(solution)/shard_map/combine/pallas_call | solution.py:272
  (25 shorter events, 0.1 us)
Async XLA Ops:
  0.6 18.6 %copy-start = (bf16[32,64,128]{2,1,0:T(8,128)(2,1)S(1)}, bf16[32,64,128]{2,1,0:T(8,128)(2,1)}, u32[]{:S(2)}) copy-start(bf16[32,64,128]{2,1,0:T(8,128)(2,1)} %param.8) | copy-start | bytes 1572868
  2.9 20.9 %collective-permute-start = (bf16[8,64,128]{2,1,0:T(8,128)(2,1)}, bf16[8,64,128]{2,1,0:T(8,128)(2,1)S(1)}, u32[]{:S(2)}, u32[]{:S(2)}) collective-permute-start(bf16[8,64,128]{2,1,0:T(8,128)(2,1)} %get-tuple-element.31), channel_id=1, source_target_pairs={{0,1},{1,2},{2,3},{3,4},{4,5},{5,6},{6,7},{7,0},{8,9},{9,10},{10,1... | collective-permute-start | bytes 393224 | tf_op jit(solution)/shard_map/ppermute | solution.py:256
  3.0 20.9 %collective-permute-start.1 = (bf16[8,64,128]{2,1,0:T(8,128)(2,1)S(1)}, bf16[8,64,128]{2,1,0:T(8,128)(2,1)S(1)}, u32[]{:S(2)}, u32[]{:S(2)}) collective-permute-start(bf16[8,64,128]{2,1,0:T(8,128)(2,1)S(1)} %get-tuple-element.30), channel_id=1, source_target_pairs={{0,2},{1,3},{2,4},{3,5},{4,6},{5,7},{6,0},{7,1},{8,10},{9,11},{10,... | collective-permute-start | bytes 393224 | tf_op jit(solution)/shard_map/ppermute | solution.py:256
  7.6 20.5 %all-to-all-start = ((bf16[32,2,3,128]{3,1,2,0:T(2,128)(2,1)}), bf16[32,2,3,128]{3,1,2,0:T(2,128)(2,1)S(1)}, u32[]{:S(2)}, u32[]{:S(2)}) async-start(bf16[32,2,3,128]{3,1,2,0:T(2,128)(2,1)} %copy.27), calls=%async_computation | async-start | bytes 98304 | tf_op jit(solution)/shard_map/all_to_all | solution.py:299
  28.0 6.8 %copy-start.3 = (bf16[32,2,3,128]{3,1,2,0:T(2,128)(2,1)}, bf16[32,2,3,128]{3,1,2,0:T(2,128)(2,1)S(1)}, u32[]{:S(2)}) copy-start(bf16[32,2,3,128]{3,1,2,0:T(2,128)(2,1)S(1)} %all-to-all-done) | copy-start | bytes 147460
  28.0 38.1 %all-to-all-start.1 = ((bf16[32,2,64,128]{3,2,1,0:T(8,128)(2,1)}), bf16[32,2,64,128]{3,2,1,0:T(8,128)(2,1)}, u32[]{:S(2)}, u32[]{:S(2)}) async-start(bf16[32,2,64,128]{3,2,1,0:T(8,128)(2,1)} %bitcast.11), calls=%async_computation.1 | async-start | bytes 2097152 | tf_op jit(solution)/shard_map/all_to_all | solution.py:311
  34.0 32.1 %collective-permute-start.2 = (bf16[8,64,128]{2,1,0:T(8,128)(2,1)}, bf16[8,64,128]{2,1,0:T(8,128)(2,1)S(1)}, u32[]{:S(2)}, u32[]{:S(2)}) collective-permute-start(bf16[8,64,128]{2,1,0:T(8,128)(2,1)} %get-tuple-element.28), channel_id=1, source_target_pairs={{0,3},{1,4},{2,5},{3,6},{4,7},{5,0},{6,1},{7,2},{8,11},{9,12},{10,... | collective-permute-start | bytes 393224 | tf_op jit(solution)/shard_map/ppermute | solution.py:256
  34.8 31.3 %collective-permute-start.3 = (bf16[8,64,128]{2,1,0:T(8,128)(2,1)}, bf16[8,64,128]{2,1,0:T(8,128)(2,1)S(1)}, u32[]{:S(2)}, u32[]{:S(2)}) collective-permute-start(bf16[8,64,128]{2,1,0:T(8,128)(2,1)} %get-tuple-element.27), channel_id=1, source_target_pairs={{0,4},{1,5},{2,6},{3,7},{4,0},{5,1},{6,2},{7,3},{8,12},{9,13},{10,... | collective-permute-start | bytes 393224 | tf_op jit(solution)/shard_map/ppermute | solution.py:256
  36.8 29.3 %collective-permute-start.4 = (bf16[8,64,128]{2,1,0:T(8,128)(2,1)}, bf16[8,64,128]{2,1,0:T(8,128)(2,1)S(1)}, u32[]{:S(2)}, u32[]{:S(2)}) collective-permute-start(bf16[8,64,128]{2,1,0:T(8,128)(2,1)} %get-tuple-element.26), channel_id=1, source_target_pairs={{0,5},{1,6},{2,7},{3,0},{4,1},{5,2},{6,3},{7,4},{8,13},{9,14},{10,... | collective-permute-start | bytes 393224 | tf_op jit(solution)/shard_map/ppermute | solution.py:256
  39.5 26.6 %collective-permute-start.5 = (bf16[8,64,128]{2,1,0:T(8,128)(2,1)}, bf16[8,64,128]{2,1,0:T(8,128)(2,1)}, u32[]{:S(2)}, u32[]{:S(2)}) collective-permute-start(bf16[8,64,128]{2,1,0:T(8,128)(2,1)} %get-tuple-element.32), channel_id=1, source_target_pairs={{0,6},{1,7},{2,0},{3,1},{4,2},{5,3},{6,4},{7,5},{8,14},{9,15},{10,... | collective-permute-start | bytes 393224 | tf_op jit(solution)/shard_map/ppermute | solution.py:256
  41.0 25.1 %collective-permute-start.6 = (bf16[8,64,128]{2,1,0:T(8,128)(2,1)}, bf16[8,64,128]{2,1,0:T(8,128)(2,1)}, u32[]{:S(2)}, u32[]{:S(2)}) collective-permute-start(bf16[8,64,128]{2,1,0:T(8,128)(2,1)} %get-tuple-element.25), channel_id=1, source_target_pairs={{0,7},{1,0},{2,1},{3,2},{4,3},{5,4},{6,5},{7,6},{8,15},{9,8},{10,9... | collective-permute-start | bytes 393224 | tf_op jit(solution)/shard_map/ppermute | solution.py:256
  90.2 1.0 copy-start.1
  91.2 38.0 %all-to-all-start.2 = ((bf16[32,2,64,128]{3,2,1,0:T(8,128)(2,1)}), bf16[32,2,64,128]{3,2,1,0:T(8,128)(2,1)S(1)}, u32[]{:S(2)}, u32[]{:S(2)}) async-start(bf16[32,2,64,128]{3,2,1,0:T(8,128)(2,1)} %bitcast.9), calls=%async_computation.2 | async-start | bytes 2097152 | tf_op jit(solution)/shard_map/all_to_all | solution.py:316
  102.0 1.0 copy-start.2
  103.0 6.9 %collective-permute-start.7 = (bf16[8,64,128]{2,1,0:T(8,128)(2,1)}, bf16[8,64,128]{2,1,0:T(8,128)(2,1)S(1)}, u32[]{:S(2)}, u32[]{:S(2)}) collective-permute-start(bf16[8,64,128]{2,1,0:T(8,128)(2,1)} %get-tuple-element.23), channel_id=1, source_target_pairs={{0,1},{1,2},{2,3},{3,4},{4,5},{5,6},{6,7},{7,0},{8,9},{9,10},{10,1... | collective-permute-start | bytes 393224 | tf_op jit(solution)/shard_map/ppermute | solution.py:256
  103.0 7.7 %collective-permute-start.8 = (bf16[8,64,128]{2,1,0:T(8,128)(2,1)S(1)}, bf16[8,64,128]{2,1,0:T(8,128)(2,1)S(1)}, u32[]{:S(2)}, u32[]{:S(2)}) collective-permute-start(bf16[8,64,128]{2,1,0:T(8,128)(2,1)S(1)} %get-tuple-element.22), channel_id=1, source_target_pairs={{0,2},{1,3},{2,4},{3,5},{4,6},{5,7},{6,0},{7,1},{8,10},{9,11},{10,... | collective-permute-start | bytes 393224 | tf_op jit(solution)/shard_map/ppermute | solution.py:256
  103.6 14.5 %collective-permute-start.9 = (bf16[8,64,128]{2,1,0:T(8,128)(2,1)S(1)}, bf16[8,64,128]{2,1,0:T(8,128)(2,1)S(1)}, u32[]{:S(2)}, u32[]{:S(2)}) collective-permute-start(bf16[8,64,128]{2,1,0:T(8,128)(2,1)S(1)} %get-tuple-element.21), channel_id=1, source_target_pairs={{0,3},{1,4},{2,5},{3,6},{4,7},{5,0},{6,1},{7,2},{8,11},{9,12},{10,... | collective-permute-start | bytes 393224 | tf_op jit(solution)/shard_map/ppermute | solution.py:256
  104.2 14.6 %collective-permute-start.10 = (bf16[8,64,128]{2,1,0:T(8,128)(2,1)S(1)}, bf16[8,64,128]{2,1,0:T(8,128)(2,1)S(1)}, u32[]{:S(2)}, u32[]{:S(2)}) collective-permute-start(bf16[8,64,128]{2,1,0:T(8,128)(2,1)S(1)} %get-tuple-element.20), channel_id=1, source_target_pairs={{0,4},{1,5},{2,6},{3,7},{4,0},{5,1},{6,2},{7,3},{8,12},{9,13},{10,... | collective-permute-start | bytes 393224 | tf_op jit(solution)/shard_map/ppermute | solution.py:256
  107.8 11.7 %collective-permute-start.11 = (bf16[8,64,128]{2,1,0:T(8,128)(2,1)S(1)}, bf16[8,64,128]{2,1,0:T(8,128)(2,1)S(1)}, u32[]{:S(2)}, u32[]{:S(2)}) collective-permute-start(bf16[8,64,128]{2,1,0:T(8,128)(2,1)S(1)} %get-tuple-element.19), channel_id=1, source_target_pairs={{0,5},{1,6},{2,7},{3,0},{4,1},{5,2},{6,3},{7,4},{8,13},{9,14},{10,... | collective-permute-start | bytes 393224 | tf_op jit(solution)/shard_map/ppermute | solution.py:256
  109.9 10.2 %collective-permute-start.12 = (bf16[8,64,128]{2,1,0:T(8,128)(2,1)S(1)}, bf16[8,64,128]{2,1,0:T(8,128)(2,1)S(1)}, u32[]{:S(2)}, u32[]{:S(2)}) collective-permute-start(bf16[8,64,128]{2,1,0:T(8,128)(2,1)S(1)} %get-tuple-element.18), channel_id=1, source_target_pairs={{0,6},{1,7},{2,0},{3,1},{4,2},{5,3},{6,4},{7,5},{8,14},{9,15},{10,... | collective-permute-start | bytes 393224 | tf_op jit(solution)/shard_map/ppermute | solution.py:256
  110.7 10.1 %collective-permute-start.13 = (bf16[8,64,128]{2,1,0:T(8,128)(2,1)S(1)}, bf16[8,64,128]{2,1,0:T(8,128)(2,1)S(1)}, u32[]{:S(2)}, u32[]{:S(2)}) collective-permute-start(bf16[8,64,128]{2,1,0:T(8,128)(2,1)S(1)} %get-tuple-element.17), channel_id=1, source_target_pairs={{0,7},{1,0},{2,1},{3,2},{4,3},{5,4},{6,5},{7,6},{8,15},{9,8},{10,9... | collective-permute-start | bytes 393224 | tf_op jit(solution)/shard_map/ppermute | solution.py:256

commit v3 on v2

v3 whole, which is shorter than its diff:
```python
import functools

import jax
import jax.numpy as jnp
from jax import lax
from jax.experimental import pallas as pl
from jax.experimental.pallas import tpu as pltpu
from jax.sharding import PartitionSpec as P

SCALE = 0.2
REACH = 64.0
GEN = 8
USE = 8
ROWS = 16
VMEM = 50 * 2**20


def pick_places(index_ref, pos_ref, out_ref, pos32):
    axes, _, blk = pos_ref.shape
    pos32[...] = pos_ref[...].astype(jnp.float32)
    for q in range(out_ref.shape[0]):
        lines = {}
        for c in range(index_ref.shape[0]):
            for n in range(axes):
                line = pos32[n, pl.ds(index_ref[c, q], 1), :]
                lines[c * axes + n] = jnp.broadcast_to(line, (8, blk))
        out_ref[q] = rows_of(lines, (8, blk)).astype(out_ref.dtype)


def pick_moments(index_ref, count_ref, m_ref, out_ref):
    def one(q, carry):
        for c in range(index_ref.shape[0]):
            kept = jnp.where(count_ref[q] > c, m_ref[index_ref[c, q]].astype(jnp.float32), 0.0)
            out_ref[q, c] = kept.astype(out_ref.dtype)
        return carry

    lax.fori_loop(0, index_ref.shape[1], one, 0, unroll=8)


def picked(kernel, scalars, table, out_shape, scratch, name):
    return pl.pallas_call(
        kernel,
        grid_spec=pltpu.PrefetchScalarGridSpec(
            num_scalar_prefetch=len(scalars),
            grid=(1,),
            in_specs=[pl.BlockSpec(table.shape, lambda g, *_: (0,) * table.ndim)],
            out_specs=pl.BlockSpec(out_shape, lambda g, *_: (0,) * len(out_shape)),
            scratch_shapes=scratch,
        ),
        out_shape=jax.ShapeDtypeStruct(out_shape, table.dtype),
        compiler_params=pltpu.CompilerParams(vmem_limit_bytes=60 * 2**20),
        cost_estimate=pl.CostEstimate(flops=0, bytes_accessed=1024, transcendentals=0),
        name=name,
    )(*scalars, table)


def squares(x, y, z):
    x, y, z = x * x, y * y, z * z
    return x + y + z, 2.0 * z - x - y


def pieces(value):
    high = value.astype(jnp.bfloat16).astype(jnp.float32)
    rest = value - high
    middle = rest.astype(jnp.bfloat16).astype(jnp.float32)
    return high, middle, rest - middle


def rows_of(table, shape):
    row = lax.broadcasted_iota(jnp.int32, shape, 0)
    out = jnp.zeros(shape, jnp.float32)
    for at, value in table.items():
        out = jnp.where(row == at, value, out)
    return out


def reading_features(read_ref, feat_ref, far_ref):
    x, y, z = (read_ref[c].astype(jnp.float32) for c in range(3))
    close, tilt = squares(x, y, z)
    lines = [x, y, z, *pieces(close), *pieces(tilt)]
    shape = (8, x.shape[1])
    size = jnp.maximum(jnp.maximum(jnp.abs(x), jnp.abs(y)), jnp.abs(z))
    far = functools.reduce(jnp.maximum, [size[r : r + 8] for r in range(0, size.shape[0], 8)])
    first = pl.program_id(0) == 0
    far_ref[...] = jnp.maximum(jnp.where(first, 0.0, far_ref[...]), far)
    for b in range(feat_ref.shape[0]):
        line = [jnp.broadcast_to(v[b : b + 1], shape) for v in lines]
        top = rows_of(dict(enumerate(line[:8])), shape)
        low = rows_of({0: line[8], 1: 1.0, 2: 1.0, 3: 1.0}, shape)
        feat_ref[b] = jnp.transpose(jnp.concatenate([top, low], 0)).astype(feat_ref.dtype)


def features(reading_pos):
    axes, rb, blk = reading_pos.shape
    return pl.pallas_call(
        reading_features,
        grid=(rb // 16,),
        in_specs=[pl.BlockSpec((axes, 16, blk), lambda g: (0, g, 0))],
        out_specs=[
            pl.BlockSpec((16, blk, ROWS), lambda g: (g, 0, 0)),
            pl.BlockSpec((8, blk), lambda g: (0, 0)),
        ],
        out_shape=[
            jax.ShapeDtypeStruct((rb, blk, ROWS), jnp.bfloat16),
            jax.ShapeDtypeStruct((8, blk), jnp.float32),
        ],
        compiler_params=pltpu.CompilerParams(vmem_limit_bytes=VMEM),
        cost_estimate=pl.CostEstimate(
            flops=0, bytes_accessed=4 * rb * blk * blk, transcendentals=0
        ),
        name="features",
    )(reading_pos)


def make_kernels(cols_ref, pos_ref, far_ref, feat_ref, out_ref, weight_ref, fits_ref):
    group, blk, wide = out_ref.shape
    near = wide // blk
    axes = 3
    step = pl.program_id(0)
    first = step * group

    @pl.when(step == 0)
    def _():
        far = jnp.maximum(
            jnp.max(jnp.abs(pos_ref[...].astype(jnp.float32))), jnp.max(far_ref[...])
        )
        fits_ref[0] = (far <= REACH).astype(jnp.int32)
        shape = (8, blk)

        def prepare(q, carry):
            p = pos_ref[q].astype(jnp.float32)
            for c in range(2):
                x, y, z = (
                    jnp.broadcast_to(p[c * axes + n : c * axes + n + 1], shape) for n in range(axes)
                )
                close, tilt = squares(x, y, z)
                a, t = pieces(close), pieces(tilt)
                lines = (
                    {0: -2.0 * x, 1: -2.0 * y, 2: -2.0 * z, 3: 1.0, 4: 1.0, 5: 1.0},
                    {1: a[0], 2: a[1], 3: a[2]},
                    {0: 2.0 * x, 1: 2.0 * y, 2: -4.0 * z, 6: 1.0, 7: 1.0},
                    {0: 1.0, 1: t[0], 2: t[1], 3: t[2]},
                )
                part = [rows_of(line, shape) for line in lines]
                left = jnp.concatenate(part[:2], 0)
                right = jnp.concatenate(part[2:], 0)
                both = jnp.concatenate([left, right], 1)
                weight_ref[2 * q + c] = both.astype(weight_ref.dtype)
            return carry

        lax.fori_loop(0, pos_ref.shape[0], prepare, 0, unroll=2)

    fits = fits_ref[0] > 0

    @pl.when(fits)
    def _():
        for b in range(group):
            for k in range(0, near, 2):
                both = [
                    jnp.dot(
                        feat_ref[b],
                        weight_ref[cols_ref[k + c, first + b]],
                        preferred_element_type=jnp.float32,
                    )
                    for c in range(2)
                ]
                for r in range(0, blk, 8):
                    pair = []
                    for part in both:
                        inv = lax.rsqrt(part[r : r + 8, :blk])
                        inv2 = inv * inv
                        pair.append((SCALE * part[r : r + 8, blk:]) * (inv2 * inv2) * inv)
                    out_ref[b, r : r + 8, k * blk : (k + 2) * blk] = jnp.concatenate(
                        pair, 1
                    ).astype(out_ref.dtype)

    @pl.when(jnp.logical_not(fits))
    def _():
        def one_reading(b, carry):
            place = feat_ref[b].astype(jnp.float32)
            rx, ry, rz = (
                jnp.broadcast_to(place[:, c : c + 1], (blk, blk)) for c in range(axes)
            )

            def one_block(k, carry):
                s = cols_ref[k, first + b]
                p = pos_ref[lax.div(s, 2)].astype(jnp.float32)
                odd = lax.rem(s, 2) > 0
                px, py, pz = (
                    jnp.where(odd, p[axes + c : axes + c + 1], p[c : c + 1]) for c in range(axes)
                )
                dx, dy, dz = rx - px, ry - py, rz - pz
                flat, up = dx * dx + dy * dy, dz * dz
                inv = lax.rsqrt(flat + up)
                inv2 = inv * inv
                value = (SCALE * (up + up - flat)) * (inv2 * inv2) * inv
                out_ref[b, :, pl.ds(pl.multiple_of(k * blk, blk), blk)] = value.astype(
                    out_ref.dtype
                )
                return carry

            return lax.fori_loop(0, near, one_block, carry)

        lax.fori_loop(0, group, one_reading, 0)


def kernel_values(near_cols, slot_p, far, feat):
    rb, blk, _ = feat.shape
    near = near_cols.shape[0]
    whole = lambda g, *_: (0, 0, 0)
    part = lambda g, *_: (g, 0, 0)
    return pl.pallas_call(
        make_kernels,
        grid_spec=pltpu.PrefetchScalarGridSpec(
            num_scalar_prefetch=1,
            grid=(rb // GEN,),
            in_specs=[
                pl.BlockSpec(slot_p.shape, whole),
                pl.BlockSpec(far.shape, lambda g, *_: (0, 0)),
                pl.BlockSpec((GEN, blk, ROWS), part),
            ],
            out_specs=pl.BlockSpec((GEN, blk, near * blk), part),
            scratch_shapes=[
                pltpu.VMEM((2 * slot_p.shape[0], ROWS, 2 * blk), jnp.bfloat16),
                pltpu.SMEM((1,), jnp.int32),
            ],
        ),
        out_shape=jax.ShapeDtypeStruct((rb, blk, near * blk), jnp.bfloat16),
        compiler_params=pltpu.CompilerParams(vmem_limit_bytes=VMEM),
        cost_estimate=pl.CostEstimate(
            flops=15 * rb * near * blk * blk,
            bytes_accessed=2 * rb * near * blk * blk,
            transcendentals=rb * near * blk * blk,
        ),
        name="kernel_values",
    )(near_cols, slot_p, far, feat)


def apply_both(cols_ref, slot_ref, me_ref, kern_ref, m_ref, *refs):
    *seen_refs, field_ref, adj_ref, total, obs_ref = refs
    group, blk, wide = kern_ref.shape
    near = wide // blk
    step = pl.program_id(0)
    tiles, rb, me = len(seen_refs), obs_ref.shape[0], me_ref[0]
    share = rb // tiles

    @pl.when(step == 0)
    def _():
        total[...] = jnp.zeros_like(total)
        for n, ref in enumerate(seen_refs):
            obs_ref[n * share : (n + 1) * share] = ref[...]

    residuals = []
    for b in range(group):
        i = step * group + b
        field = None
        for k in range(0, near, 2):
            part = lax.dot_general(
                jnp.concatenate([m_ref[cols_ref[k, i]], m_ref[cols_ref[k + 1, i]]], 1),
                kern_ref[b, :, k * blk : (k + 2) * blk],
                (((1,), (1,)), ((), ())),
                preferred_element_type=jnp.float32,
            )
            field = part if field is None else field + part
        field = field.astype(jnp.bfloat16)
        there = lax.div(slot_ref[i], rb)
        within = lax.rem(slot_ref[i], share)
        field_ref[lax.rem(there + tiles - me, tiles) * share + within] = field
        row = lax.rem(me + tiles - there, tiles) * share + within
        seen = obs_ref[row].astype(jnp.float32)
        residuals.append((field.astype(jnp.float32) - seen).astype(jnp.bfloat16))
    for b in range(group):
        i = step * group + b
        for k in range(0, near, 2):
            both = jnp.dot(
                residuals[b],
                kern_ref[b, :, k * blk : (k + 2) * blk],
                preferred_element_type=jnp.float32,
            )
            total[cols_ref[k, i]] += both[:, :blk]
            total[cols_ref[k + 1, i]] += both[:, blk:]

    @pl.when(step == pl.num_programs(0) - 1)
    def _():
        adj_ref[...] = total[...].astype(adj_ref.dtype)


def forward_adjoint(near_cols, grid_slot, me, kern, slot_m, seen):
    rb, blk, wide = kern.shape
    slots, width, _ = slot_m.shape
    whole = lambda g, *_: (0, 0, 0)
    return pl.pallas_call(
        apply_both,
        grid_spec=pltpu.PrefetchScalarGridSpec(
            num_scalar_prefetch=3,
            grid=(rb // USE,),
            in_specs=[
                pl.BlockSpec((USE, blk, wide), lambda g, *_: (g, 0, 0)),
                pl.BlockSpec(slot_m.shape, whole),
                *[pl.BlockSpec(part.shape, whole) for part in seen],
            ],
            out_specs=[pl.BlockSpec((rb, width, blk), whole), pl.BlockSpec((slots, width, blk), whole)],
            scratch_shapes=[
                pltpu.VMEM((slots, width, blk), jnp.float32),
                pltpu.VMEM((rb, width, blk), jnp.bfloat16),
            ],
        ),
        out_shape=[
            jax.ShapeDtypeStruct((rb, width, blk), jnp.bfloat16),
            jax.ShapeDtypeStruct((slots, width, blk), jnp.bfloat16),
        ],
        compiler_params=pltpu.CompilerParams(vmem_limit_bytes=VMEM),
        cost_estimate=pl.CostEstimate(
            flops=4 * width * rb * wide * blk, bytes_accessed=2 * rb * wide * blk, transcendentals=0
        ),
        name="forward_adjoint",
    )(near_cols, grid_slot, me, kern, slot_m, *seen)


def shift(block, axis, by, size):
    return lax.ppermute(block, axis, [(i, (i + by) % size) for i in range(size)])


def add_back(index_ref, count_ref, back_ref, out_ref):
    out_ref[...] = jnp.zeros_like(out_ref)

    def one(q, carry):
        for c in range(back_ref.shape[1]):
            value = back_ref[q, c].astype(jnp.float32)
            out_ref[index_ref[c, q]] += jnp.where(count_ref[q] > c, value, 0.0)
        return carry

    lax.fori_loop(0, back_ref.shape[0], one, 0, unroll=2)


def combine(send_index, send_count, back, old):
    _, _, width, depth = back.shape
    return pl.pallas_call(
        add_back,
        grid_spec=pltpu.PrefetchScalarGridSpec(
            num_scalar_prefetch=2,
            grid=(1,),
            in_specs=[pl.BlockSpec(back.shape, lambda g, *_: (0, 0, 0, 0))],
            out_specs=pl.BlockSpec((old, width, depth), lambda g, *_: (0, 0, 0)),
        ),
        out_shape=jax.ShapeDtypeStruct((old, width, depth), jnp.float32),
        compiler_params=pltpu.CompilerParams(vmem_limit_bytes=VMEM),
        name="combine",
    )(send_index, send_count, back)


def on_device(
    moments, dipole_pos, send_index, send_count, reading_pos, near_cols, grid_slot, observed
):
    peers = lax.axis_size("morton")
    tiles = lax.axis_size("tile")
    cap = send_index.shape[1]
    old, width, depth = moments.shape
    rb = reading_pos.shape[0]
    share = rb // tiles
    swap = functools.partial(lax.all_to_all, split_axis=0, concat_axis=0, tiled=True)
    send_index, near_cols = send_index.T, near_cols.T
    dipole_pos, reading_pos = (jnp.swapaxes(a, 0, 1) for a in (dipole_pos, reading_pos))
    send_p = picked(
        pick_places,
        (send_index,),
        dipole_pos,
        (peers, 8, depth),
        [pltpu.VMEM(dipole_pos.shape, jnp.float32)],
        "pick_places",
    )
    send_m = picked(
        pick_moments,
        (send_index, send_count),
        moments,
        (peers, cap, width, depth),
        [],
        "pick_moments",
    )
    slot_p = swap(send_p, "morton")
    feat, far = features(reading_pos)
    feat, observed = lax.optimization_barrier((feat, observed))
    me = lax.axis_index("tile")
    seen = [
        lax.dynamic_slice_in_dim(observed, (me + by) % tiles * share, share, 0)
        for by in range(tiles)
    ]
    slot_p, *seen = lax.optimization_barrier((slot_p, *seen))
    send_m, feat, *seen = lax.optimization_barrier((send_m, feat, *seen))
    seen = [shift(part, "tile", by, tiles) if by else part for by, part in enumerate(seen)]
    slot_m = swap(send_m, "morton").reshape(peers * cap, width, depth)
    kern = kernel_values(near_cols, slot_p, far, feat)
    ordered, slot_adj = forward_adjoint(near_cols, grid_slot, me.reshape(1), kern, slot_m, seen)
    back = swap(slot_adj.reshape(peers, cap, width, depth), "morton")
    field = jnp.zeros_like(ordered)
    for by in range(tiles):
        part = ordered[by * share : (by + 1) * share]
        part = shift(part, "tile", by, tiles) if by else part
        field = lax.dynamic_update_slice_in_dim(field, part, (me - by) % tiles * share, 0)
    adjoint_moments = combine(send_index, send_count, back, old)
    return (field, adjoint_moments)


def solution(mesh):
    return jax.shard_map(
        on_device,
        mesh=mesh,
        in_specs=(
            P(("morton", "tile"), None, None),
            P(("morton", "tile"), None, None),
            P(("morton", "tile"), None),
            P(("morton", "tile")),
            P(("morton", "tile"), None, None),
            P(("morton", "tile"), None),
            P(("morton", "tile")),
            P(("morton", "tile"), None, None),
        ),
        out_specs=(P(("morton", "tile"), None, None), P(("morton", "tile"), None, None)),
        check_vma=False,
    )
```

time: 132 us -> 129 us (0.977)
  local copies, waits for them, and re-layouts: 16.2 us -> 4.76 us
  waiting for transfers between devices: 14 us -> 20.7 us
  Pallas kernels: 49.8 us -> 54.9 us
  other arithmetic: 2.55 us -> 0 us
    ppermute x14, waiting for transfers between devices: 2.12 us -> 8.98 us  [shift(): lax.ppermute(block, axis, [(i, (i + by) % size) for i in range(size)])]
    pallas_call x0 -> x2, Pallas kernels: none -> 5.2 us  [picked(): pl.pallas_call(kernel, grid_spec=pltpu.PrefetchScalarGridSpec(num_scalar_...]
    dynamic_update_slice x7, local copies, waits for them, and re-layouts: 4.65 us -> 0.13 us  [on_device(): lax.dynamic_update_slice_in_dim(field, part, (me - by) % tiles * share, 0)]
    unnamed x11 -> x14, local copies, waits for them, and re-layouts: 4.33 us -> 1.51 us
    ppermute x14, starting transfers between devices: 20.1 us -> 17.5 us  [shift(): lax.ppermute(block, axis, [(i, (i + by) % size) for i in range(size)])]
    gather x2 -> x0, local copies, waits for them, and re-layouts: 2.26 us -> none  [the longest x1 1.51 us: on_device(): send_p = dipole_pos[flat_index]]
    all_to_all x3, starting transfers between devices: 27.5 us -> 29.5 us  [the longest x1 11.7 us: on_device(): slot_p = swap(send_p, 'morton')]
  transfers between devices with their start and end apart: 17 -> 17, of which waited for: 3 -> 9; matrix products, arithmetic and copies ran while one was open for 11% -> 3% of each run, Pallas kernels for 18% -> 20%
where the time goes in v3:
time: 129 us; the launch traced here: 128 us
  Pallas kernels  54.9 us (43%)
  starting transfers between devices  47 us (36%)
  waiting for transfers between devices  20.7 us (16%)
  local copies, waits for them, and re-layouts  4.76 us (4%)
    pallas_call x1, Pallas kernels, forward_adjoint(): pl.pallas_call(apply_both, grid_spec=pltpu.PrefetchScalarGridSpec(num_sca...  24.5 us
    pallas_call x1, Pallas kernels, kernel_values(): pl.pallas_call(make_kernels, grid_spec=pltpu.PrefetchScalarGridSpec(num_s...  22.2 us
    ppermute x14, starting transfers between devices, shift(): lax.ppermute(block, axis, [(i, (i + by) % size) for i in range(size)])  17.5 us
    all_to_all x1, starting transfers between devices, on_device(): slot_p = swap(send_p, 'morton')  11.7 us
    all_to_all x1, waiting for transfers between devices, on_device(): back = swap(slot_adj.reshape(peers, cap, width, depth), 'morton')  9.92 us
    all_to_all x1, starting transfers between devices, on_device(): back = swap(slot_adj.reshape(peers, cap, width, depth), 'morton')  9.77 us
    ppermute x14, waiting for transfers between devices, shift(): lax.ppermute(block, axis, [(i, (i + by) % size) for i in range(size)])  8.98 us
    all_to_all x1, starting transfers between devices, on_device(): slot_m = swap(send_m, 'morton').reshape(peers * cap, width, depth)  8.01 us
  transfers between devices with their start and end apart: 17, of which 9 were waited for; matrix products, arithmetic and copies ran while one was open for 3% of the time, Pallas kernels for 20%

profile of v3, /device:TPU:8, one launch (start us, length us, event | category | flops | bytes accessed | tf_op | source)
XLA Modules:
  0.0 128.4 jit_solution(11996889510517927069)
XLA Ops:
  0.6 0.0 copy-start.2
  0.7 2.3 %pick_places.1 = bf16[32,8,128]{2,1,0:T(8,128)(2,1)} custom-call(s32[2,32]{1,0:T(2,128)} %bitcast.10, bf16[3,32,128]{2,1,0:T(8,128)(2,1)} %bitcast.13), custom_call_target="tpu_custom_call" | custom-call | bytes 1024 | tf_op jit(solution)/shard_map/pick_places/pallas_call | solution.py:41
  2.9 11.7 %all-to-all-start = ((bf16[32,8,128]{2,1,0:T(8,128)(2,1)}), bf16[32,8,128]{2,1,0:T(8,128)(2,1)S(1)}, u32[]{:S(2)}, u32[]{:S(2)}) async-start(bf16[32,8,128]{2,1,0:T(8,128)(2,1)} %pick_places.1), calls=%async_computation | async-start | bytes 131072 | tf_op jit(solution)/shard_map/all_to_all | solution.py:380
  14.8 0.0 copy-start
  14.8 0.8 copy-done
  15.6 1.0 features.1
  16.6 2.9 %pick_moments.1 = bf16[32,2,64,128]{3,2,1,0:T(8,128)(2,1)} custom-call(s32[2,32]{1,0:T(2,128)} %bitcast.11, s32[32]{0:T(128)} %count_ref.3, bf16[32,64,128]{2,1,0:T(8,128)(2,1)} %m_ref.1), custom_call_target="tpu_custom_call" | custom-call | bytes 1024 | tf_op jit(solution)/shard_map/pick_moments/pallas_call | solution.py:41
  19.5 2.0 %constant_dynamic-slice_fusion = (bf16[8,64,128]{2,1,0:T(8,128)(2,1)S(1)}, bf16[8,64,128]{2,1,0:T(8,128)(2,1)S(1)}, bf16[8,64,128]{2,1,0:T(8,128)(2,1)}, bf16[8,...) fusion(bf16[64,64,128]{2,1,0:T(8,128)(2,1)} %param.15, ...), kind=kLoop, calls=%fused_computation.8 | loop fusion | bytes 2097184 | tf_op jit(solution)/shard_map/dynamic_slice | solution.py:385
  21.5 1.8 %all-to-all-done.pos_ref = bf16[32,8,128]{2,1,0:T(8,128)(2,1)S(1)} async-done(((bf16[32,8,128]{2,1,0:T(8,128)(2,1)}), bf16[32,8,128]{2,1,0:T(8,128)(2,1)S(1)}, u32[]{:S(2)}, u32[]{:S(2)}) %all-to-all-start) | async-done | bytes 65568 | tf_op jit(solution)/shard_map/all_to_all | solution.py:380
  23.3 8.0 %all-to-all-start.1 = ((bf16[32,2,64,128]{3,2,1,0:T(8,128)(2,1)}), bf16[32,2,64,128]{3,2,1,0:T(8,128)(2,1)}, u32[]{:S(2)}, u32[]{:S(2)}) async-start(bf16[32,2,64,128]{3,2,1,0:T(8,128)(2,1)} %pick_moments.1), calls=%async_computation.1 | async-start | bytes 2097152 | tf_op jit(solution)/shard_map/all_to_all | solution.py:391
  31.4 0.0 collective-permute-start
  31.4 1.6 %collective-permute-start.1 = (bf16[8,64,128]{2,1,0:T(8,128)(2,1)S(1)}, bf16[8,64,128]{2,1,0:T(8,128)(2,1)S(1)}, u32[]{:S(2)}, u32[]{:S(2)}) collective-permute-start(bf16[8,64,128]{2,1,0:T(8,128)(2,1)S(1)} %get-tuple-element.44), channel_id=1, source_target_pairs={{0,2},{1,3},{2,4},{3,5},{4,6},{5,7},{6,0},{7,1},{8,10},{9,11},{10,... | collective-permute-start | bytes 393224 | tf_op jit(solution)/shard_map/ppermute | solution.py:321
  32.9 2.0 %collective-permute-start.2 = (bf16[8,64,128]{2,1,0:T(8,128)(2,1)}, bf16[8,64,128]{2,1,0:T(8,128)(2,1)S(1)}, u32[]{:S(2)}, u32[]{:S(2)}) collective-permute-start(bf16[8,64,128]{2,1,0:T(8,128)(2,1)} %get-tuple-element.45), channel_id=1, source_target_pairs={{0,3},{1,4},{2,5},{3,6},{4,7},{5,0},{6,1},{7,2},{8,11},{9,12},{10,... | collective-permute-start | bytes 393224 | tf_op jit(solution)/shard_map/ppermute | solution.py:321
  35.0 2.0 %collective-permute-start.3 = (bf16[8,64,128]{2,1,0:T(8,128)(2,1)}, bf16[8,64,128]{2,1,0:T(8,128)(2,1)S(1)}, u32[]{:S(2)}, u32[]{:S(2)}) collective-permute-start(bf16[8,64,128]{2,1,0:T(8,128)(2,1)} %get-tuple-element.46), channel_id=1, source_target_pairs={{0,4},{1,5},{2,6},{3,7},{4,0},{5,1},{6,2},{7,3},{8,12},{9,13},{10,... | collective-permute-start | bytes 393224 | tf_op jit(solution)/shard_map/ppermute | solution.py:321
  37.0 1.7 %collective-permute-start.4 = (bf16[8,64,128]{2,1,0:T(8,128)(2,1)}, bf16[8,64,128]{2,1,0:T(8,128)(2,1)S(1)}, u32[]{:S(2)}, u32[]{:S(2)}) collective-permute-start(bf16[8,64,128]{2,1,0:T(8,128)(2,1)} %get-tuple-element.47), channel_id=1, source_target_pairs={{0,5},{1,6},{2,7},{3,0},{4,1},{5,2},{6,3},{7,4},{8,13},{9,14},{10,... | collective-permute-start | bytes 393224 | tf_op jit(solution)/shard_map/ppermute | solution.py:321
  38.6 0.0 collective-permute-done.refs_1_
  38.7 1.4 %collective-permute-start.5 = (bf16[8,64,128]{2,1,0:T(8,128)(2,1)S(1)}, bf16[8,64,128]{2,1,0:T(8,128)(2,1)S(1)}, u32[]{:S(2)}, u32[]{:S(2)}) collective-permute-start(bf16[8,64,128]{2,1,0:T(8,128)(2,1)S(1)} %get-tuple-element.48), channel_id=1, source_target_pairs={{0,6},{1,7},{2,0},{3,1},{4,2},{5,3},{6,4},{7,5},{8,14},{9,15},{10,... | collective-permute-start | bytes 393224 | tf_op jit(solution)/shard_map/ppermute | solution.py:321
  40.1 0.0 collective-permute-done.1.refs_2_
  40.1 1.8 %collective-permute-start.6 = (bf16[8,64,128]{2,1,0:T(8,128)(2,1)S(1)}, bf16[8,64,128]{2,1,0:T(8,128)(2,1)S(1)}, u32[]{:S(2)}, u32[]{:S(2)}) collective-permute-start(bf16[8,64,128]{2,1,0:T(8,128)(2,1)S(1)} %get-tuple-element.49), channel_id=1, source_target_pairs={{0,7},{1,0},{2,1},{3,2},{4,3},{5,4},{6,5},{7,6},{8,15},{9,8},{10,9... | collective-permute-start | bytes 393224 | tf_op jit(solution)/shard_map/ppermute | solution.py:321
  41.9 0.7 copy-done.1
  42.6 22.2 %kernel_values.1.kern_ref = bf16[64,128,2048]{2,1,0:T(8,128)(2,1)} custom-call(s32[16,64]{1,0:T(8,128)S(1)} %bitcast.8, bf16[32,8,128]{2,1,0:T(8,128)(2,1)S(1)} %all-to-all-done.pos_ref, f32[8,128]{1,0:T(8,128)S(1)} %get-tuple-element.30.far_ref, bf16[64,128,16]{2,1,0:T(8,128)(2,1)S(1)} %get-tuple-element.40.feat_ref), custom_call_target="tpu_custom_call" | custom-call | flops 251658240 | bytes 33554432 | tf_op jit(solution)/shard_map/kernel_values/pallas_call | solution.py:212
  64.9 0.0 collective-permute-done.2.refs_3_
  64.9 0.0 collective-permute-done.3.refs_4_
  64.9 0.0 collective-permute-done.4.refs_5_
  64.9 0.0 collective-permute-done.5.refs_6_
  64.9 0.0 collective-permute-done.6.refs_7_
  64.9 0.0 all-to-all-done.1
  64.9 24.5 %forward_adjoint.1 = (bf16[64,64,128]{2,1,0:T(8,128)(2,1)S(1)}, bf16[64,64,128]{2,1,0:T(8,128)(2,1)}) custom-call(s32[16,64]{1,0:T(8,128)S(1)} %bitcast.9, s32[64]{0:T(128)S(1)} %copy-done.5, s32[1]{0:T(128)} %bitcast.1.me_ref, bf16[64,128,2048]{2,1,0:T(8,128)(2,1)} %kernel_values.1.kern_ref, bf16[64,64,128]{2,1,0:T(8,128)(2,1)} %bitcast.5.m_ref, ...), custom_call_target="tpu_custom_call" | custom-call | flops 4294967296 | bytes 33554432 | tf_op jit(solution)/shard_map/forward_adjoint/pallas_call | solution.py:292
  89.5 9.8 %all-to-all-start.2 = ((bf16[32,2,64,128]{3,2,1,0:T(8,128)(2,1)}), bf16[32,2,64,128]{3,2,1,0:T(8,128)(2,1)S(1)}, u32[]{:S(2)}, u32[]{:S(2)}) async-start(bf16[32,2,64,128]{3,2,1,0:T(8,128)(2,1)} %bitcast.6), calls=%async_computation.2 | async-start | bytes 2097152 | tf_op jit(solution)/shard_map/all_to_all | solution.py:394
  99.3 0.2 broadcast_in_dim.3
  99.5 0.8 fusion
  100.4 0.0 collective-permute-start.7
  100.4 0.5 collective-permute-start.8
  100.9 1.2 collective-permute-start.9
  102.1 2.9 %collective-permute-start.10 = (bf16[8,64,128]{2,1,0:T(8,128)(2,1)}, bf16[8,64,128]{2,1,0:T(8,128)(2,1)S(1)}, u32[]{:S(2)}, u32[]{:S(2)}) collective-permute-start(bf16[8,64,128]{2,1,0:T(8,128)(2,1)} %get-tuple-element.55), channel_id=1, source_target_pairs={{0,4},{1,5},{2,6},{3,7},{4,0},{5,1},{6,2},{7,3},{8,12},{9,13},{10,... | collective-permute-start | bytes 393224 | tf_op jit(solution)/shard_map/ppermute | solution.py:321
  105.0 0.7 collective-permute-start.11
  105.7 1.3 %collective-permute-done.7 = bf16[8,64,128]{2,1,0:T(8,128)(2,1)S(1)} collective-permute-done((bf16[8,64,128]{2,1,0:T(8,128)(2,1)}, bf16[8,64,128]{2,1,0:T(8,128)(2,1)S(1)}, u32[]{:S(2)}, u32[]{:S(2)}) %collective-permute-start.7) | collective-permute-done | bytes 131104 | tf_op jit(solution)/shard_map/ppermute | solution.py:321
  107.0 0.1 collective-permute-start.12
  107.2 0.9 collective-permute-done.8
  108.1 1.5 %collective-permute-start.13 = (bf16[8,64,128]{2,1,0:T(8,128)(2,1)S(1)}, bf16[8,64,128]{2,1,0:T(8,128)(2,1)S(1)}, u32[]{:S(2)}, u32[]{:S(2)}) collective-permute-start(bf16[8,64,128]{2,1,0:T(8,128)(2,1)S(1)} %get-tuple-element.52), channel_id=1, source_target_pairs={{0,7},{1,0},{2,1},{3,2},{4,3},{5,4},{6,5},{7,6},{8,15},{9,8},{10,9... | collective-permute-start | bytes 393224 | tf_op jit(solution)/shard_map/ppermute | solution.py:321
  109.6 2.2 %collective-permute-done.9 = bf16[8,64,128]{2,1,0:T(8,128)(2,1)S(1)} collective-permute-done((bf16[8,64,128]{2,1,0:T(8,128)(2,1)}, bf16[8,64,128]{2,1,0:T(8,128)(2,1)S(1)}, u32[]{:S(2)}, u32[]{:S(2)}) %collective-permute-start.9) | collective-permute-done | bytes 131104 | tf_op jit(solution)/shard_map/ppermute | solution.py:321
  111.9 1.1 collective-permute-done.10
  113.0 0.4 collective-permute-done.11
  113.4 1.5 %collective-permute-done.12 = bf16[8,64,128]{2,1,0:T(8,128)(2,1)S(1)} collective-permute-done((bf16[8,64,128]{2,1,0:T(8,128)(2,1)S(1)}, bf16[8,64,128]{2,1,0:T(8,128)(2,1)S(1)}, u32[]{:S(2)}, u32[]{:S(2)}) %collective-permute-start.12) | collective-permute-done | bytes 131104 | tf_op jit(solution)/shard_map/ppermute | solution.py:321
  114.9 1.5 %collective-permute-done.13 = bf16[8,64,128]{2,1,0:T(8,128)(2,1)S(1)} collective-permute-done((bf16[8,64,128]{2,1,0:T(8,128)(2,1)S(1)}, bf16[8,64,128]{2,1,0:T(8,128)(2,1)S(1)}, u32[]{:S(2)}, u32[]{:S(2)}) %collective-permute-start.13) | collective-permute-done | bytes 131104 | tf_op jit(solution)/shard_map/ppermute | solution.py:321
  116.4 0.0 copy-start.6
  116.4 9.9 %all-to-all-done.2.back_ref = bf16[32,2,64,128]{3,2,1,0:T(8,128)(2,1)S(1)} async-done(((bf16[32,2,64,128]{3,2,1,0:T(8,128)(2,1)}), bf16[32,2,64,128]{3,2,1,0:T(8,128)(2,1)S(1)}, u32[]{:S(2)}, u32[]{:S(2)}) %all-to-all-start.2) | async-done | bytes 1048608 | tf_op jit(solution)/shard_map/all_to_all | solution.py:394
  126.4 2.0 %combine.1 = f32[32,64,128]{2,1,0:T(8,128)} custom-call(s32[2,32]{1,0:T(2,128)S(1)} %bitcast.12, s32[32]{0:T(128)S(1)} %copy-done.4, bf16[32,2,64,128]{3,2,1,0:T(8,128)(2,1)S(1)} %all-to-all-done.2.back_ref), custom_call_target="tpu_custom_call" | custom-call | tf_op jit(solution)/shard_map/combine/pallas_call | solution.py:338
  (16 shorter events, 0.1 us)
Async XLA Ops:
  0.6 64.3 %copy-start.2 = (s32[64,16]{0,1:T(8,128)S(1)}, s32[64,16]{0,1:T(8,128)}, u32[]{:S(2)}) copy-start(s32[64,16]{0,1:T(8,128)} %param.13) | copy-start | bytes 12292
  0.6 64.3 %copy-start.5 = (s32[64]{0:T(128)S(1)}, s32[64]{0:T(128)}, u32[]{:S(2)}) copy-start(s32[64]{0:T(128)} %slot_ref.1) | copy-start | bytes 772
  2.9 20.4 %all-to-all-start = ((bf16[32,8,128]{2,1,0:T(8,128)(2,1)}), bf16[32,8,128]{2,1,0:T(8,128)(2,1)S(1)}, u32[]{:S(2)}, u32[]{:S(2)}) async-start(bf16[32,8,128]{2,1,0:T(8,128)(2,1)} %pick_places.1), calls=%async_computation | async-start | bytes 131072 | tf_op jit(solution)/shard_map/all_to_all | solution.py:380
  14.8 0.8 copy-start
  23.3 41.6 %all-to-all-start.1 = ((bf16[32,2,64,128]{3,2,1,0:T(8,128)(2,1)}), bf16[32,2,64,128]{3,2,1,0:T(8,128)(2,1)}, u32[]{:S(2)}, u32[]{:S(2)}) async-start(bf16[32,2,64,128]{3,2,1,0:T(8,128)(2,1)} %pick_moments.1), calls=%async_computation.1 | async-start | bytes 2097152 | tf_op jit(solution)/shard_map/all_to_all | solution.py:391
  31.4 7.3 %collective-permute-start = (bf16[8,64,128]{2,1,0:T(8,128)(2,1)S(1)}, bf16[8,64,128]{2,1,0:T(8,128)(2,1)S(1)}, u32[]{:S(2)}, u32[]{:S(2)}) collective-permute-start(bf16[8,64,128]{2,1,0:T(8,128)(2,1)S(1)} %get-tuple-element.43), channel_id=1, source_target_pairs={{0,1},{1,2},{2,3},{3,4},{4,5},{5,6},{6,7},{7,0},{8,9},{9,10},{10,1... | collective-permute-start | bytes 393224 | tf_op jit(solution)/shard_map/ppermute | solution.py:321
  31.4 8.7 %collective-permute-start.1 = (bf16[8,64,128]{2,1,0:T(8,128)(2,1)S(1)}, bf16[8,64,128]{2,1,0:T(8,128)(2,1)S(1)}, u32[]{:S(2)}, u32[]{:S(2)}) collective-permute-start(bf16[8,64,128]{2,1,0:T(8,128)(2,1)S(1)} %get-tuple-element.44), channel_id=1, source_target_pairs={{0,2},{1,3},{2,4},{3,5},{4,6},{5,7},{6,0},{7,1},{8,10},{9,11},{10,... | collective-permute-start | bytes 393224 | tf_op jit(solution)/shard_map/ppermute | solution.py:321
  32.9 31.9 %collective-permute-start.2 = (bf16[8,64,128]{2,1,0:T(8,128)(2,1)}, bf16[8,64,128]{2,1,0:T(8,128)(2,1)S(1)}, u32[]{:S(2)}, u32[]{:S(2)}) collective-permute-start(bf16[8,64,128]{2,1,0:T(8,128)(2,1)} %get-tuple-element.45), channel_id=1, source_target_pairs={{0,3},{1,4},{2,5},{3,6},{4,7},{5,0},{6,1},{7,2},{8,11},{9,12},{10,... | collective-permute-start | bytes 393224 | tf_op jit(solution)/shard_map/ppermute | solution.py:321
  35.0 29.9 %collective-permute-start.3 = (bf16[8,64,128]{2,1,0:T(8,128)(2,1)}, bf16[8,64,128]{2,1,0:T(8,128)(2,1)S(1)}, u32[]{:S(2)}, u32[]{:S(2)}) collective-permute-start(bf16[8,64,128]{2,1,0:T(8,128)(2,1)} %get-tuple-element.46), channel_id=1, source_target_pairs={{0,4},{1,5},{2,6},{3,7},{4,0},{5,1},{6,2},{7,3},{8,12},{9,13},{10,... | collective-permute-start | bytes 393224 | tf_op jit(solution)/shard_map/ppermute | solution.py:321
  37.0 27.9 %collective-permute-start.4 = (bf16[8,64,128]{2,1,0:T(8,128)(2,1)}, bf16[8,64,128]{2,1,0:T(8,128)(2,1)S(1)}, u32[]{:S(2)}, u32[]{:S(2)}) collective-permute-start(bf16[8,64,128]{2,1,0:T(8,128)(2,1)} %get-tuple-element.47), channel_id=1, source_target_pairs={{0,5},{1,6},{2,7},{3,0},{4,1},{5,2},{6,3},{7,4},{8,13},{9,14},{10,... | collective-permute-start | bytes 393224 | tf_op jit(solution)/shard_map/ppermute | solution.py:321
  38.7 26.2 %collective-permute-start.5 = (bf16[8,64,128]{2,1,0:T(8,128)(2,1)S(1)}, bf16[8,64,128]{2,1,0:T(8,128)(2,1)S(1)}, u32[]{:S(2)}, u32[]{:S(2)}) collective-permute-start(bf16[8,64,128]{2,1,0:T(8,128)(2,1)S(1)} %get-tuple-element.48), channel_id=1, source_target_pairs={{0,6},{1,7},{2,0},{3,1},{4,2},{5,3},{6,4},{7,5},{8,14},{9,15},{10,... | collective-permute-start | bytes 393224 | tf_op jit(solution)/shard_map/ppermute | solution.py:321
  40.1 24.8 %collective-permute-start.6 = (bf16[8,64,128]{2,1,0:T(8,128)(2,1)S(1)}, bf16[8,64,128]{2,1,0:T(8,128)(2,1)S(1)}, u32[]{:S(2)}, u32[]{:S(2)}) collective-permute-start(bf16[8,64,128]{2,1,0:T(8,128)(2,1)S(1)} %get-tuple-element.49), channel_id=1, source_target_pairs={{0,7},{1,0},{2,1},{3,2},{4,3},{5,4},{6,5},{7,6},{8,15},{9,8},{10,9... | collective-permute-start | bytes 393224 | tf_op jit(solution)/shard_map/ppermute | solution.py:321
  41.9 0.7 copy-start.1
  42.6 83.7 %copy-start.3 = (s32[32,2]{0,1:T(2,128)S(1)}, s32[32,2]{0,1:T(2,128)}, u32[]{:S(2)}) copy-start(s32[32,2]{0,1:T(2,128)} %param.10) | copy-start | bytes 772
  42.6 83.7 %copy-start.4 = (s32[32]{0:T(128)S(1)}, s32[32]{0:T(128)}, u32[]{:S(2)}) copy-start(s32[32]{0:T(128)} %count_ref.3) | copy-start | bytes 388
  89.5 36.9 %all-to-all-start.2 = ((bf16[32,2,64,128]{3,2,1,0:T(8,128)(2,1)}), bf16[32,2,64,128]{3,2,1,0:T(8,128)(2,1)S(1)}, u32[]{:S(2)}, u32[]{:S(2)}) async-start(bf16[32,2,64,128]{3,2,1,0:T(8,128)(2,1)} %bitcast.6), calls=%async_computation.2 | async-start | bytes 2097152 | tf_op jit(solution)/shard_map/all_to_all | solution.py:394
  100.4 6.7 %collective-permute-start.7 = (bf16[8,64,128]{2,1,0:T(8,128)(2,1)}, bf16[8,64,128]{2,1,0:T(8,128)(2,1)S(1)}, u32[]{:S(2)}, u32[]{:S(2)}) collective-permute-start(bf16[8,64,128]{2,1,0:T(8,128)(2,1)} %get-tuple-element.58), channel_id=1, source_target_pairs={{0,1},{1,2},{2,3},{3,4},{4,5},{5,6},{6,7},{7,0},{8,9},{9,10},{10,1... | collective-permute-start | bytes 393224 | tf_op jit(solution)/shard_map/ppermute | solution.py:321
  100.4 7.8 %collective-permute-start.8 = (bf16[8,64,128]{2,1,0:T(8,128)(2,1)}, bf16[8,64,128]{2,1,0:T(8,128)(2,1)S(1)}, u32[]{:S(2)}, u32[]{:S(2)}) collective-permute-start(bf16[8,64,128]{2,1,0:T(8,128)(2,1)} %get-tuple-element.57), channel_id=1, source_target_pairs={{0,2},{1,3},{2,4},{3,5},{4,6},{5,7},{6,0},{7,1},{8,10},{9,11},{10,... | collective-permute-start | bytes 393224 | tf_op jit(solution)/shard_map/ppermute | solution.py:321
  100.9 10.9 %collective-permute-start.9 = (bf16[8,64,128]{2,1,0:T(8,128)(2,1)}, bf16[8,64,128]{2,1,0:T(8,128)(2,1)S(1)}, u32[]{:S(2)}, u32[]{:S(2)}) collective-permute-start(bf16[8,64,128]{2,1,0:T(8,128)(2,1)} %get-tuple-element.56), channel_id=1, source_target_pairs={{0,3},{1,4},{2,5},{3,6},{4,7},{5,0},{6,1},{7,2},{8,11},{9,12},{10,... | collective-permute-start | bytes 393224 | tf_op jit(solution)/shard_map/ppermute | solution.py:321
  102.1 10.8 %collective-permute-start.10 = (bf16[8,64,128]{2,1,0:T(8,128)(2,1)}, bf16[8,64,128]{2,1,0:T(8,128)(2,1)S(1)}, u32[]{:S(2)}, u32[]{:S(2)}) collective-permute-start(bf16[8,64,128]{2,1,0:T(8,128)(2,1)} %get-tuple-element.55), channel_id=1, source_target_pairs={{0,4},{1,5},{2,6},{3,7},{4,0},{5,1},{6,2},{7,3},{8,12},{9,13},{10,... | collective-permute-start | bytes 393224 | tf_op jit(solution)/shard_map/ppermute | solution.py:321
  105.0 8.4 %collective-permute-start.11 = (bf16[8,64,128]{2,1,0:T(8,128)(2,1)}, bf16[8,64,128]{2,1,0:T(8,128)(2,1)S(1)}, u32[]{:S(2)}, u32[]{:S(2)}) collective-permute-start(bf16[8,64,128]{2,1,0:T(8,128)(2,1)} %get-tuple-element.54), channel_id=1, source_target_pairs={{0,5},{1,6},{2,7},{3,0},{4,1},{5,2},{6,3},{7,4},{8,13},{9,14},{10,... | collective-permute-start | bytes 393224 | tf_op jit(solution)/shard_map/ppermute | solution.py:321
  107.0 7.8 %collective-permute-start.12 = (bf16[8,64,128]{2,1,0:T(8,128)(2,1)S(1)}, bf16[8,64,128]{2,1,0:T(8,128)(2,1)S(1)}, u32[]{:S(2)}, u32[]{:S(2)}) collective-permute-start(bf16[8,64,128]{2,1,0:T(8,128)(2,1)S(1)} %get-tuple-element.53), channel_id=1, source_target_pairs={{0,6},{1,7},{2,0},{3,1},{4,2},{5,3},{6,4},{7,5},{8,14},{9,15},{10,... | collective-permute-start | bytes 393224 | tf_op jit(solution)/shard_map/ppermute | solution.py:321
  108.1 8.3 %collective-permute-start.13 = (bf16[8,64,128]{2,1,0:T(8,128)(2,1)S(1)}, bf16[8,64,128]{2,1,0:T(8,128)(2,1)S(1)}, u32[]{:S(2)}, u32[]{:S(2)}) collective-permute-start(bf16[8,64,128]{2,1,0:T(8,128)(2,1)S(1)} %get-tuple-element.52), channel_id=1, source_target_pairs={{0,7},{1,0},{2,1},{3,2},{4,3},{5,4},{6,5},{7,6},{8,15},{9,8},{10,9... | collective-permute-start | bytes 393224 | tf_op jit(solution)/shard_map/ppermute | solution.py:321
  116.4 11.9 %copy-start.6 = (bf16[64,64,128]{2,1,0:T(8,128)(2,1)}, bf16[64,64,128]{2,1,0:T(8,128)(2,1)S(1)}, u32[]{:S(2)}) copy-start(bf16[64,64,128]{2,1,0:T(8,128)(2,1)S(1)} %constant_dynamic-update-slice_fusion) | copy-start | bytes 3145732

commit v4 on v3

--- a/solution.py
+++ b/solution.py
@@ -11,6 +11,7 @@
 REACH = 64.0
 GEN = 8
 USE = 8
+LAG = 3
 ROWS = 16
 VMEM = 50 * 2**20
 
@@ -250,8 +251,7 @@
         for n, ref in enumerate(seen_refs):
             obs_ref[n * share : (n + 1) * share] = ref[...]
 
-    residuals = []
-    for b in range(group):
+    def forward(b):
         i = step * group + b
         field = None
         for k in range(0, near, 2):
@@ -268,17 +268,26 @@
         field_ref[lax.rem(there + tiles - me, tiles) * share + within] = field
         row = lax.rem(me + tiles - there, tiles) * share + within
         seen = obs_ref[row].astype(jnp.float32)
-        residuals.append((field.astype(jnp.float32) - seen).astype(jnp.bfloat16))
-    for b in range(group):
+        return (field.astype(jnp.float32) - seen).astype(jnp.bfloat16)
+
+    def adjoint(b, residual):
         i = step * group + b
         for k in range(0, near, 2):
             both = jnp.dot(
-                residuals[b],
+                residual,
                 kern_ref[b, :, k * blk : (k + 2) * blk],
                 preferred_element_type=jnp.float32,
             )
             total[cols_ref[k, i]] += both[:, :blk]
             total[cols_ref[k + 1, i]] += both[:, blk:]
+
+    residuals = []
+    for b in range(group):
+        residuals.append(forward(b))
+        if b >= LAG:
+            adjoint(b - LAG, residuals[b - LAG])
+    for b in range(group - LAG, group):
+        adjoint(b, residuals[b])
 
     @pl.when(step == pl.num_programs(0) - 1)
     def _():

time: 129 us -> 127 us (0.984)
  Pallas kernels: 54.9 us -> 53 us
    pallas_call x1, Pallas kernels: 24.5 us -> 22.6 us  [forward_adjoint(): pl.pallas_call(apply_both, grid_spec=pltpu.PrefetchScalarGridSpec(num_sca...]
  transfers between devices with their start and end apart: 17 -> 17, of which waited for: 9 -> 9; matrix products, arithmetic and copies ran while one was open for 3% -> 3% of each run, Pallas kernels for 20% -> 21%
where the time goes in v4:
time: 127 us; the launch traced here: 126 us
  Pallas kernels  53 us (42%)
  starting transfers between devices  47 us (37%)
  waiting for transfers between devices  20.7 us (16%)
  local copies, waits for them, and re-layouts  4.76 us (4%)
    pallas_call x1, Pallas kernels, forward_adjoint(): pl.pallas_call(apply_both, grid_spec=pltpu.PrefetchScalarGridSpec(num_sca...  22.6 us
    pallas_call x1, Pallas kernels, kernel_values(): pl.pallas_call(make_kernels, grid_spec=pltpu.PrefetchScalarGridSpec(num_s...  22.2 us
    ppermute x14, starting transfers between devices, shift(): lax.ppermute(block, axis, [(i, (i + by) % size) for i in range(size)])  17.5 us
    all_to_all x1, starting transfers between devices, on_device(): slot_p = swap(send_p, 'morton')  11.7 us
    all_to_all x1, waiting for transfers between devices, on_device(): back = swap(slot_adj.reshape(peers, cap, width, depth), 'morton')  9.91 us
    all_to_all x1, starting transfers between devices, on_device(): back = swap(slot_adj.reshape(peers, cap, width, depth), 'morton')  9.73 us
    ppermute x14, waiting for transfers between devices, shift(): lax.ppermute(block, axis, [(i, (i + by) % size) for i in range(size)])  8.98 us
    all_to_all x1, starting transfers between devices, on_device(): slot_m = swap(send_m, 'morton').reshape(peers * cap, width, depth)  8.01 us
  transfers between devices with their start and end apart: 17, of which 9 were waited for; matrix products, arithmetic and copies ran while one was open for 3% of the time, Pallas kernels for 21%

profile of v4, /device:TPU:8, one launch (start us, length us, event | category | flops | bytes accessed | tf_op | source)
XLA Modules:
  0.0 126.3 jit_solution(5378480323934576204)
XLA Ops:
  0.6 0.0 copy-start.2
  0.7 2.3 %pick_places.1 = bf16[32,8,128]{2,1,0:T(8,128)(2,1)} custom-call(s32[2,32]{1,0:T(2,128)} %bitcast.10, bf16[3,32,128]{2,1,0:T(8,128)(2,1)} %bitcast.13), custom_call_target="tpu_custom_call" | custom-call | bytes 1024 | tf_op jit(solution)/shard_map/pick_places/pallas_call | solution.py:42
  2.9 11.7 %all-to-all-start = ((bf16[32,8,128]{2,1,0:T(8,128)(2,1)}), bf16[32,8,128]{2,1,0:T(8,128)(2,1)S(1)}, u32[]{:S(2)}, u32[]{:S(2)}) async-start(bf16[32,8,128]{2,1,0:T(8,128)(2,1)} %pick_places.1), calls=%async_computation | async-start | bytes 131072 | tf_op jit(solution)/shard_map/all_to_all | solution.py:389
  14.8 0.0 copy-start
  14.8 0.8 copy-done
  15.6 1.0 features.1
  16.6 2.9 %pick_moments.1 = bf16[32,2,64,128]{3,2,1,0:T(8,128)(2,1)} custom-call(s32[2,32]{1,0:T(2,128)} %bitcast.11, s32[32]{0:T(128)} %count_ref.3, bf16[32,64,128]{2,1,0:T(8,128)(2,1)} %m_ref.1), custom_call_target="tpu_custom_call" | custom-call | bytes 1024 | tf_op jit(solution)/shard_map/pick_moments/pallas_call | solution.py:42
  19.5 2.0 %constant_dynamic-slice_fusion = (bf16[8,64,128]{2,1,0:T(8,128)(2,1)S(1)}, bf16[8,64,128]{2,1,0:T(8,128)(2,1)S(1)}, bf16[8,64,128]{2,1,0:T(8,128)(2,1)}, bf16[8,...) fusion(bf16[64,64,128]{2,1,0:T(8,128)(2,1)} %param.15, ...), kind=kLoop, calls=%fused_computation.8 | loop fusion | bytes 2097184 | tf_op jit(solution)/shard_map/dynamic_slice | solution.py:394
  21.5 1.8 %all-to-all-done.pos_ref = bf16[32,8,128]{2,1,0:T(8,128)(2,1)S(1)} async-done(((bf16[32,8,128]{2,1,0:T(8,128)(2,1)}), bf16[32,8,128]{2,1,0:T(8,128)(2,1)S(1)}, u32[]{:S(2)}, u32[]{:S(2)}) %all-to-all-start) | async-done | bytes 65568 | tf_op jit(solution)/shard_map/all_to_all | solution.py:389
  23.3 8.0 %all-to-all-start.1 = ((bf16[32,2,64,128]{3,2,1,0:T(8,128)(2,1)}), bf16[32,2,64,128]{3,2,1,0:T(8,128)(2,1)}, u32[]{:S(2)}, u32[]{:S(2)}) async-start(bf16[32,2,64,128]{3,2,1,0:T(8,128)(2,1)} %pick_moments.1), calls=%async_computation.1 | async-start | bytes 2097152 | tf_op jit(solution)/shard_map/all_to_all | solution.py:400
  31.4 0.0 collective-permute-start
  31.4 1.6 %collective-permute-start.1 = (bf16[8,64,128]{2,1,0:T(8,128)(2,1)S(1)}, bf16[8,64,128]{2,1,0:T(8,128)(2,1)S(1)}, u32[]{:S(2)}, u32[]{:S(2)}) collective-permute-start(bf16[8,64,128]{2,1,0:T(8,128)(2,1)S(1)} %get-tuple-element.44), channel_id=1, source_target_pairs={{0,2},{1,3},{2,4},{3,5},{4,6},{5,7},{6,0},{7,1},{8,10},{9,11},{10,... | collective-permute-start | bytes 393224 | tf_op jit(solution)/shard_map/ppermute | solution.py:330
  32.9 2.0 %collective-permute-start.2 = (bf16[8,64,128]{2,1,0:T(8,128)(2,1)}, bf16[8,64,128]{2,1,0:T(8,128)(2,1)S(1)}, u32[]{:S(2)}, u32[]{:S(2)}) collective-permute-start(bf16[8,64,128]{2,1,0:T(8,128)(2,1)} %get-tuple-element.45), channel_id=1, source_target_pairs={{0,3},{1,4},{2,5},{3,6},{4,7},{5,0},{6,1},{7,2},{8,11},{9,12},{10,... | collective-permute-start | bytes 393224 | tf_op jit(solution)/shard_map/ppermute | solution.py:330
  35.0 2.0 %collective-permute-start.3 = (bf16[8,64,128]{2,1,0:T(8,128)(2,1)}, bf16[8,64,128]{2,1,0:T(8,128)(2,1)S(1)}, u32[]{:S(2)}, u32[]{:S(2)}) collective-permute-start(bf16[8,64,128]{2,1,0:T(8,128)(2,1)} %get-tuple-element.46), channel_id=1, source_target_pairs={{0,4},{1,5},{2,6},{3,7},{4,0},{5,1},{6,2},{7,3},{8,12},{9,13},{10,... | collective-permute-start | bytes 393224 | tf_op jit(solution)/shard_map/ppermute | solution.py:330
  37.0 1.7 %collective-permute-start.4 = (bf16[8,64,128]{2,1,0:T(8,128)(2,1)}, bf16[8,64,128]{2,1,0:T(8,128)(2,1)S(1)}, u32[]{:S(2)}, u32[]{:S(2)}) collective-permute-start(bf16[8,64,128]{2,1,0:T(8,128)(2,1)} %get-tuple-element.47), channel_id=1, source_target_pairs={{0,5},{1,6},{2,7},{3,0},{4,1},{5,2},{6,3},{7,4},{8,13},{9,14},{10,... | collective-permute-start | bytes 393224 | tf_op jit(solution)/shard_map/ppermute | solution.py:330
  38.6 0.0 collective-permute-done.refs_1_
  38.7 1.4 %collective-permute-start.5 = (bf16[8,64,128]{2,1,0:T(8,128)(2,1)S(1)}, bf16[8,64,128]{2,1,0:T(8,128)(2,1)S(1)}, u32[]{:S(2)}, u32[]{:S(2)}) collective-permute-start(bf16[8,64,128]{2,1,0:T(8,128)(2,1)S(1)} %get-tuple-element.48), channel_id=1, source_target_pairs={{0,6},{1,7},{2,0},{3,1},{4,2},{5,3},{6,4},{7,5},{8,14},{9,15},{10,... | collective-permute-start | bytes 393224 | tf_op jit(solution)/shard_map/ppermute | solution.py:330
  40.1 0.0 collective-permute-done.1.refs_2_
  40.1 1.8 %collective-permute-start.6 = (bf16[8,64,128]{2,1,0:T(8,128)(2,1)S(1)}, bf16[8,64,128]{2,1,0:T(8,128)(2,1)S(1)}, u32[]{:S(2)}, u32[]{:S(2)}) collective-permute-start(bf16[8,64,128]{2,1,0:T(8,128)(2,1)S(1)} %get-tuple-element.49), channel_id=1, source_target_pairs={{0,7},{1,0},{2,1},{3,2},{4,3},{5,4},{6,5},{7,6},{8,15},{9,8},{10,9... | collective-permute-start | bytes 393224 | tf_op jit(solution)/shard_map/ppermute | solution.py:330
  41.9 0.7 copy-done.1
  42.6 22.2 %kernel_values.1.kern_ref = bf16[64,128,2048]{2,1,0:T(8,128)(2,1)} custom-call(s32[16,64]{1,0:T(8,128)S(1)} %bitcast.8, bf16[32,8,128]{2,1,0:T(8,128)(2,1)S(1)} %all-to-all-done.pos_ref, f32[8,128]{1,0:T(8,128)S(1)} %get-tuple-element.30.far_ref, bf16[64,128,16]{2,1,0:T(8,128)(2,1)S(1)} %get-tuple-element.40.feat_ref), custom_call_target="tpu_custom_call" | custom-call | flops 251658240 | bytes 33554432 | tf_op jit(solution)/shard_map/kernel_values/pallas_call | solution.py:213
  64.9 0.0 collective-permute-done.2.refs_3_
  64.9 0.0 collective-permute-done.3.refs_4_
  64.9 0.0 collective-permute-done.4.refs_5_
  64.9 0.0 collective-permute-done.5.refs_6_
  64.9 0.0 collective-permute-done.6.refs_7_
  64.9 0.0 all-to-all-done.1
  64.9 22.6 %forward_adjoint.1 = (bf16[64,64,128]{2,1,0:T(8,128)(2,1)S(1)}, bf16[64,64,128]{2,1,0:T(8,128)(2,1)}) custom-call(s32[16,64]{1,0:T(8,128)S(1)} %bitcast.9, s32[64]{0:T(128)S(1)} %copy-done.5, s32[1]{0:T(128)} %bitcast.1.me_ref, bf16[64,128,2048]{2,1,0:T(8,128)(2,1)} %kernel_values.1.kern_ref, bf16[64,64,128]{2,1,0:T(8,128)(2,1)} %bitcast.5.m_ref, ...), custom_call_target="tpu_custom_call" | custom-call | flops 4294967296 | bytes 33554432 | tf_op jit(solution)/shard_map/forward_adjoint/pallas_call | solution.py:301
  87.5 9.7 %all-to-all-start.2 = ((bf16[32,2,64,128]{3,2,1,0:T(8,128)(2,1)}), bf16[32,2,64,128]{3,2,1,0:T(8,128)(2,1)S(1)}, u32[]{:S(2)}, u32[]{:S(2)}) async-start(bf16[32,2,64,128]{3,2,1,0:T(8,128)(2,1)} %bitcast.6), calls=%async_computation.2 | async-start | bytes 2097152 | tf_op jit(solution)/shard_map/all_to_all | solution.py:403
  97.3 0.2 broadcast_in_dim.3
  97.5 0.8 fusion
  98.4 0.0 collective-permute-start.7
  98.4 0.5 collective-permute-start.8
  98.8 1.2 collective-permute-start.9
  100.1 2.9 %collective-permute-start.10 = (bf16[8,64,128]{2,1,0:T(8,128)(2,1)}, bf16[8,64,128]{2,1,0:T(8,128)(2,1)S(1)}, u32[]{:S(2)}, u32[]{:S(2)}) collective-permute-start(bf16[8,64,128]{2,1,0:T(8,128)(2,1)} %get-tuple-element.55), channel_id=1, source_target_pairs={{0,4},{1,5},{2,6},{3,7},{4,0},{5,1},{6,2},{7,3},{8,12},{9,13},{10,... | collective-permute-start | bytes 393224 | tf_op jit(solution)/shard_map/ppermute | solution.py:330
  103.0 0.7 collective-permute-start.11
  103.7 1.3 %collective-permute-done.7 = bf16[8,64,128]{2,1,0:T(8,128)(2,1)S(1)} collective-permute-done((bf16[8,64,128]{2,1,0:T(8,128)(2,1)}, bf16[8,64,128]{2,1,0:T(8,128)(2,1)S(1)}, u32[]{:S(2)}, u32[]{:S(2)}) %collective-permute-start.7) | collective-permute-done | bytes 131104 | tf_op jit(solution)/shard_map/ppermute | solution.py:330
  105.0 0.1 collective-permute-start.12
  105.2 0.9 collective-permute-done.8
  106.1 1.5 %collective-permute-start.13 = (bf16[8,64,128]{2,1,0:T(8,128)(2,1)S(1)}, bf16[8,64,128]{2,1,0:T(8,128)(2,1)S(1)}, u32[]{:S(2)}, u32[]{:S(2)}) collective-permute-start(bf16[8,64,128]{2,1,0:T(8,128)(2,1)S(1)} %get-tuple-element.52), channel_id=1, source_target_pairs={{0,7},{1,0},{2,1},{3,2},{4,3},{5,4},{6,5},{7,6},{8,15},{9,8},{10,9... | collective-permute-start | bytes 393224 | tf_op jit(solution)/shard_map/ppermute | solution.py:330
  107.6 2.2 %collective-permute-done.9 = bf16[8,64,128]{2,1,0:T(8,128)(2,1)S(1)} collective-permute-done((bf16[8,64,128]{2,1,0:T(8,128)(2,1)}, bf16[8,64,128]{2,1,0:T(8,128)(2,1)S(1)}, u32[]{:S(2)}, u32[]{:S(2)}) %collective-permute-start.9) | collective-permute-done | bytes 131104 | tf_op jit(solution)/shard_map/ppermute | solution.py:330
  109.9 1.1 collective-permute-done.10
  111.0 0.3 collective-permute-done.11
  111.3 1.6 %collective-permute-done.12 = bf16[8,64,128]{2,1,0:T(8,128)(2,1)S(1)} collective-permute-done((bf16[8,64,128]{2,1,0:T(8,128)(2,1)S(1)}, bf16[8,64,128]{2,1,0:T(8,128)(2,1)S(1)}, u32[]{:S(2)}, u32[]{:S(2)}) %collective-permute-start.12) | collective-permute-done | bytes 131104 | tf_op jit(solution)/shard_map/ppermute | solution.py:330
  112.9 1.5 %collective-permute-done.13 = bf16[8,64,128]{2,1,0:T(8,128)(2,1)S(1)} collective-permute-done((bf16[8,64,128]{2,1,0:T(8,128)(2,1)S(1)}, bf16[8,64,128]{2,1,0:T(8,128)(2,1)S(1)}, u32[]{:S(2)}, u32[]{:S(2)}) %collective-permute-start.13) | collective-permute-done | bytes 131104 | tf_op jit(solution)/shard_map/ppermute | solution.py:330
  114.4 0.0 copy-start.6
  114.4 9.9 %all-to-all-done.2.back_ref = bf16[32,2,64,128]{3,2,1,0:T(8,128)(2,1)S(1)} async-done(((bf16[32,2,64,128]{3,2,1,0:T(8,128)(2,1)}), bf16[32,2,64,128]{3,2,1,0:T(8,128)(2,1)S(1)}, u32[]{:S(2)}, u32[]{:S(2)}) %all-to-all-start.2) | async-done | bytes 1048608 | tf_op jit(solution)/shard_map/all_to_all | solution.py:403
  124.3 2.0 %combine.1 = f32[32,64,128]{2,1,0:T(8,128)} custom-call(s32[2,32]{1,0:T(2,128)S(1)} %bitcast.12, s32[32]{0:T(128)S(1)} %copy-done.4, bf16[32,2,64,128]{3,2,1,0:T(8,128)(2,1)S(1)} %all-to-all-done.2.back_ref), custom_call_target="tpu_custom_call" | custom-call | tf_op jit(solution)/shard_map/combine/pallas_call | solution.py:347
  (16 shorter events, 0.1 us)
Async XLA Ops:
  0.6 64.3 %copy-start.2 = (s32[64,16]{0,1:T(8,128)S(1)}, s32[64,16]{0,1:T(8,128)}, u32[]{:S(2)}) copy-start(s32[64,16]{0,1:T(8,128)} %param.13) | copy-start | bytes 12292
  0.6 64.3 %copy-start.5 = (s32[64]{0:T(128)S(1)}, s32[64]{0:T(128)}, u32[]{:S(2)}) copy-start(s32[64]{0:T(128)} %slot_ref.1) | copy-start | bytes 772
  2.9 20.4 %all-to-all-start = ((bf16[32,8,128]{2,1,0:T(8,128)(2,1)}), bf16[32,8,128]{2,1,0:T(8,128)(2,1)S(1)}, u32[]{:S(2)}, u32[]{:S(2)}) async-start(bf16[32,8,128]{2,1,0:T(8,128)(2,1)} %pick_places.1), calls=%async_computation | async-start | bytes 131072 | tf_op jit(solution)/shard_map/all_to_all | solution.py:389
  14.8 0.8 copy-start
  23.3 41.6 %all-to-all-start.1 = ((bf16[32,2,64,128]{3,2,1,0:T(8,128)(2,1)}), bf16[32,2,64,128]{3,2,1,0:T(8,128)(2,1)}, u32[]{:S(2)}, u32[]{:S(2)}) async-start(bf16[32,2,64,128]{3,2,1,0:T(8,128)(2,1)} %pick_moments.1), calls=%async_computation.1 | async-start | bytes 2097152 | tf_op jit(solution)/shard_map/all_to_all | solution.py:400
  31.4 7.3 %collective-permute-start = (bf16[8,64,128]{2,1,0:T(8,128)(2,1)S(1)}, bf16[8,64,128]{2,1,0:T(8,128)(2,1)S(1)}, u32[]{:S(2)}, u32[]{:S(2)}) collective-permute-start(bf16[8,64,128]{2,1,0:T(8,128)(2,1)S(1)} %get-tuple-element.43), channel_id=1, source_target_pairs={{0,1},{1,2},{2,3},{3,4},{4,5},{5,6},{6,7},{7,0},{8,9},{9,10},{10,1... | collective-permute-start | bytes 393224 | tf_op jit(solution)/shard_map/ppermute | solution.py:330
  31.4 8.7 %collective-permute-start.1 = (bf16[8,64,128]{2,1,0:T(8,128)(2,1)S(1)}, bf16[8,64,128]{2,1,0:T(8,128)(2,1)S(1)}, u32[]{:S(2)}, u32[]{:S(2)}) collective-permute-start(bf16[8,64,128]{2,1,0:T(8,128)(2,1)S(1)} %get-tuple-element.44), channel_id=1, source_target_pairs={{0,2},{1,3},{2,4},{3,5},{4,6},{5,7},{6,0},{7,1},{8,10},{9,11},{10,... | collective-permute-start | bytes 393224 | tf_op jit(solution)/shard_map/ppermute | solution.py:330
  32.9 31.9 %collective-permute-start.2 = (bf16[8,64,128]{2,1,0:T(8,128)(2,1)}, bf16[8,64,128]{2,1,0:T(8,128)(2,1)S(1)}, u32[]{:S(2)}, u32[]{:S(2)}) collective-permute-start(bf16[8,64,128]{2,1,0:T(8,128)(2,1)} %get-tuple-element.45), channel_id=1, source_target_pairs={{0,3},{1,4},{2,5},{3,6},{4,7},{5,0},{6,1},{7,2},{8,11},{9,12},{10,... | collective-permute-start | bytes 393224 | tf_op jit(solution)/shard_map/ppermute | solution.py:330
  35.0 29.9 %collective-permute-start.3 = (bf16[8,64,128]{2,1,0:T(8,128)(2,1)}, bf16[8,64,128]{2,1,0:T(8,128)(2,1)S(1)}, u32[]{:S(2)}, u32[]{:S(2)}) collective-permute-start(bf16[8,64,128]{2,1,0:T(8,128)(2,1)} %get-tuple-element.46), channel_id=1, source_target_pairs={{0,4},{1,5},{2,6},{3,7},{4,0},{5,1},{6,2},{7,3},{8,12},{9,13},{10,... | collective-permute-start | bytes 393224 | tf_op jit(solution)/shard_map/ppermute | solution.py:330
  37.0 27.9 %collective-permute-start.4 = (bf16[8,64,128]{2,1,0:T(8,128)(2,1)}, bf16[8,64,128]{2,1,0:T(8,128)(2,1)S(1)}, u32[]{:S(2)}, u32[]{:S(2)}) collective-permute-start(bf16[8,64,128]{2,1,0:T(8,128)(2,1)} %get-tuple-element.47), channel_id=1, source_target_pairs={{0,5},{1,6},{2,7},{3,0},{4,1},{5,2},{6,3},{7,4},{8,13},{9,14},{10,... | collective-permute-start | bytes 393224 | tf_op jit(solution)/shard_map/ppermute | solution.py:330
  38.7 26.2 %collective-permute-start.5 = (bf16[8,64,128]{2,1,0:T(8,128)(2,1)S(1)}, bf16[8,64,128]{2,1,0:T(8,128)(2,1)S(1)}, u32[]{:S(2)}, u32[]{:S(2)}) collective-permute-start(bf16[8,64,128]{2,1,0:T(8,128)(2,1)S(1)} %get-tuple-element.48), channel_id=1, source_target_pairs={{0,6},{1,7},{2,0},{3,1},{4,2},{5,3},{6,4},{7,5},{8,14},{9,15},{10,... | collective-permute-start | bytes 393224 | tf_op jit(solution)/shard_map/ppermute | solution.py:330
  40.1 24.8 %collective-permute-start.6 = (bf16[8,64,128]{2,1,0:T(8,128)(2,1)S(1)}, bf16[8,64,128]{2,1,0:T(8,128)(2,1)S(1)}, u32[]{:S(2)}, u32[]{:S(2)}) collective-permute-start(bf16[8,64,128]{2,1,0:T(8,128)(2,1)S(1)} %get-tuple-element.49), channel_id=1, source_target_pairs={{0,7},{1,0},{2,1},{3,2},{4,3},{5,4},{6,5},{7,6},{8,15},{9,8},{10,9... | collective-permute-start | bytes 393224 | tf_op jit(solution)/shard_map/ppermute | solution.py:330
  41.9 0.7 copy-start.1
  42.6 81.7 %copy-start.3 = (s32[32,2]{0,1:T(2,128)S(1)}, s32[32,2]{0,1:T(2,128)}, u32[]{:S(2)}) copy-start(s32[32,2]{0,1:T(2,128)} %param.10) | copy-start | bytes 772
  42.6 81.7 %copy-start.4 = (s32[32]{0:T(128)S(1)}, s32[32]{0:T(128)}, u32[]{:S(2)}) copy-start(s32[32]{0:T(128)} %count_ref.3) | copy-start | bytes 388
  87.5 36.8 %all-to-all-start.2 = ((bf16[32,2,64,128]{3,2,1,0:T(8,128)(2,1)}), bf16[32,2,64,128]{3,2,1,0:T(8,128)(2,1)S(1)}, u32[]{:S(2)}, u32[]{:S(2)}) async-start(bf16[32,2,64,128]{3,2,1,0:T(8,128)(2,1)} %bitcast.6), calls=%async_computation.2 | async-start | bytes 2097152 | tf_op jit(solution)/shard_map/all_to_all | solution.py:403
  98.4 6.7 %collective-permute-start.7 = (bf16[8,64,128]{2,1,0:T(8,128)(2,1)}, bf16[8,64,128]{2,1,0:T(8,128)(2,1)S(1)}, u32[]{:S(2)}, u32[]{:S(2)}) collective-permute-start(bf16[8,64,128]{2,1,0:T(8,128)(2,1)} %get-tuple-element.58), channel_id=1, source_target_pairs={{0,1},{1,2},{2,3},{3,4},{4,5},{5,6},{6,7},{7,0},{8,9},{9,10},{10,1... | collective-permute-start | bytes 393224 | tf_op jit(solution)/shard_map/ppermute | solution.py:330
  98.4 7.8 %collective-permute-start.8 = (bf16[8,64,128]{2,1,0:T(8,128)(2,1)}, bf16[8,64,128]{2,1,0:T(8,128)(2,1)S(1)}, u32[]{:S(2)}, u32[]{:S(2)}) collective-permute-start(bf16[8,64,128]{2,1,0:T(8,128)(2,1)} %get-tuple-element.57), channel_id=1, source_target_pairs={{0,2},{1,3},{2,4},{3,5},{4,6},{5,7},{6,0},{7,1},{8,10},{9,11},{10,... | collective-permute-start | bytes 393224 | tf_op jit(solution)/shard_map/ppermute | solution.py:330
  98.8 11.0 %collective-permute-start.9 = (bf16[8,64,128]{2,1,0:T(8,128)(2,1)}, bf16[8,64,128]{2,1,0:T(8,128)(2,1)S(1)}, u32[]{:S(2)}, u32[]{:S(2)}) collective-permute-start(bf16[8,64,128]{2,1,0:T(8,128)(2,1)} %get-tuple-element.56), channel_id=1, source_target_pairs={{0,3},{1,4},{2,5},{3,6},{4,7},{5,0},{6,1},{7,2},{8,11},{9,12},{10,... | collective-permute-start | bytes 393224 | tf_op jit(solution)/shard_map/ppermute | solution.py:330
  100.1 10.8 %collective-permute-start.10 = (bf16[8,64,128]{2,1,0:T(8,128)(2,1)}, bf16[8,64,128]{2,1,0:T(8,128)(2,1)S(1)}, u32[]{:S(2)}, u32[]{:S(2)}) collective-permute-start(bf16[8,64,128]{2,1,0:T(8,128)(2,1)} %get-tuple-element.55), channel_id=1, source_target_pairs={{0,4},{1,5},{2,6},{3,7},{4,0},{5,1},{6,2},{7,3},{8,12},{9,13},{10,... | collective-permute-start | bytes 393224 | tf_op jit(solution)/shard_map/ppermute | solution.py:330
  103.0 8.3 %collective-permute-start.11 = (bf16[8,64,128]{2,1,0:T(8,128)(2,1)}, bf16[8,64,128]{2,1,0:T(8,128)(2,1)S(1)}, u32[]{:S(2)}, u32[]{:S(2)}) collective-permute-start(bf16[8,64,128]{2,1,0:T(8,128)(2,1)} %get-tuple-element.54), channel_id=1, source_target_pairs={{0,5},{1,6},{2,7},{3,0},{4,1},{5,2},{6,3},{7,4},{8,13},{9,14},{10,... | collective-permute-start | bytes 393224 | tf_op jit(solution)/shard_map/ppermute | solution.py:330
  105.0 7.9 %collective-permute-start.12 = (bf16[8,64,128]{2,1,0:T(8,128)(2,1)S(1)}, bf16[8,64,128]{2,1,0:T(8,128)(2,1)S(1)}, u32[]{:S(2)}, u32[]{:S(2)}) collective-permute-start(bf16[8,64,128]{2,1,0:T(8,128)(2,1)S(1)} %get-tuple-element.53), channel_id=1, source_target_pairs={{0,6},{1,7},{2,0},{3,1},{4,2},{5,3},{6,4},{7,5},{8,14},{9,15},{10,... | collective-permute-start | bytes 393224 | tf_op jit(solution)/shard_map/ppermute | solution.py:330
  106.1 8.3 %collective-permute-start.13 = (bf16[8,64,128]{2,1,0:T(8,128)(2,1)S(1)}, bf16[8,64,128]{2,1,0:T(8,128)(2,1)S(1)}, u32[]{:S(2)}, u32[]{:S(2)}) collective-permute-start(bf16[8,64,128]{2,1,0:T(8,128)(2,1)S(1)} %get-tuple-element.52), channel_id=1, source_target_pairs={{0,7},{1,0},{2,1},{3,2},{4,3},{5,4},{6,5},{7,6},{8,15},{9,8},{10,9... | collective-permute-start | bytes 393224 | tf_op jit(solution)/shard_map/ppermute | solution.py:330
  114.4 11.9 %copy-start.6 = (bf16[64,64,128]{2,1,0:T(8,128)(2,1)}, bf16[64,64,128]{2,1,0:T(8,128)(2,1)S(1)}, u32[]{:S(2)}) copy-start(bf16[64,64,128]{2,1,0:T(8,128)(2,1)S(1)} %constant_dynamic-update-slice_fusion) | copy-start | bytes 3145732

commit v5 on v4

--- a/solution.py
+++ b/solution.py
@@ -12,6 +12,7 @@
 GEN = 8
 USE = 8
 LAG = 3
+CUT = 32
 ROWS = 16
 VMEM = 50 * 2**20
 
@@ -348,9 +349,9 @@
         add_back,
         grid_spec=pltpu.PrefetchScalarGridSpec(
             num_scalar_prefetch=2,
-            grid=(1,),
-            in_specs=[pl.BlockSpec(back.shape, lambda g, *_: (0, 0, 0, 0))],
-            out_specs=pl.BlockSpec((old, width, depth), lambda g, *_: (0, 0, 0)),
+            grid=(width // CUT,),
+            in_specs=[pl.BlockSpec((*back.shape[:2], CUT, depth), lambda g, *_: (0, 0, g, 0))],
+            out_specs=pl.BlockSpec((old, CUT, depth), lambda g, *_: (0, g, 0)),
         ),
         out_shape=jax.ShapeDtypeStruct((old, width, depth), jnp.float32),
         compiler_params=pltpu.CompilerParams(vmem_limit_bytes=VMEM),

time: 127 us -> 127 us (level)
  no operation moved by 1% of the time
where the time goes in v5:
time: 127 us
  Pallas kernels  53.2 us (42%)
  starting transfers between devices  47 us (37%)
  waiting for transfers between devices  20.7 us (16%)
  local copies, waits for them, and re-layouts  4.76 us (4%)
    pallas_call x1, Pallas kernels, forward_adjoint(): pl.pallas_call(apply_both, grid_spec=pltpu.PrefetchScalarGridSpec(num_sca...  22.6 us
    pallas_call x1, Pallas kernels, kernel_values(): pl.pallas_call(make_kernels, grid_spec=pltpu.PrefetchScalarGridSpec(num_s...  22.2 us
    ppermute x14, starting transfers between devices, shift(): lax.ppermute(block, axis, [(i, (i + by) % size) for i in range(size)])  17.5 us
    all_to_all x1, starting transfers between devices, on_device(): slot_p = swap(send_p, 'morton')  11.7 us
    all_to_all x1, waiting for transfers between devices, on_device(): back = swap(slot_adj.reshape(peers, cap, width, depth), 'morton')  9.89 us
    all_to_all x1, starting transfers between devices, on_device(): back = swap(slot_adj.reshape(peers, cap, width, depth), 'morton')  9.77 us
    ppermute x14, waiting for transfers between devices, shift(): lax.ppermute(block, axis, [(i, (i + by) % size) for i in range(size)])  8.97 us
    all_to_all x1, starting transfers between devices, on_device(): slot_m = swap(send_m, 'morton').reshape(peers * cap, width, depth)  8.01 us
  transfers between devices with their start and end apart: 17, of which 9 were waited for; matrix products, arithmetic and copies ran while one was open for 3% of the time, Pallas kernels for 21%

profile of v5, /device:TPU:8, one launch (start us, length us, event | category | flops | bytes accessed | tf_op | source)
XLA Modules:
  0.0 126.6 jit_solution(17237701340856239909)
XLA Ops:
  0.6 0.0 copy-start.2
  0.7 2.3 %pick_places.1 = bf16[32,8,128]{2,1,0:T(8,128)(2,1)} custom-call(s32[2,32]{1,0:T(2,128)} %bitcast.10, bf16[3,32,128]{2,1,0:T(8,128)(2,1)} %bitcast.13), custom_call_target="tpu_custom_call" | custom-call | bytes 1024 | tf_op jit(solution)/shard_map/pick_places/pallas_call | solution.py:43
  2.9 11.7 %all-to-all-start = ((bf16[32,8,128]{2,1,0:T(8,128)(2,1)}), bf16[32,8,128]{2,1,0:T(8,128)(2,1)S(1)}, u32[]{:S(2)}, u32[]{:S(2)}) async-start(bf16[32,8,128]{2,1,0:T(8,128)(2,1)} %pick_places.1), calls=%async_computation | async-start | bytes 131072 | tf_op jit(solution)/shard_map/all_to_all | solution.py:390
  14.8 0.0 copy-start
  14.8 0.8 copy-done
  15.6 1.0 features.1
  16.6 2.9 %pick_moments.1 = bf16[32,2,64,128]{3,2,1,0:T(8,128)(2,1)} custom-call(s32[2,32]{1,0:T(2,128)} %bitcast.11, s32[32]{0:T(128)} %count_ref.3, bf16[32,64,128]{2,1,0:T(8,128)(2,1)} %m_ref.1), custom_call_target="tpu_custom_call" | custom-call | bytes 1024 | tf_op jit(solution)/shard_map/pick_moments/pallas_call | solution.py:43
  19.5 2.0 %constant_dynamic-slice_fusion = (bf16[8,64,128]{2,1,0:T(8,128)(2,1)S(1)}, bf16[8,64,128]{2,1,0:T(8,128)(2,1)S(1)}, bf16[8,64,128]{2,1,0:T(8,128)(2,1)}, bf16[8,...) fusion(bf16[64,64,128]{2,1,0:T(8,128)(2,1)} %param.15, ...), kind=kLoop, calls=%fused_computation.8 | loop fusion | bytes 2097184 | tf_op jit(solution)/shard_map/dynamic_slice | solution.py:395
  21.5 1.8 %all-to-all-done.pos_ref = bf16[32,8,128]{2,1,0:T(8,128)(2,1)S(1)} async-done(((bf16[32,8,128]{2,1,0:T(8,128)(2,1)}), bf16[32,8,128]{2,1,0:T(8,128)(2,1)S(1)}, u32[]{:S(2)}, u32[]{:S(2)}) %all-to-all-start) | async-done | bytes 65568 | tf_op jit(solution)/shard_map/all_to_all | solution.py:390
  23.3 8.0 %all-to-all-start.1 = ((bf16[32,2,64,128]{3,2,1,0:T(8,128)(2,1)}), bf16[32,2,64,128]{3,2,1,0:T(8,128)(2,1)}, u32[]{:S(2)}, u32[]{:S(2)}) async-start(bf16[32,2,64,128]{3,2,1,0:T(8,128)(2,1)} %pick_moments.1), calls=%async_computation.1 | async-start | bytes 2097152 | tf_op jit(solution)/shard_map/all_to_all | solution.py:401
  31.4 0.0 collective-permute-start
  31.4 1.6 %collective-permute-start.1 = (bf16[8,64,128]{2,1,0:T(8,128)(2,1)S(1)}, bf16[8,64,128]{2,1,0:T(8,128)(2,1)S(1)}, u32[]{:S(2)}, u32[]{:S(2)}) collective-permute-start(bf16[8,64,128]{2,1,0:T(8,128)(2,1)S(1)} %get-tuple-element.44), channel_id=1, source_target_pairs={{0,2},{1,3},{2,4},{3,5},{4,6},{5,7},{6,0},{7,1},{8,10},{9,11},{10,... | collective-permute-start | bytes 393224 | tf_op jit(solution)/shard_map/ppermute | solution.py:331
  32.9 2.0 %collective-permute-start.2 = (bf16[8,64,128]{2,1,0:T(8,128)(2,1)}, bf16[8,64,128]{2,1,0:T(8,128)(2,1)S(1)}, u32[]{:S(2)}, u32[]{:S(2)}) collective-permute-start(bf16[8,64,128]{2,1,0:T(8,128)(2,1)} %get-tuple-element.45), channel_id=1, source_target_pairs={{0,3},{1,4},{2,5},{3,6},{4,7},{5,0},{6,1},{7,2},{8,11},{9,12},{10,... | collective-permute-start | bytes 393224 | tf_op jit(solution)/shard_map/ppermute | solution.py:331
  35.0 2.0 %collective-permute-start.3 = (bf16[8,64,128]{2,1,0:T(8,128)(2,1)}, bf16[8,64,128]{2,1,0:T(8,128)(2,1)S(1)}, u32[]{:S(2)}, u32[]{:S(2)}) collective-permute-start(bf16[8,64,128]{2,1,0:T(8,128)(2,1)} %get-tuple-element.46), channel_id=1, source_target_pairs={{0,4},{1,5},{2,6},{3,7},{4,0},{5,1},{6,2},{7,3},{8,12},{9,13},{10,... | collective-permute-start | bytes 393224 | tf_op jit(solution)/shard_map/ppermute | solution.py:331
  37.0 1.7 %collective-permute-start.4 = (bf16[8,64,128]{2,1,0:T(8,128)(2,1)}, bf16[8,64,128]{2,1,0:T(8,128)(2,1)S(1)}, u32[]{:S(2)}, u32[]{:S(2)}) collective-permute-start(bf16[8,64,128]{2,1,0:T(8,128)(2,1)} %get-tuple-element.47), channel_id=1, source_target_pairs={{0,5},{1,6},{2,7},{3,0},{4,1},{5,2},{6,3},{7,4},{8,13},{9,14},{10,... | collective-permute-start | bytes 393224 | tf_op jit(solution)/shard_map/ppermute | solution.py:331
  38.6 0.0 collective-permute-done.refs_1_
  38.7 1.4 %collective-permute-start.5 = (bf16[8,64,128]{2,1,0:T(8,128)(2,1)S(1)}, bf16[8,64,128]{2,1,0:T(8,128)(2,1)S(1)}, u32[]{:S(2)}, u32[]{:S(2)}) collective-permute-start(bf16[8,64,128]{2,1,0:T(8,128)(2,1)S(1)} %get-tuple-element.48), channel_id=1, source_target_pairs={{0,6},{1,7},{2,0},{3,1},{4,2},{5,3},{6,4},{7,5},{8,14},{9,15},{10,... | collective-permute-start | bytes 393224 | tf_op jit(solution)/shard_map/ppermute | solution.py:331
  40.1 0.0 collective-permute-done.1.refs_2_
  40.1 1.8 %collective-permute-start.6 = (bf16[8,64,128]{2,1,0:T(8,128)(2,1)S(1)}, bf16[8,64,128]{2,1,0:T(8,128)(2,1)S(1)}, u32[]{:S(2)}, u32[]{:S(2)}) collective-permute-start(bf16[8,64,128]{2,1,0:T(8,128)(2,1)S(1)} %get-tuple-element.49), channel_id=1, source_target_pairs={{0,7},{1,0},{2,1},{3,2},{4,3},{5,4},{6,5},{7,6},{8,15},{9,8},{10,9... | collective-permute-start | bytes 393224 | tf_op jit(solution)/shard_map/ppermute | solution.py:331
  41.9 0.7 copy-done.1
  42.6 22.2 %kernel_values.1.kern_ref = bf16[64,128,2048]{2,1,0:T(8,128)(2,1)} custom-call(s32[16,64]{1,0:T(8,128)S(1)} %bitcast.8, bf16[32,8,128]{2,1,0:T(8,128)(2,1)S(1)} %all-to-all-done.pos_ref, f32[8,128]{1,0:T(8,128)S(1)} %get-tuple-element.30.far_ref, bf16[64,128,16]{2,1,0:T(8,128)(2,1)S(1)} %get-tuple-element.40.feat_ref), custom_call_target="tpu_custom_call" | custom-call | flops 251658240 | bytes 33554432 | tf_op jit(solution)/shard_map/kernel_values/pallas_call | solution.py:214
  64.9 0.0 collective-permute-done.2.refs_3_
  64.9 0.0 collective-permute-done.3.refs_4_
  64.9 0.0 collective-permute-done.4.refs_5_
  64.9 0.0 collective-permute-done.5.refs_6_
  64.9 0.0 collective-permute-done.6.refs_7_
  64.9 0.0 all-to-all-done.1
  64.9 22.6 %forward_adjoint.1 = (bf16[64,64,128]{2,1,0:T(8,128)(2,1)S(1)}, bf16[64,64,128]{2,1,0:T(8,128)(2,1)}) custom-call(s32[16,64]{1,0:T(8,128)S(1)} %bitcast.9, s32[64]{0:T(128)S(1)} %copy-done.5, s32[1]{0:T(128)} %bitcast.1.me_ref, bf16[64,128,2048]{2,1,0:T(8,128)(2,1)} %kernel_values.1.kern_ref, bf16[64,64,128]{2,1,0:T(8,128)(2,1)} %bitcast.5.m_ref, ...), custom_call_target="tpu_custom_call" | custom-call | flops 4294967296 | bytes 33554432 | tf_op jit(solution)/shard_map/forward_adjoint/pallas_call | solution.py:302
  87.5 9.8 %all-to-all-start.2 = ((bf16[32,2,64,128]{3,2,1,0:T(8,128)(2,1)}), bf16[32,2,64,128]{3,2,1,0:T(8,128)(2,1)S(1)}, u32[]{:S(2)}, u32[]{:S(2)}) async-start(bf16[32,2,64,128]{3,2,1,0:T(8,128)(2,1)} %bitcast.6), calls=%async_computation.2 | async-start | bytes 2097152 | tf_op jit(solution)/shard_map/all_to_all | solution.py:404
  97.3 0.2 broadcast_in_dim.3
  97.5 0.8 fusion
  98.4 0.0 collective-permute-start.7
  98.4 0.5 collective-permute-start.8
  98.9 1.2 collective-permute-start.9
  100.1 2.9 %collective-permute-start.10 = (bf16[8,64,128]{2,1,0:T(8,128)(2,1)}, bf16[8,64,128]{2,1,0:T(8,128)(2,1)S(1)}, u32[]{:S(2)}, u32[]{:S(2)}) collective-permute-start(bf16[8,64,128]{2,1,0:T(8,128)(2,1)} %get-tuple-element.55), channel_id=1, source_target_pairs={{0,4},{1,5},{2,6},{3,7},{4,0},{5,1},{6,2},{7,3},{8,12},{9,13},{10,... | collective-permute-start | bytes 393224 | tf_op jit(solution)/shard_map/ppermute | solution.py:331
  103.0 0.7 collective-permute-start.11
  103.7 1.3 %collective-permute-done.7 = bf16[8,64,128]{2,1,0:T(8,128)(2,1)S(1)} collective-permute-done((bf16[8,64,128]{2,1,0:T(8,128)(2,1)}, bf16[8,64,128]{2,1,0:T(8,128)(2,1)S(1)}, u32[]{:S(2)}, u32[]{:S(2)}) %collective-permute-start.7) | collective-permute-done | bytes 131104 | tf_op jit(solution)/shard_map/ppermute | solution.py:331
  105.0 0.1 collective-permute-start.12
  105.2 0.9 collective-permute-done.8
  106.1 1.5 %collective-permute-start.13 = (bf16[8,64,128]{2,1,0:T(8,128)(2,1)S(1)}, bf16[8,64,128]{2,1,0:T(8,128)(2,1)S(1)}, u32[]{:S(2)}, u32[]{:S(2)}) collective-permute-start(bf16[8,64,128]{2,1,0:T(8,128)(2,1)S(1)} %get-tuple-element.52), channel_id=1, source_target_pairs={{0,7},{1,0},{2,1},{3,2},{4,3},{5,4},{6,5},{7,6},{8,15},{9,8},{10,9... | collective-permute-start | bytes 393224 | tf_op jit(solution)/shard_map/ppermute | solution.py:331
  107.6 2.2 %collective-permute-done.9 = bf16[8,64,128]{2,1,0:T(8,128)(2,1)S(1)} collective-permute-done((bf16[8,64,128]{2,1,0:T(8,128)(2,1)}, bf16[8,64,128]{2,1,0:T(8,128)(2,1)S(1)}, u32[]{:S(2)}, u32[]{:S(2)}) %collective-permute-start.9) | collective-permute-done | bytes 131104 | tf_op jit(solution)/shard_map/ppermute | solution.py:331
  109.8 1.1 collective-permute-done.10
  111.0 0.4 collective-permute-done.11
  111.4 1.5 %collective-permute-done.12 = bf16[8,64,128]{2,1,0:T(8,128)(2,1)S(1)} collective-permute-done((bf16[8,64,128]{2,1,0:T(8,128)(2,1)S(1)}, bf16[8,64,128]{2,1,0:T(8,128)(2,1)S(1)}, u32[]{:S(2)}, u32[]{:S(2)}) %collective-permute-start.12) | collective-permute-done | bytes 131104 | tf_op jit(solution)/shard_map/ppermute | solution.py:331
  112.9 1.5 %collective-permute-done.13 = bf16[8,64,128]{2,1,0:T(8,128)(2,1)S(1)} collective-permute-done((bf16[8,64,128]{2,1,0:T(8,128)(2,1)S(1)}, bf16[8,64,128]{2,1,0:T(8,128)(2,1)S(1)}, u32[]{:S(2)}, u32[]{:S(2)}) %collective-permute-start.13) | collective-permute-done | bytes 131104 | tf_op jit(solution)/shard_map/ppermute | solution.py:331
  114.4 0.0 copy-start.6
  114.4 9.9 %all-to-all-done.2.back_ref = bf16[32,2,64,128]{3,2,1,0:T(8,128)(2,1)S(1)} async-done(((bf16[32,2,64,128]{3,2,1,0:T(8,128)(2,1)}), bf16[32,2,64,128]{3,2,1,0:T(8,128)(2,1)S(1)}, u32[]{:S(2)}, u32[]{:S(2)}) %all-to-all-start.2) | async-done | bytes 1048608 | tf_op jit(solution)/shard_map/all_to_all | solution.py:404
  124.3 2.2 %combine.1 = f32[32,64,128]{2,1,0:T(8,128)} custom-call(s32[2,32]{1,0:T(2,128)S(1)} %bitcast.12, s32[32]{0:T(128)S(1)} %copy-done.4, bf16[32,2,64,128]{3,2,1,0:T(8,128)(2,1)S(1)} %all-to-all-done.2.back_ref), custom_call_target="tpu_custom_call" | custom-call | tf_op jit(solution)/shard_map/combine/pallas_call | solution.py:348
  (16 shorter events, 0.1 us)
Async XLA Ops:
  0.6 64.3 %copy-start.2 = (s32[64,16]{0,1:T(8,128)S(1)}, s32[64,16]{0,1:T(8,128)}, u32[]{:S(2)}) copy-start(s32[64,16]{0,1:T(8,128)} %param.13) | copy-start | bytes 12292
  0.6 64.3 %copy-start.5 = (s32[64]{0:T(128)S(1)}, s32[64]{0:T(128)}, u32[]{:S(2)}) copy-start(s32[64]{0:T(128)} %slot_ref.1) | copy-start | bytes 772
  2.9 20.4 %all-to-all-start = ((bf16[32,8,128]{2,1,0:T(8,128)(2,1)}), bf16[32,8,128]{2,1,0:T(8,128)(2,1)S(1)}, u32[]{:S(2)}, u32[]{:S(2)}) async-start(bf16[32,8,128]{2,1,0:T(8,128)(2,1)} %pick_places.1), calls=%async_computation | async-start | bytes 131072 | tf_op jit(solution)/shard_map/all_to_all | solution.py:390
  14.8 0.8 copy-start
  23.3 41.6 %all-to-all-start.1 = ((bf16[32,2,64,128]{3,2,1,0:T(8,128)(2,1)}), bf16[32,2,64,128]{3,2,1,0:T(8,128)(2,1)}, u32[]{:S(2)}, u32[]{:S(2)}) async-start(bf16[32,2,64,128]{3,2,1,0:T(8,128)(2,1)} %pick_moments.1), calls=%async_computation.1 | async-start | bytes 2097152 | tf_op jit(solution)/shard_map/all_to_all | solution.py:401
  31.4 7.3 %collective-permute-start = (bf16[8,64,128]{2,1,0:T(8,128)(2,1)S(1)}, bf16[8,64,128]{2,1,0:T(8,128)(2,1)S(1)}, u32[]{:S(2)}, u32[]{:S(2)}) collective-permute-start(bf16[8,64,128]{2,1,0:T(8,128)(2,1)S(1)} %get-tuple-element.43), channel_id=1, source_target_pairs={{0,1},{1,2},{2,3},{3,4},{4,5},{5,6},{6,7},{7,0},{8,9},{9,10},{10,1... | collective-permute-start | bytes 393224 | tf_op jit(solution)/shard_map/ppermute | solution.py:331
  31.4 8.7 %collective-permute-start.1 = (bf16[8,64,128]{2,1,0:T(8,128)(2,1)S(1)}, bf16[8,64,128]{2,1,0:T(8,128)(2,1)S(1)}, u32[]{:S(2)}, u32[]{:S(2)}) collective-permute-start(bf16[8,64,128]{2,1,0:T(8,128)(2,1)S(1)} %get-tuple-element.44), channel_id=1, source_target_pairs={{0,2},{1,3},{2,4},{3,5},{4,6},{5,7},{6,0},{7,1},{8,10},{9,11},{10,... | collective-permute-start | bytes 393224 | tf_op jit(solution)/shard_map/ppermute | solution.py:331
  32.9 31.9 %collective-permute-start.2 = (bf16[8,64,128]{2,1,0:T(8,128)(2,1)}, bf16[8,64,128]{2,1,0:T(8,128)(2,1)S(1)}, u32[]{:S(2)}, u32[]{:S(2)}) collective-permute-start(bf16[8,64,128]{2,1,0:T(8,128)(2,1)} %get-tuple-element.45), channel_id=1, source_target_pairs={{0,3},{1,4},{2,5},{3,6},{4,7},{5,0},{6,1},{7,2},{8,11},{9,12},{10,... | collective-permute-start | bytes 393224 | tf_op jit(solution)/shard_map/ppermute | solution.py:331
  35.0 29.9 %collective-permute-start.3 = (bf16[8,64,128]{2,1,0:T(8,128)(2,1)}, bf16[8,64,128]{2,1,0:T(8,128)(2,1)S(1)}, u32[]{:S(2)}, u32[]{:S(2)}) collective-permute-start(bf16[8,64,128]{2,1,0:T(8,128)(2,1)} %get-tuple-element.46), channel_id=1, source_target_pairs={{0,4},{1,5},{2,6},{3,7},{4,0},{5,1},{6,2},{7,3},{8,12},{9,13},{10,... | collective-permute-start | bytes 393224 | tf_op jit(solution)/shard_map/ppermute | solution.py:331
  37.0 27.9 %collective-permute-start.4 = (bf16[8,64,128]{2,1,0:T(8,128)(2,1)}, bf16[8,64,128]{2,1,0:T(8,128)(2,1)S(1)}, u32[]{:S(2)}, u32[]{:S(2)}) collective-permute-start(bf16[8,64,128]{2,1,0:T(8,128)(2,1)} %get-tuple-element.47), channel_id=1, source_target_pairs={{0,5},{1,6},{2,7},{3,0},{4,1},{5,2},{6,3},{7,4},{8,13},{9,14},{10,... | collective-permute-start | bytes 393224 | tf_op jit(solution)/shard_map/ppermute | solution.py:331
  38.7 26.2 %collective-permute-start.5 = (bf16[8,64,128]{2,1,0:T(8,128)(2,1)S(1)}, bf16[8,64,128]{2,1,0:T(8,128)(2,1)S(1)}, u32[]{:S(2)}, u32[]{:S(2)}) collective-permute-start(bf16[8,64,128]{2,1,0:T(8,128)(2,1)S(1)} %get-tuple-element.48), channel_id=1, source_target_pairs={{0,6},{1,7},{2,0},{3,1},{4,2},{5,3},{6,4},{7,5},{8,14},{9,15},{10,... | collective-permute-start | bytes 393224 | tf_op jit(solution)/shard_map/ppermute | solution.py:331
  40.1 24.8 %collective-permute-start.6 = (bf16[8,64,128]{2,1,0:T(8,128)(2,1)S(1)}, bf16[8,64,128]{2,1,0:T(8,128)(2,1)S(1)}, u32[]{:S(2)}, u32[]{:S(2)}) collective-permute-start(bf16[8,64,128]{2,1,0:T(8,128)(2,1)S(1)} %get-tuple-element.49), channel_id=1, source_target_pairs={{0,7},{1,0},{2,1},{3,2},{4,3},{5,4},{6,5},{7,6},{8,15},{9,8},{10,9... | collective-permute-start | bytes 393224 | tf_op jit(solution)/shard_map/ppermute | solution.py:331
  41.9 0.7 copy-start.1
  42.6 81.7 %copy-start.3 = (s32[32,2]{0,1:T(2,128)S(1)}, s32[32,2]{0,1:T(2,128)}, u32[]{:S(2)}) copy-start(s32[32,2]{0,1:T(2,128)} %param.10) | copy-start | bytes 772
  42.6 81.7 %copy-start.4 = (s32[32]{0:T(128)S(1)}, s32[32]{0:T(128)}, u32[]{:S(2)}) copy-start(s32[32]{0:T(128)} %count_ref.3) | copy-start | bytes 388
  87.5 36.8 %all-to-all-start.2 = ((bf16[32,2,64,128]{3,2,1,0:T(8,128)(2,1)}), bf16[32,2,64,128]{3,2,1,0:T(8,128)(2,1)S(1)}, u32[]{:S(2)}, u32[]{:S(2)}) async-start(bf16[32,2,64,128]{3,2,1,0:T(8,128)(2,1)} %bitcast.6), calls=%async_computation.2 | async-start | bytes 2097152 | tf_op jit(solution)/shard_map/all_to_all | solution.py:404
  98.4 6.7 %collective-permute-start.7 = (bf16[8,64,128]{2,1,0:T(8,128)(2,1)}, bf16[8,64,128]{2,1,0:T(8,128)(2,1)S(1)}, u32[]{:S(2)}, u32[]{:S(2)}) collective-permute-start(bf16[8,64,128]{2,1,0:T(8,128)(2,1)} %get-tuple-element.58), channel_id=1, source_target_pairs={{0,1},{1,2},{2,3},{3,4},{4,5},{5,6},{6,7},{7,0},{8,9},{9,10},{10,1... | collective-permute-start | bytes 393224 | tf_op jit(solution)/shard_map/ppermute | solution.py:331
  98.4 7.8 %collective-permute-start.8 = (bf16[8,64,128]{2,1,0:T(8,128)(2,1)}, bf16[8,64,128]{2,1,0:T(8,128)(2,1)S(1)}, u32[]{:S(2)}, u32[]{:S(2)}) collective-permute-start(bf16[8,64,128]{2,1,0:T(8,128)(2,1)} %get-tuple-element.57), channel_id=1, source_target_pairs={{0,2},{1,3},{2,4},{3,5},{4,6},{5,7},{6,0},{7,1},{8,10},{9,11},{10,... | collective-permute-start | bytes 393224 | tf_op jit(solution)/shard_map/ppermute | solution.py:331
  98.9 10.9 %collective-permute-start.9 = (bf16[8,64,128]{2,1,0:T(8,128)(2,1)}, bf16[8,64,128]{2,1,0:T(8,128)(2,1)S(1)}, u32[]{:S(2)}, u32[]{:S(2)}) collective-permute-start(bf16[8,64,128]{2,1,0:T(8,128)(2,1)} %get-tuple-element.56), channel_id=1, source_target_pairs={{0,3},{1,4},{2,5},{3,6},{4,7},{5,0},{6,1},{7,2},{8,11},{9,12},{10,... | collective-permute-start | bytes 393224 | tf_op jit(solution)/shard_map/ppermute | solution.py:331
  100.1 10.9 %collective-permute-start.10 = (bf16[8,64,128]{2,1,0:T(8,128)(2,1)}, bf16[8,64,128]{2,1,0:T(8,128)(2,1)S(1)}, u32[]{:S(2)}, u32[]{:S(2)}) collective-permute-start(bf16[8,64,128]{2,1,0:T(8,128)(2,1)} %get-tuple-element.55), channel_id=1, source_target_pairs={{0,4},{1,5},{2,6},{3,7},{4,0},{5,1},{6,2},{7,3},{8,12},{9,13},{10,... | collective-permute-start | bytes 393224 | tf_op jit(solution)/shard_map/ppermute | solution.py:331
  103.0 8.4 %collective-permute-start.11 = (bf16[8,64,128]{2,1,0:T(8,128)(2,1)}, bf16[8,64,128]{2,1,0:T(8,128)(2,1)S(1)}, u32[]{:S(2)}, u32[]{:S(2)}) collective-permute-start(bf16[8,64,128]{2,1,0:T(8,128)(2,1)} %get-tuple-element.54), channel_id=1, source_target_pairs={{0,5},{1,6},{2,7},{3,0},{4,1},{5,2},{6,3},{7,4},{8,13},{9,14},{10,... | collective-permute-start | bytes 393224 | tf_op jit(solution)/shard_map/ppermute | solution.py:331
  105.0 7.9 %collective-permute-start.12 = (bf16[8,64,128]{2,1,0:T(8,128)(2,1)S(1)}, bf16[8,64,128]{2,1,0:T(8,128)(2,1)S(1)}, u32[]{:S(2)}, u32[]{:S(2)}) collective-permute-start(bf16[8,64,128]{2,1,0:T(8,128)(2,1)S(1)} %get-tuple-element.53), channel_id=1, source_target_pairs={{0,6},{1,7},{2,0},{3,1},{4,2},{5,3},{6,4},{7,5},{8,14},{9,15},{10,... | collective-permute-start | bytes 393224 | tf_op jit(solution)/shard_map/ppermute | solution.py:331
  106.1 8.3 %collective-permute-start.13 = (bf16[8,64,128]{2,1,0:T(8,128)(2,1)S(1)}, bf16[8,64,128]{2,1,0:T(8,128)(2,1)S(1)}, u32[]{:S(2)}, u32[]{:S(2)}) collective-permute-start(bf16[8,64,128]{2,1,0:T(8,128)(2,1)S(1)} %get-tuple-element.52), channel_id=1, source_target_pairs={{0,7},{1,0},{2,1},{3,2},{4,3},{5,4},{6,5},{7,6},{8,15},{9,8},{10,9... | collective-permute-start | bytes 393224 | tf_op jit(solution)/shard_map/ppermute | solution.py:331
  114.4 12.2 %copy-start.6 = (bf16[64,64,128]{2,1,0:T(8,128)(2,1)}, bf16[64,64,128]{2,1,0:T(8,128)(2,1)S(1)}, u32[]{:S(2)}) copy-start(bf16[64,64,128]{2,1,0:T(8,128)(2,1)S(1)} %constant_dynamic-update-slice_fusion) | copy-start | bytes 3145732
